TPU v7x, 512 devices: a whole 4x8x8 slice. The times are simulated.
512 devices in a mesh: ens: 2 (over x_hi), lat: 32 (over x_lo, y, core), lon: 8 (over z).
Axes of the slice: x: 4 (x_hi: 2, x_lo: 2; x = x_hi * 2 + x_lo), y: 8, z: 8, core: 2. Of those that a mesh axis runs over, the one named last changes fastest.
Arguments:
- fields: bfloat16 [2, 128, 1440, 128], P('ens', 'lat', 'lon'), may hold values from -6 to 6
- cotangent: bfloat16 [2, 128, 1440, 128], P('ens', 'lat', 'lon'), may hold values from -6 to 6
- basis_weights: bfloat16 [3, 128, 12], P(None, 'lat'), may hold values from -1.75 to 1.75
- band_support: int32 [32, 3], P('lat'), may hold values from 0 to 1, as said below
- spectrum_real: float32 [3, 128, 720], P(None, 'lat'), may hold values from -6 to 6
- spectrum_imag: float32 [3, 128, 720], P(None, 'lat'), may hold values from -6 to 6
- filter_weights: bfloat16 [3, 128, 128], replicated, may hold values from -0.3125 to 0.3125
- inner_weights: bfloat16 [128, 256], replicated, may hold values from -0.5 to 0.5
- outer_weights: bfloat16 [256, 128], replicated, may hold values from -0.375 to 0.375
Outputs:
- field_grad: bfloat16 [2, 128, 1440, 128], P('ens', 'lat', 'lon')
- filter_grad: float32 [3, 128, 128], replicated
- inner_grad: float32 [128, 256], replicated
- outer_grad: float32 [256, 128], replicated
Inputs may be any that keep to these rules, and one draw needn't show every extreme that they name: `band_support`: the middle column is 1 in every band; the bands among the first and the last max(8, 1), and the bands 32 // 2 - 1, 16 and 17, have all three columns 1; band 32 // 4 has a 0 in its first column.
All inputs are finite; a program needn't handle non-finite values.
Results may differ from a plain program's by a relative error of at most 0.019.
Values may be sent and summed in bfloat16 or wider, within the bound.
No kernel may reach another device: no remote copies, remote signals or barrier semaphores. Data moves between devices by JAX's collectives and lax.ppermute only.
A program may use at most 64 MiB of HBM per device.

v0:
```python
import math

import jax
import jax.numpy as jnp
from jax import lax
from jax.sharding import PartitionSpec as P

GELU_SCALE = 0.7978845608028654
CUBIC_TERM = 0.044715


def padded(cells, sides, width):
    for axis, dim in sides:
        count = lax.axis_size(axis)
        ends = count - 1
        head = lax.slice_in_dim(cells, 0, width, axis=dim)
        tail = lax.slice_in_dim(cells, cells.shape[dim] - width, cells.shape[dim], axis=dim)
        cells = jnp.concatenate(
            [
                lax.ppermute(tail, axis, [(i, (i + 1) % count) for i in range(ends)]),
                cells,
                lax.ppermute(head, axis, [((i + 1) % count, i) for i in range(ends)]),
            ],
            axis=dim,
        )
    return cells


def shifted(value, axis, steps):
    count = lax.axis_size(axis)
    leading, last = (max(0, -steps), min(count, count - steps))
    return lax.ppermute(value, axis, [(source, source + steps) for source in range(leading, last)])


def gelu_parts(hidden):
    inner_part = GELU_SCALE * (hidden + CUBIC_TERM * hidden * hidden * hidden)
    tangent = jnp.tanh(inner_part)
    gelu_value = 0.5 * hidden * (1.0 + tangent)
    gelu_slope = 0.5 * (1.0 + tangent) + 0.5 * hidden * (1.0 - tangent * tangent) * GELU_SCALE * (
        1.0 + 3.0 * CUBIC_TERM * hidden * hidden
    )
    return (gelu_value, gelu_slope)


def dft_tables(length, mode_count):
    column = jnp.arange(length, dtype=jnp.int32)
    frequency = jnp.arange(mode_count, dtype=jnp.int32)
    phase_angle = (column[:, None] * frequency[None, :] % length).astype(jnp.float32) * (
        2.0 * math.pi / length
    )
    forward_cos = jnp.cos(phase_angle).astype(jnp.bfloat16)
    forward_sin = (-jnp.sin(phase_angle)).astype(jnp.bfloat16)
    weight = jnp.where(frequency == 0, 1.0, 2.0).astype(jnp.float32) / length
    inverse_cos = (weight[:, None] * jnp.cos(phase_angle.T)).astype(jnp.bfloat16)
    inverse_sin = (-weight[:, None] * jnp.sin(phase_angle.T)).astype(jnp.bfloat16)
    return (forward_cos, forward_sin, inverse_cos, inverse_sin)


def filter_rows(basis_rows, spec_real, spec_imag, tables):
    forward_cos, forward_sin, inverse_cos, inverse_sin = tables
    part_a = jnp.einsum(
        "krcj,jm->krcm", basis_rows, forward_cos, preferred_element_type=jnp.float32
    )
    part_b = jnp.einsum(
        "krcj,jm->krcm", basis_rows, forward_sin, preferred_element_type=jnp.float32
    )
    gain_a = spec_real[:, :, None, :]
    gain_b = spec_imag[:, :, None, :]
    filt_a = (gain_a * part_a - gain_b * part_b).astype(jnp.bfloat16)
    filt_b = (gain_a * part_b + gain_b * part_a).astype(jnp.bfloat16)
    result = jnp.einsum("krcm,mj->krcj", filt_a, inverse_cos, preferred_element_type=jnp.float32)
    result = result + jnp.einsum(
        "krcm,mj->krcj", filt_b, inverse_sin, preferred_element_type=jnp.float32
    )
    return result.astype(jnp.bfloat16)


def adjoint_rows(cot_rows, spec_real, spec_imag, tables):
    forward_cos, forward_sin, inverse_cos, inverse_sin = tables
    grad_a = jnp.einsum("krcj,mj->krcm", cot_rows, inverse_cos, preferred_element_type=jnp.float32)
    grad_b = jnp.einsum("krcj,mj->krcm", cot_rows, inverse_sin, preferred_element_type=jnp.float32)
    gain_a = spec_real[:, :, None, :]
    gain_b = spec_imag[:, :, None, :]
    back_a = (gain_a * grad_a + gain_b * grad_b).astype(jnp.bfloat16)
    back_b = (gain_a * grad_b - gain_b * grad_a).astype(jnp.bfloat16)
    result = jnp.einsum("krcm,jm->krcj", back_a, forward_cos, preferred_element_type=jnp.float32)
    result = result + jnp.einsum(
        "krcm,jm->krcj", back_b, forward_sin, preferred_element_type=jnp.float32
    )
    return result.astype(jnp.bfloat16)


def widen(row_block):
    return padded(row_block, (("lat", 0),), row_block.shape[0])


def block_term(weights, row_block):
    return jnp.einsum("kir,rab->kiba", weights, row_block, preferred_element_type=jnp.float32)


def block_skip(weights, row_block):
    return jnp.zeros(
        (weights.shape[0], weights.shape[1], row_block.shape[2], row_block.shape[1]), jnp.float32
    )


def contract(masked, support, wide_rows, band_rows):
    running = jnp.zeros(
        (masked.shape[0], band_rows, wide_rows.shape[2], wide_rows.shape[1]), jnp.float32
    )
    for offset in range(3):
        weights = masked[:, :, offset * band_rows : (offset + 1) * band_rows]
        row_block = wide_rows[offset * band_rows : (offset + 1) * band_rows]
        running = running + lax.cond(
            support[offset] > 0, block_term, block_skip, weights, row_block
        )
    return running.astype(jnp.bfloat16)


def spread_term(weights, cot_rows):
    return jnp.einsum("kir,kiba->rab", weights, cot_rows, preferred_element_type=jnp.float32)


def spread_skip(weights, cot_rows):
    return jnp.zeros((weights.shape[2], cot_rows.shape[3], cot_rows.shape[2]), jnp.float32)


def latitude_adjoint(masked, support, cot_rows, band_rows):
    pieces = []
    for offset in range(3):
        weights = masked[:, :, offset * band_rows : (offset + 1) * band_rows]
        pieces.append(lax.cond(support[offset] > 0, spread_term, spread_skip, weights, cot_rows))
    running = pieces[1] + shifted(pieces[0].astype(jnp.bfloat16), "lat", -1).astype(jnp.float32)
    running = running + shifted(pieces[2].astype(jnp.bfloat16), "lat", 1).astype(jnp.float32)
    return running.astype(jnp.bfloat16)


def local(
    fields,
    cotangent,
    basis_weights,
    band_support,
    spectrum_real,
    spectrum_imag,
    filter_weights,
    inner_weights,
    outer_weights,
):
    band_rows = fields.shape[1]
    length = fields.shape[2] * lax.axis_size("lon")
    tables = dft_tables(length, spectrum_real.shape[2])
    grad_scale = 1.0 / math.sqrt(lax.axis_size("ens") * lax.axis_size("lat") * band_rows * length)
    support = band_support[0]
    mask_cols = jnp.repeat(support, band_rows).astype(jnp.bfloat16)
    masked = basis_weights * mask_cols[None, None, :]
    local_rows = fields[0]
    basis_local = contract(masked, support, widen(local_rows), band_rows)
    basis_moved = lax.all_to_all(basis_local, "lon", split_axis=2, concat_axis=3, tiled=True)
    filtered_moved = filter_rows(basis_moved, spectrum_real, spectrum_imag, tables)
    filtered = lax.all_to_all(filtered_moved, "lon", split_axis=3, concat_axis=2, tiled=True)
    mixed_out = jnp.einsum(
        "kicj,kcd->ijd", filtered, filter_weights, preferred_element_type=jnp.float32
    )
    state_rows = (local_rows.astype(jnp.float32) + mixed_out).astype(jnp.bfloat16)
    hidden = jnp.einsum(
        "ijc,ch->ijh", state_rows, inner_weights, preferred_element_type=jnp.float32
    )
    gelu_value, gelu_slope = gelu_parts(hidden)
    active = gelu_value.astype(jnp.bfloat16)
    member_cot = cotangent[0]
    d_active = jnp.einsum(
        "ijc,hc->ijh", member_cot, outer_weights, preferred_element_type=jnp.float32
    )
    d_hidden = (d_active * gelu_slope).astype(jnp.bfloat16)
    d_state = member_cot.astype(jnp.float32) + jnp.einsum(
        "ijh,ch->ijc", d_hidden, inner_weights, preferred_element_type=jnp.float32
    )
    d_state_b = d_state.astype(jnp.bfloat16)
    outer_local = jnp.einsum("ijh,ijc->hc", active, member_cot, preferred_element_type=jnp.float32)
    inner_local = jnp.einsum(
        "ijc,ijh->ch", state_rows, d_hidden, preferred_element_type=jnp.float32
    )
    filter_local = jnp.einsum(
        "kicj,ijd->kcd", filtered, d_state_b, preferred_element_type=jnp.float32
    )
    d_filtered = jnp.einsum(
        "ijd,kcd->kicj", d_state_b, filter_weights, preferred_element_type=jnp.float32
    ).astype(jnp.bfloat16)
    d_filtered_moved = lax.all_to_all(d_filtered, "lon", split_axis=2, concat_axis=3, tiled=True)
    d_basis_moved = adjoint_rows(d_filtered_moved, spectrum_real, spectrum_imag, tables)
    d_basis = lax.all_to_all(d_basis_moved, "lon", split_axis=3, concat_axis=2, tiled=True)
    lat_part = latitude_adjoint(masked, support, d_basis, band_rows)
    field_grad = (d_state + lat_part.astype(jnp.float32)).astype(jnp.bfloat16)[None]
    filter_total, inner_sum, outer_sum = lax.psum(
        (filter_local, inner_local, outer_local), ("ens", "lat", "lon")
    )
    return (field_grad, filter_total * grad_scale, inner_sum * grad_scale, outer_sum * grad_scale)


def solution(mesh):
    placed = (
        P("ens", "lat", "lon", None),
        P("ens", "lat", "lon", None),
        P(None, "lat", None),
        P("lat", None),
        P(None, "lat", None),
        P(None, "lat", None),
        P(),
        P(),
        P(),
    )
    return jax.shard_map(
        local,
        mesh=mesh,
        in_specs=placed,
        out_specs=(P("ens", "lat", "lon", None), P(), P(), P()),
        check_vma=False,
    )
```

profile of v0, /device:TPU:1, one launch (start us, length us, event | category | flops | bytes accessed | tf_op | source)
XLA Modules:
  0.0 621.9 jit_solution(6378865005062982101)
XLA Ops:
  7.2 1.7 copy.209
  8.8 4.6 collective-permute-start
  13.4 5.5 collective-permute-start.1
  18.9 0.7 convert_bitcast_fusion
  19.6 1.4 fusion.102
  23.1 0.8 copy.119
  23.9 0.6 fusion.101
  24.5 1.6 conditional.7
  24.5 1.4 convolution_bitcast_fusion.1
  26.1 1.4 conditional.8
  26.2 1.2 convolution_bitcast_fusion.2
  27.6 0.7 conditional.6
  27.6 0.5 convolution_bitcast_fusion
  28.3 1.4 add_convert_fusion
  29.6 2.4 copy.129
  32.1 6.5 %all-to-all-start = ((bf16[3,4,128,180]{3,1,0,2:T(4,128)(2,1)}), bf16[3,4,128,180]{3,1,0,2:T(4,128)(2,1)S(1)}, u32[]{:S(2)}, u32[]{:S(2)}) async-start(bf16[3,4,128,180]{3,1,0,2:T(4,128)(2,1)} %copy.129), calls=%async_computation | async-start | bytes 1572864 | tf_op jit(solution)/shard_map/all_to_all | solution.py:158
  38.6 22.3 %all-to-all-done = bf16[3,4,128,180]{3,1,0,2:T(4,128)(2,1)S(1)} async-done(((bf16[3,4,128,180]{3,1,0,2:T(4,128)(2,1)}), bf16[3,4,128,180]{3,1,0,2:T(4,128)(2,1)S(1)}, u32[]{:S(2)}, u32[]{:S(2)}) %all-to-all-start) | async-done | bytes 552992 | tf_op jit(solution)/shard_map/all_to_all | solution.py:158
  61.0 0.3 copy.131
  61.3 0.9 all_to_all.55
  62.3 17.9 %fusion.39 = f32[3,4,16,720]{3,2,1,0:T(8,128)S(1)} fusion(bf16[3,4,16,1440]{3,2,1,0:T(8,128)(2,1)S(1)} %all_to_all.55), kind=kOutput, calls=%fused_computation.48 | convolution fusion | flops 409536000 | bytes 1105920 | tf_op jit(solution)/shard_map/krcj,jm->krcm/dot_general | solution.py:64
  80.2 17.9 %fusion.36 = f32[3,4,16,720]{3,2,1,0:T(8,128)S(1)} fusion(bf16[3,4,16,1440]{3,2,1,0:T(8,128)(2,1)S(1)} %all_to_all.55), kind=kOutput, calls=%fused_computation.47 | convolution fusion | flops 408499200 | bytes 1105920 | tf_op jit(solution)/shard_map/krcj,jm->krcm/dot_general | solution.py:61
  98.1 26.4 %fusion.27 = f32[3,4,16,1440]{3,2,1,0:T(8,128)S(1)} fusion(f32[720]{0:T(1024)S(1)} %select_multiply_fusion, f32[3,4,16,720]{3,2,1,0:T(8,128)S(1)} %fusion.39, f32[3,4,16,720]{3,2,1,0:T(8,128)S(1)} %fusion.36, f32[3,4,720]{2,1,0:T(4,128)S(1)} %copy-done.13, f32[3,4,720]{2,1,0:T(4,128)S(1)} %copy-done.15), kind=kOutput, calls=%fused_computation.42 | convolution fusion | flops 410088960 | bytes 2283840 | tf_op jit(solution)/shard_map/krcm,mj->krcj/dot_general | solution.py:71
  124.5 19.2 %fusion.19 = bf16[3,4,16,1440]{3,2,1,0:T(8,128)(2,1)S(1)} fusion(f32[3,4,16,1440]{3,2,1,0:T(8,128)S(1)} %fusion.27, f32[720]{0:T(1024)S(1)} %fusion.72, f32[3,4,16,720]{3,2,1,0:T(8,128)S(1)} %fusion.36, f32[3,4,16,720]{3,2,1,0:T(8,128)S(1)} %fusion.39, f32[3,4,720]{2,1,0:T(4,128)S(1)} %copy-done.13, f32[3,4,720]{2,1,0:T(4,128)S(1)} %copy-done.15), kind=kOutput, calls=%fused_computation.35 | convolution fusion | flops 410641920 | bytes 2836800 | tf_op jit(solution)/shard_map/krcm,mj->krcj/dot_general | solution.py:72
  143.7 5.6 copy.132
  149.3 6.2 reshape.74
  155.5 20.7 %all_to_all.72 = bf16[8,2,17280]{2,1,0:T(2,128)(2,1)S(1)} all-to-all(bf16[8,2,17280]{2,1,0:T(2,128)(2,1)S(1)} %reshape.74), channel_id=1, replica_groups=mesh['ens'=2,'lat'=32,'lon'=8] {'lon'}, dimensions={0} | all-to-all | bytes 1105920 | tf_op jit(solution)/shard_map/all_to_all | solution.py:160
  176.2 5.4 reshape.75
  181.6 6.0 copy.133
  187.6 0.4 fusion.44
  188.3 0.6 fusion.41
  189.2 0.4 fusion.42
  189.6 1.4 copy.137
  191.1 3.5 all-to-all-start.2
  194.6 1.0 convolution_bitcast_fusion.7
  195.7 20.6 %all-to-all-done.2 = bf16[3,4,128,180]{3,1,0,2:T(4,128)(2,1)S(1)} async-done(((bf16[3,4,128,180]{3,1,0,2:T(4,128)(2,1)}), bf16[3,4,128,180]{3,1,0,2:T(4,128)(2,1)S(1)}, u32[]{:S(2)}, u32[]{:S(2)}) %all-to-all-start.2) | async-done | bytes 552992 | tf_op jit(solution)/shard_map/all_to_all | solution.py:189
  216.7 0.9 all_to_all.63
  217.6 18.1 %fusion.29 = f32[3,4,16,720]{3,2,1,0:T(8,128)S(1)} fusion(bf16[3,4,16,1440]{3,2,1,0:T(8,128)(2,1)S(1)} %all_to_all.63, f32[720]{0:T(1024)S(1)} %copy-done.11), kind=kOutput, calls=%fused_computation.43 | convolution fusion | flops 409536000 | bytes 1108800 | tf_op jit(solution)/shard_map/krcj,mj->krcm/dot_general | solution.py:81
  235.8 18.0 %fusion.25 = f32[3,4,16,720]{3,2,1,0:T(8,128)S(1)} fusion(bf16[3,4,16,1440]{3,2,1,0:T(8,128)(2,1)S(1)} %all_to_all.63, f32[720]{0:T(1024)S(1)} %copy-done.9), kind=kOutput, calls=%fused_computation.41 | convolution fusion | flops 409536000 | bytes 1108800 | tf_op jit(solution)/shard_map/krcj,mj->krcm/dot_general | solution.py:80
  253.8 17.8 %fusion.34 = f32[3,4,16,1440]{3,2,1,0:T(8,128)S(1)} fusion(f32[3,4,16,720]{3,2,1,0:T(8,128)S(1)} %fusion.29, f32[3,4,16,720]{3,2,1,0:T(8,128)S(1)} %fusion.25, f32[3,4,720]{2,1,0:T(4,128)S(1)} %copy-done.14, f32[3,4,720]{2,1,0:T(4,128)S(1)} %copy-done.16), kind=kOutput, calls=%fused_computation.46 | convolution fusion | flops 409052160 | bytes 2280960 | tf_op jit(solution)/shard_map/krcm,jm->krcj/dot_general | solution.py:86
  271.6 18.1 %fusion.20 = bf16[3,4,16,1440]{3,2,1,0:T(8,128)(2,1)S(1)} fusion(f32[3,4,16,1440]{3,2,1,0:T(8,128)S(1)} %fusion.34, f32[3,4,16,720]{3,2,1,0:T(8,128)S(1)} %fusion.25, f32[3,4,16,720]{3,2,1,0:T(8,128)S(1)} %fusion.29, f32[3,4,720]{2,1,0:T(4,128)S(1)} %copy-done.14, f32[3,4,720]{2,1,0:T(4,128)S(1)} %copy-done.16), kind=kOutput, calls=%fused_computation.36 | convolution fusion | flops 410641920 | bytes 2833920 | tf_op jit(solution)/shard_map/krcm,jm->krcj/dot_general | solution.py:87
  289.7 5.6 copy.140
  295.4 6.9 %reshape.76 = bf16[8,2,17280]{2,1,0:T(2,128)(2,1)} reshape(bf16[1440,3,4,16]{3,2,1,0:T(4,128)(2,1)} %bitcast.153) | data formatting | bytes 1105920
  302.3 3.5 all-to-all-start.3
  305.9 0.9 convolution_bitcast_fusion.9
  306.8 1.1 convolution_bitcast_fusion.8
  307.9 278.5 %all-reduce.3.cloned.1.call-done = (f32[3,128,128]{2,1,0:T(8,128)}, f32[128,256]{1,0:T(8,128)}, f32[256,128]{1,0:T(8,128)}) async-done(((f32[3,128,128]{2,1,0:T(8,128)}, f32[128,256]{1,0:T(8,128)}, f32[256,128]{1,0:T(8,128)}), (f32[3,128,128]{2,1,0:T(8,128)}, f32[128,256]{1,0:T(8,128)}, f32[256,128]{1,0:T(8,128)})) %all-reduce.3.cloned.1.call-update) | async-done | bytes 458768 | tf_op jit(solution)/shard_map/psum | solution.py:194
  586.5 1.6 broadcast_multiply_fusion.2
  588.0 1.6 broadcast_multiply_fusion
  589.6 5.4 reshape.77
  595.0 6.0 copy.141
  601.0 2.1 conditional.11
  601.0 1.0 copy.144
  602.0 1.1 convolution_bitcast_fusion.5
  603.1 2.6 collective-permute-start.3
  605.7 1.4 conditional.10
  605.7 1.0 copy.143
  606.7 0.4 convolution_bitcast_fusion.4
  607.1 1.9 collective-permute-start.2
  609.0 0.7 broadcast_multiply_fusion.1
  609.7 1.4 conditional.9
  609.7 1.0 copy.142
  610.7 0.4 convolution_bitcast_fusion.3
  611.1 2.9 collective-permute-done.2
  614.0 0.9 fusion.62
  (54 shorter events, 2.1 us)
Async XLA Ops:
  7.2 180.4 %copy-start = (bf16[3,128,128]{2,1,0:T(8,128)(2,1)S(1)}, bf16[3,128,128]{2,1,0:T(8,128)(2,1)}, u32[]{:S(2)}) copy-start(bf16[3,128,128]{2,1,0:T(8,128)(2,1)} %param.27) | copy-start | bytes 294916
  8.8 18.7 %collective-permute-start = (bf16[4,180,128]{2,1,0:T(8,128)(2,1)}, bf16[4,180,128]{2,1,0:T(8,128)(2,1)S(1)}, u32[]{:S(2)}, u32[]{:S(2)}) collective-permute-start(bf16[4,180,128]{2,1,0:T(8,128)(2,1)} %bitcast.149), channel_id=1, source_target_pairs={{0,8},{8,16},{16,24},{24,32},{32,40},{40,48},{48,56},{56,64},{64,7... | collective-permute-start | bytes 552968 | tf_op jit(solution)/shard_map/ppermute | solution.py:20
  13.4 12.7 %collective-permute-start.1 = (bf16[4,180,128]{2,1,0:T(8,128)(2,1)}, bf16[4,180,128]{2,1,0:T(8,128)(2,1)S(1)}, u32[]{:S(2)}, u32[]{:S(2)}) collective-permute-start(bf16[4,180,128]{2,1,0:T(8,128)(2,1)} %bitcast.149), channel_id=1, source_target_pairs={{8,0},{16,8},{24,16},{32,24},{40,32},{48,40},{56,48},{64,56},{72,6... | collective-permute-start | bytes 552968 | tf_op jit(solution)/shard_map/ppermute | solution.py:22
  24.5 3.0 copy-start.6
  32.1 28.8 %all-to-all-start = ((bf16[3,4,128,180]{3,1,0,2:T(4,128)(2,1)}), bf16[3,4,128,180]{3,1,0,2:T(4,128)(2,1)S(1)}, u32[]{:S(2)}, u32[]{:S(2)}) async-start(bf16[3,4,128,180]{3,1,0,2:T(4,128)(2,1)} %copy.129), calls=%async_computation | async-start | bytes 1572864 | tf_op jit(solution)/shard_map/all_to_all | solution.py:158
  38.6 86.0 %copy-start.10 = (f32[720]{0:T(1024)}, f32[720]{0:T(1024)S(1)}, u32[]{:S(2)}) copy-start(f32[720]{0:T(1024)S(1)} %fusion.72) | copy-start | bytes 8644
  38.6 59.5 %copy-start.8 = (f32[720]{0:T(1024)}, f32[720]{0:T(1024)S(1)}, u32[]{:S(2)}) copy-start(f32[720]{0:T(1024)S(1)} %select_multiply_fusion) | copy-start | bytes 8644
  80.1 17.9 %copy-start.13 = (f32[3,4,720]{2,1,0:T(4,128)S(1)}, f32[3,4,720]{2,1,0:T(4,128)}, u32[]{:S(2)}) copy-start(f32[3,4,720]{2,1,0:T(4,128)} %param.26) | copy-start | bytes 103684
  80.1 17.9 %copy-start.15 = (f32[3,4,720]{2,1,0:T(4,128)S(1)}, f32[3,4,720]{2,1,0:T(4,128)}, u32[]{:S(2)}) copy-start(f32[3,4,720]{2,1,0:T(4,128)} %param.25) | copy-start | bytes 103684
  176.2 11.4 %copy-start.1 = (bf16[1,4,180,128]{3,1,2,0:T(4,128)(2,1)S(1)}, bf16[1,4,180,128]{3,1,2,0:T(4,128)(2,1)}, u32[]{:S(2)}) copy-start(bf16[1,4,180,128]{3,1,2,0:T(4,128)(2,1)} %param.21) | copy-start | bytes 552964
  181.5 6.4 %copy-start.4 = (bf16[128,256]{1,0:T(8,128)(2,1)S(1)}, bf16[128,256]{1,0:T(8,128)(2,1)}, u32[]{:S(2)}) copy-start(bf16[128,256]{1,0:T(8,128)(2,1)} %param.28) | copy-start | bytes 196612
  181.5 6.7 %copy-start.2 = (bf16[1,4,180,128]{3,1,2,0:T(4,128)(2,1)S(1)}, bf16[1,4,180,128]{3,1,2,0:T(4,128)(2,1)}, u32[]{:S(2)}) copy-start(bf16[1,4,180,128]{3,1,2,0:T(4,128)(2,1)} %param.22) | copy-start | bytes 552964
  181.5 6.7 %copy-start.12 = (bf16[256,128]{1,0:T(8,128)(2,1)S(1)}, bf16[256,128]{1,0:T(8,128)(2,1)}, u32[]{:S(2)}) copy-start(bf16[256,128]{1,0:T(8,128)(2,1)} %param.29) | copy-start | bytes 196612
  191.1 25.2 %all-to-all-start.2 = ((bf16[3,4,128,180]{3,1,0,2:T(4,128)(2,1)}), bf16[3,4,128,180]{3,1,0,2:T(4,128)(2,1)S(1)}, u32[]{:S(2)}, u32[]{:S(2)}) async-start(bf16[3,4,128,180]{3,1,0,2:T(4,128)(2,1)} %copy.137), calls=%async_computation.2 | async-start | bytes 1572864 | tf_op jit(solution)/shard_map/all_to_all | solution.py:189
  195.7 22.0 %copy-start.11 = (f32[720]{0:T(1024)S(1)}, f32[720]{0:T(1024)}, u32[]{:S(2)}) copy-start(f32[720]{0:T(1024)} %copy-done.10) | copy-start | bytes 8644
  217.6 18.1 %copy-start.9 = (f32[720]{0:T(1024)S(1)}, f32[720]{0:T(1024)}, u32[]{:S(2)}) copy-start(f32[720]{0:T(1024)} %copy-done.8) | copy-start | bytes 8644
  235.8 18.0 %copy-start.14 = (f32[3,4,720]{2,1,0:T(4,128)S(1)}, f32[3,4,720]{2,1,0:T(4,128)}, u32[]{:S(2)}) copy-start(f32[3,4,720]{2,1,0:T(4,128)} %param.26) | copy-start | bytes 103684
  235.8 18.0 %copy-start.16 = (f32[3,4,720]{2,1,0:T(4,128)S(1)}, f32[3,4,720]{2,1,0:T(4,128)}, u32[]{:S(2)}) copy-start(f32[3,4,720]{2,1,0:T(4,128)} %param.25) | copy-start | bytes 103684
  295.4 11.4 %copy-start.3 = (bf16[1,4,180,128]{3,1,2,0:T(4,128)(2,1)S(1)}, bf16[1,4,180,128]{3,1,2,0:T(4,128)(2,1)}, u32[]{:S(2)}) copy-start(bf16[1,4,180,128]{3,1,2,0:T(4,128)(2,1)} %param.22) | copy-start | bytes 552964
  302.3 287.4 %all-to-all-start.3 = ((bf16[8,2,17280]{2,1,0:T(2,128)(2,1)}), bf16[8,2,17280]{2,1,0:T(2,128)(2,1)S(1)}, u32[]{:S(2)}, u32[]{:S(2)}) async-start(bf16[8,2,17280]{2,1,0:T(2,128)(2,1)} %reshape.76), calls=%async_computation.3 | async-start | bytes 1105920 | tf_op jit(solution)/shard_map/all_to_all | solution.py:191
  305.8 280.6 %all-reduce.3.cloned.1.call-start = ((), (), s32[]{:S(2)}) async-start(), calls=%async_computation.4 | async-start | bytes 917504 | tf_op jit(solution)/shard_map/psum | solution.py:194
  595.0 8.1 %copy-start.7 = (bf16[3,4,4]{1,2,0:T(4,128)(2,1)S(1)}, bf16[3,4,4]{1,2,0:T(4,128)(2,1)}, u32[]{:S(2)}) copy-start(bf16[3,4,4]{1,2,0:T(4,128)(2,1)} %copy-done.6) | copy-start | bytes 292
  595.0 14.0 %copy-start.5 = (f32[256,128]{1,0:T(8,128)S(1)}, f32[256,128]{1,0:T(8,128)}, u32[]{:S(2)}) copy-start(f32[256,128]{1,0:T(8,128)} %get-tuple-element.133) | copy-start | bytes 393220
  603.1 8.0 %collective-permute-start.3 = (bf16[4,180,128]{2,0,1:T(4,128)(2,1)S(1)}, bf16[4,180,128]{2,0,1:T(4,128)(2,1)S(1)}, u32[]{:S(2)}, u32[]{:S(2)}) collective-permute-start(bf16[4,180,128]{2,0,1:T(4,128)(2,1)S(1)} %get-tuple-element.151), channel_id=1, source_target_pairs={{0,8},{8,16},{16,24},{24,32},{32,40},{40,48},{48,56},{56,64},{64,7... | collective-permute-start | bytes 552968 | tf_op jit(solution)/shard_map/ppermute | solution.py:32
  607.1 6.9 %collective-permute-start.2 = (bf16[4,180,128]{2,0,1:T(4,128)(2,1)S(1)}, bf16[4,180,128]{2,0,1:T(4,128)(2,1)S(1)}, u32[]{:S(2)}, u32[]{:S(2)}) collective-permute-start(bf16[4,180,128]{2,0,1:T(4,128)(2,1)S(1)} %get-tuple-element.150), channel_id=1, source_target_pairs={{8,0},{16,8},{24,16},{32,24},{40,32},{48,40},{56,48},{64,56},{72,6... | collective-permute-start | bytes 552968 | tf_op jit(solution)/shard_map/ppermute | solution.py:32
Sparse Core Ops, SparseCore 0:
  312.8 273.6 all-reduce.2
where the time goes:
time: 627 us; the launch traced here: 622 us
  waiting for transfers between devices  324 us (52%)
  matrix products  163 us (26%)
  local copies, waits for them, and re-layouts  61.7 us (10%)
  starting transfers between devices  28.2 us (4%)
  blocking collectives  20.7 us (3%)
  between operations  16.7 us (3%)
  other arithmetic  7.01 us (1%)
    psum x1, waiting for transfers between devices, local(): lax.psum((filter_local, inner_local, outer_local), ('ens', 'lat', 'lon'))  279 us
    dot_general x1, matrix products, filter_rows(): jnp.einsum('krcm,mj->krcj', filt_a, inverse_cos, preferred_element_type=j...  26.4 us
    unnamed x40, local copies, waits for them, and re-layouts  26.3 us
    all_to_all x1, waiting for transfers between devices, local(): lax.all_to_all(basis_local, 'lon', split_axis=2, concat_axis=3, tiled=True)  22.3 us
    all_to_all x1, blocking collectives, local(): lax.all_to_all(filtered_moved, 'lon', split_axis=3, concat_axis=2, tiled=...  20.7 us
    all_to_all x1, waiting for transfers between devices, local(): lax.all_to_all(d_filtered, 'lon', split_axis=2, concat_axis=3, tiled=True)  20.6 us
    dot_general x1, matrix products, filter_rows(): jnp.einsum('krcm,mj->krcj', filt_b, inverse_sin, preferred_element_type=j...  19.2 us
    dot_general x1, matrix products, adjoint_rows(): jnp.einsum('krcm,jm->krcj', back_b, forward_sin, preferred_element_type=j...  18.1 us
  transfers between devices with their start and end apart: 8, of which 4 were waited for; matrix products, arithmetic and copies ran while one was open for 3% of the time, Pallas kernels for 0%

commit v1 on v0

v1 whole, which is shorter than its diff:
```python
import math

import jax
import jax.numpy as jnp
import ml_dtypes
import numpy as np
from jax import lax
from jax.experimental import pallas as pl
from jax.experimental.pallas import tpu as pltpu
from jax.sharding import PartitionSpec as P

GELU_SCALE = 0.7978845608028654
CUBIC_TERM = 0.044715
BF = jnp.bfloat16
F32 = jnp.float32
NLON = 1440
NZ = 8
LON = 180
MODES = 720
MP = 768
KP = 1536
CB = 16
NK = 3
NR = 4
LIMIT = 48 * 1024 * 1024


def dft_table():
    lane = np.arange(KP)
    tail = lane >= NZ * 128
    owner = np.where(tail, 2 * ((lane - NZ * 128) // 128) + (lane % 128 >= 64), lane // 128)
    place = np.where(tail, 128 + lane % 64, lane % 128)
    column = owner * LON + place
    frequency = np.arange(MP)
    phase = 2.0 * math.pi * ((column[:, None] * frequency[None, :]) % NLON) / NLON
    valid = (place < LON)[:, None] & (frequency < MODES)[None, :]
    table = np.concatenate(
        [np.where(valid, np.cos(phase), 0.0), np.where(valid, -np.sin(phase), 0.0)], axis=1
    )
    return table.astype(ml_dtypes.bfloat16)


def point_select():
    lane = np.arange(384)
    tile = lane // 128
    upper = np.where(tile == 1, lane % 128 >= 64, tile == 2).astype(np.int64)
    place = np.where(tile == 1, 128 + lane % 64, lane % 128)
    out = np.zeros((LON * NR, 2 * 384), np.float32)
    for first in range(2):
        row = 2 * upper + first
        good = place < LON
        out[(place * NR + row)[good], first * 384 + lane[good]] = 1.0
    return out.astype(ml_dtypes.bfloat16)


def dot(a, b):
    return jnp.dot(a, b, preferred_element_type=F32)


def dot_tn(a, b):
    return lax.dot_general(a, b, (((0,), (0,)), ((), ())), preferred_element_type=F32)


def dot_nt(a, b):
    return lax.dot_general(a, b, (((1,), (1,)), ((), ())), preferred_element_type=F32)


def low_halves(a, b):
    return jnp.concatenate([a[:, :64], b[:, :64]], axis=1)


def high_halves(a, b):
    return jnp.concatenate([a[:, 64:], b[:, 64:]], axis=1)


def unpack(ref, x_ref, base, rows):
    for z in range(NZ):
        lanes = slice(128 * z, 128 * z + 128)
        x_ref[base : base + rows, lanes] = ref[z, :rows, 0:128]
        x_ref[base + rows : base + 2 * rows, lanes] = ref[z, :rows, 256:384]
    for pair in range(NZ // 2):
        lanes = slice(128 * (NZ + pair), 128 * (NZ + pair) + 128)
        even = ref[2 * pair, :rows, 128:256]
        odd = ref[2 * pair + 1, :rows, 128:256]
        x_ref[base : base + rows, lanes] = low_halves(even, odd)
        x_ref[base + rows : base + 2 * rows, lanes] = high_halves(even, odd)


def pack(ref, tile, value, rows):
    lower, upper = value[:rows], value[rows : 2 * rows]
    if tile < NZ:
        ref[tile, :rows, 0:128] = lower
        ref[tile, :rows, 256:384] = upper
    else:
        pair = tile - NZ
        ref[2 * pair, :rows, 128:256] = low_halves(lower, upper)
        ref[2 * pair + 1, :rows, 128:256] = high_halves(lower, upper)


def coupling_matrix(weights):
    size = 12 * CB
    rows = lax.broadcasted_iota(jnp.int32, (size, 128), 0)
    cols = lax.broadcasted_iota(jnp.int32, (size, 128), 1)
    expand = (rows // CB == cols).astype(F32).astype(BF)
    wide = dot_nt(dot(expand, weights).astype(BF), expand)
    left = lax.broadcasted_iota(jnp.int32, (size, size), 0)
    right = lax.broadcasted_iota(jnp.int32, (size, size), 1)
    return jnp.where(left % CB == right % CB, wide, 0.0).astype(BF)


def pack_kernel(points_ref, select_ref, wide_ref, send_ref):
    wide = dot_tn(points_ref[...], select_ref[...]).astype(BF)
    wide_ref[...] = wide
    for s in range(NZ):
        for first in range(2):
            send_ref[s, CB * first : CB * first + CB, :] = wide[
                CB * s : CB * s + CB, 384 * first : 384 * first + 384
            ]


def turn_kernel(points_ref, select_ref, wide_ref):
    wide_ref[...] = dot_tn(points_ref[...], select_ref[...]).astype(BF)


def spectral(x, table_ref, gain_ref, filt_ref, sign):
    for q in range(MP // 256):
        lanes = slice(256 * q, 256 * q + 256)
        upper = slice(MP + 256 * q, MP + 256 * q + 256)
        part_a = dot(x, table_ref[:, lanes])
        part_b = dot(x, table_ref[:, upper])
        for g in range(12):
            rows = slice(CB * g, CB * g + CB)
            real = gain_ref[g : g + 1, lanes]
            imag = sign * gain_ref[12 + g : 13 + g, lanes]
            filt_ref[rows, lanes] = (real * part_a[rows] - imag * part_b[rows]).astype(BF)
            filt_ref[rows, upper] = (real * part_b[rows] + imag * part_a[rows]).astype(BF)


def filter_kernel(
    low_ref, own_ref, high_ref, weights_ref, gain_ref, table_ref, send_ref, x_ref, filt_ref
):
    for band, ref in enumerate((low_ref, own_ref, high_ref)):
        unpack(ref, x_ref, 64 * band, 32)
    basis = dot(coupling_matrix(weights_ref[...]), x_ref[...]).astype(BF)
    spectral(basis, table_ref, gain_ref, filt_ref, 1.0)
    for q in range(KP // 256):
        rows = slice(256 * q, 256 * q + 256)
        result = (dot_nt(filt_ref[...], table_ref[rows, :]) * (2.0 / NLON)).astype(BF)
        pack(send_ref, 2 * q, result[:, :128], 96)
        pack(send_ref, 2 * q + 1, result[:, 128:], 96)


def gelu_parts(hidden):
    inner_part = GELU_SCALE * (hidden + CUBIC_TERM * hidden * hidden * hidden)
    tangent = jnp.tanh(inner_part)
    gelu_value = 0.5 * hidden * (1.0 + tangent)
    gelu_slope = 0.5 * (1.0 + tangent) + 0.5 * hidden * (1.0 - tangent * tangent) * GELU_SCALE * (
        1.0 + 3.0 * CUBIC_TERM * hidden * hidden
    )
    return (gelu_value, gelu_slope)


def mlp_kernel(
    recv_ref,
    fields_ref,
    cot_ref,
    filter_ref,
    inner_ref,
    outer_ref,
    send_ref,
    state_grad_ref,
    grads_ref,
):
    mix = jnp.concatenate(
        [filter_ref[k, CB * s : CB * s + CB, :] for s in range(NZ) for k in range(NK)], axis=0
    )
    inner = inner_ref[...]
    outer = outer_ref[...]
    sums = None
    for first in range(2):
        lanes = slice(384 * first, 384 * first + 384)
        filtered = jnp.concatenate(
            [recv_ref[s, 48 * first : 48 * first + 48, :] for s in range(NZ)], axis=0
        )
        cot = cot_ref[:, lanes]
        state = (fields_ref[:, lanes].astype(F32) + dot_tn(mix, filtered)).astype(BF)
        hidden = dot_tn(inner, state)
        value, slope = gelu_parts(hidden)
        active = value.astype(BF)
        d_hidden = (dot(outer, cot) * slope).astype(BF)
        d_state = cot.astype(F32) + dot(inner, d_hidden)
        state_grad_ref[:, lanes] = d_state
        d_state_b = d_state.astype(BF)
        d_filtered = dot(mix, d_state_b).astype(BF)
        for s in range(NZ):
            send_ref[s, 48 * first : 48 * first + 48, :] = d_filtered[48 * s : 48 * s + 48]
        parts = (dot_nt(filtered, d_state_b), dot_nt(active, cot), dot_nt(state, d_hidden))
        sums = parts if sums is None else tuple(a + b for a, b in zip(sums, parts))
    grads_ref[0:384, :] = sums[0].astype(BF)
    grads_ref[384:640, :] = sums[1].astype(BF)
    grads_ref[640:768, :] = sums[2][:, :128].astype(BF)
    grads_ref[768:896, :] = sums[2][:, 128:].astype(BF)
    for s in range(NZ):
        chunk_out(send_ref, s, 96, grads_ref[112 * s : 112 * s + 112, :])


def chunk_out(ref, s, base, chunk):
    ref[s, base : base + 48, 0:128] = chunk[0:48]
    ref[s, base : base + 48, 128:256] = chunk[48:96]
    ref[s, base : base + 16, 256:384] = chunk[96:112]
    ref[s, base + 16 : base + 48, 256:384] = jnp.zeros((32, 128), BF)


def chunk_sum_kernel(recv_ref, out_ref):
    total = recv_ref[0].astype(F32)
    for z in range(1, NZ):
        total = total + recv_ref[z].astype(F32)
    total = total.astype(BF)
    out_ref[0:48, :] = total[:, 0:128]
    out_ref[48:96, :] = total[:, 128:256]
    out_ref[96:128, :] = total[0:32, 256:384]


def adjoint_kernel(
    recv_ref,
    weights_ref,
    gain_ref,
    table_ref,
    low_ref,
    own_ref,
    high_ref,
    x_ref,
    filt_ref,
):
    unpack(recv_ref, x_ref, 0, 96)
    spectral(x_ref[...], table_ref, gain_ref, filt_ref, -1.0)
    coupling = coupling_matrix(weights_ref[...])
    for q in range(KP // 256):
        rows = slice(256 * q, 256 * q + 256)
        result = (dot_nt(filt_ref[...], table_ref[rows, :]) * (2.0 / NLON)).astype(BF)
        parts = dot(coupling, result)
        for half in range(2):
            lanes = slice(128 * half, 128 * half + 128)
            pack(low_ref, 2 * q + half, parts[0:64, lanes].astype(BF), 32)
            pack(own_ref, 2 * q + half, parts[64:128, lanes], 32)
            pack(high_ref, 2 * q + half, parts[128:192, lanes].astype(BF), 32)


def halo_sum_kernel(own_ref, from_high_ref, from_low_ref, chunk_ref, send_ref):
    chunk = chunk_ref[...]
    for z in range(NZ):
        total = own_ref[z] + from_high_ref[z].astype(F32) + from_low_ref[z].astype(F32)
        send_ref[z, 0:32, :] = total.astype(BF)
        chunk_out(send_ref, z, 32, chunk)


def finish_kernel(scale, recv_ref, state_grad_ref, select_ref, grad_ref, filter_ref, inner_ref, outer_ref, all_ref):
    for first in range(2):
        lanes = slice(384 * first, 384 * first + 384)
        lat_part = jnp.concatenate(
            [recv_ref[s, CB * first : CB * first + CB, :] for s in range(NZ)], axis=0
        )
        total = (state_grad_ref[:, lanes] + lat_part.astype(F32)).astype(BF)
        part = dot_nt(select_ref[:, lanes], total)
        if first == 0:
            held = part
        else:
            grad_ref[...] = (held + part).astype(BF)
    for s in range(NZ):
        base = 112 * s
        all_ref[base : base + 48, :] = recv_ref[s, 32:80, 0:128].astype(F32) * scale
        all_ref[base + 48 : base + 96, :] = recv_ref[s, 32:80, 128:256].astype(F32) * scale
        all_ref[base + 96 : base + 112, :] = recv_ref[s, 32:48, 256:384].astype(F32) * scale
    for s in range(NZ):
        for k in range(NK):
            base = 48 * s + CB * k
            filter_ref[k, CB * s : CB * s + CB, :] = all_ref[base : base + CB, :]
    outer_ref[...] = all_ref[384:640, :]
    inner_ref[:, :128] = all_ref[640:768, :]
    inner_ref[:, 128:] = all_ref[768:896, :]


def call(kernel, outs, flops, scratch=(), in_specs=None):
    single = not isinstance(outs, (list, tuple))
    shapes = [outs] if single else list(outs)
    moved = sum(math.prod(o.shape) * o.dtype.itemsize for o in shapes)
    run = pl.pallas_call(
        kernel,
        out_shape=outs,
        in_specs=in_specs,
        out_specs=jax.tree.map(lambda _: pl.BlockSpec(memory_space=pltpu.VMEM), outs),
        scratch_shapes=scratch,
        compiler_params=pltpu.CompilerParams(vmem_limit_bytes=LIMIT),
        cost_estimate=pl.CostEstimate(flops=flops, bytes_accessed=2 * moved, transcendentals=0),
    )
    return run


def shaped(shape, dtype=BF):
    return jax.ShapeDtypeStruct(shape, dtype)


def vmem(count):
    return [pl.BlockSpec(memory_space=pltpu.VMEM)] * count


def shifted(value, axis, steps):
    count = lax.axis_size(axis)
    leading, last = (max(0, -steps), min(count, count - steps))
    return lax.ppermute(value, axis, [(source, source + steps) for source in range(leading, last)])


def local(
    fields,
    cotangent,
    basis_weights,
    band_support,
    spectrum_real,
    spectrum_imag,
    filter_weights,
    inner_weights,
    outer_weights,
):
    group = lax.axis_size("ens") * lax.axis_size("lat")
    grad_scale = 1.0 / math.sqrt(group * NR * NLON)
    table = jnp.asarray(dft_table())
    select = jnp.asarray(point_select())

    field_points = fields[0].transpose(1, 0, 2).reshape(LON * NR, 128)
    cot_points = cotangent[0].transpose(1, 0, 2).reshape(LON * NR, 128)
    field_wide, send_fields = call(
        pack_kernel, (shaped((128, 768)), shaped((NZ, 32, 384))), 2 * 720 * 768 * 128, (), vmem(2)
    )(field_points, select)
    own = lax.all_to_all(send_fields, "lon", 0, 0, tiled=True)

    cot_wide = call(turn_kernel, shaped((128, 768)), 2 * 720 * 768 * 128, (), vmem(2))(
        cot_points, select
    )
    mask = jnp.repeat(band_support[0], NR).astype(BF)
    masked = (basis_weights * mask[None, None, :]).transpose(1, 0, 2).reshape(12, 12)
    weights = jnp.pad(masked, ((0, 116), (0, 116)))
    weights_t = jnp.pad(masked.T, ((0, 116), (0, 116)))
    first_half = jnp.where(jnp.arange(MODES) == 0, 0.5, 1.0).astype(F32)
    gains = jnp.concatenate(
        [
            (s * first_half).transpose(1, 0, 2).reshape(12, MODES)
            for s in (spectrum_real, spectrum_imag)
        ],
        axis=0,
    )
    gains = jnp.pad(gains, ((0, 0), (0, MP - MODES)))

    low = shifted(own, "lat", 1)
    high = shifted(own, "lat", -1)
    work = [pltpu.VMEM((192, KP), BF), pltpu.VMEM((192, KP), BF)]
    send_filtered = call(
        filter_kernel, shaped((NZ, 96, 384)), 4 * 192 * KP * KP, work, vmem(6)
    )(low, own, high, weights, gains, table)
    filtered = lax.all_to_all(send_filtered, "lon", 0, 0, tiled=True)

    send_back, state_grad = call(
        mlp_kernel,
        (shaped((NZ, 144, 384)), shaped((128, 768), F32)),
        2 * 768 * 128 * 256 * 10,
        [pltpu.VMEM((896, 128), BF)],
        vmem(6),
    )(filtered, field_wide, cot_wide, filter_weights, inner_weights, outer_weights)
    back = lax.all_to_all(send_back, "lon", 0, 0, tiled=True)

    chunk = pl.pallas_call(
        chunk_sum_kernel,
        grid=(1,),
        in_specs=[pl.BlockSpec((NZ, 48, 384), lambda i: (0, 2, 0))],
        out_specs=pl.BlockSpec((128, 128), lambda i: (0, 0)),
        out_shape=shaped((128, 128)),
        cost_estimate=pl.CostEstimate(flops=150000, bytes_accessed=400000, transcendentals=0),
    )(back)
    share = 128 // group
    ids = np.arange(128) % share
    same = jnp.asarray((ids[:, None] == ids[None, :]).astype(ml_dtypes.bfloat16))
    chunk = lax.all_to_all(chunk, ("ens", "lat"), 0, 0, tiled=True)
    chunk = dot(same, chunk).astype(BF)
    chunk = lax.all_to_all(chunk, ("ens", "lat"), 0, 0, tiled=True)

    to_low, kept, to_high = call(
        adjoint_kernel,
        (shaped((NZ, 32, 384)), shaped((NZ, 32, 384), F32), shaped((NZ, 32, 384))),
        4 * 192 * KP * KP,
        work,
        vmem(4),
    )(back, weights_t, gains, table)
    from_high = shifted(to_low, "lat", -1)
    from_low = shifted(to_high, "lat", 1)
    send_lat = call(halo_sum_kernel, shaped((NZ, 80, 384)), 300000, (), vmem(4))(
        kept, from_high, from_low, chunk
    )
    lat_parts = lax.all_to_all(send_lat, "lon", 0, 0, tiled=True)

    def finish(*refs):
        finish_kernel(grad_scale, *refs)

    grad_points, filter_grad, inner_grad, outer_grad = call(
        finish,
        (
            shaped((LON * NR, 128)),
            shaped((NK, 128, 128), F32),
            shaped((128, 256), F32),
            shaped((256, 128), F32),
        ),
        2 * 720 * 768 * 128,
        [pltpu.VMEM((896, 128), F32)],
        vmem(3),
    )(lat_parts, state_grad, select)
    field_grad = grad_points.reshape(LON, NR, 128).transpose(1, 0, 2)[None]
    return (field_grad, filter_grad, inner_grad, outer_grad)


def solution(mesh):
    placed = (
        P("ens", "lat", "lon", None),
        P("ens", "lat", "lon", None),
        P(None, "lat", None),
        P("lat", None),
        P(None, "lat", None),
        P(None, "lat", None),
        P(),
        P(),
        P(),
    )
    return jax.shard_map(
        local,
        mesh=mesh,
        in_specs=placed,
        out_specs=(P("ens", "lat", "lon", None), P(), P(), P()),
        check_vma=False,
    )
```

time: 627 us -> 164 us (0.26)
  waiting for transfers between devices: 324 us -> 50.9 us
  matrix products: 163 us -> 0.13 us
  local copies, waits for them, and re-layouts: 61.7 us -> 6.99 us
  Pallas kernels: 0 us -> 18.4 us
  starting transfers between devices: 28.2 us -> 45.9 us
  blocking collectives: 20.7 us -> 37.4 us
  between operations: 16.7 us -> 0.86 us
    psum x1 -> x0, waiting for transfers between devices: 279 us -> none  [local(): lax.psum((filter_local, inner_local, outer_local), ('ens', 'lat', 'lon'))]
    dot_general x22 -> x1, matrix products: 163 us -> 0.13 us  [dot(): return jnp.dot(a, b, preferred_element_type=F32)]
    unnamed x40 -> x22, local copies, waits for them, and re-layouts: 26.3 us -> 6.63 us
    all_to_all x3 -> x4, starting transfers between devices: 13.5 us -> 32.7 us  [the longest x1 14.5 us: local(): chunk = lax.all_to_all(chunk, ('ens', 'lat'), 0, 0, tiled=True)]
    pallas_call x0 -> x8, Pallas kernels: none -> 18.4 us  [the longest x1 7.1 us: local(): call(adjoint_kernel, (shaped((NZ, 32, 384)), shaped((NZ, 32, 384), F32),...]
    all_to_all x1 -> x2, blocking collectives: 20.7 us -> 37.4 us  [the longest x1 19.2 us: local(): chunk = lax.all_to_all(chunk, ('ens', 'lat'), 0, 0, tiled=True)]
    convert_element_type x5 -> x1, local copies, waits for them, and re-layouts: 15.2 us -> 0.09 us  [local(): mask = jnp.repeat(band_support[0], NR).astype(BF)]
    all_to_all x8 -> x0, local copies, waits for them, and re-layouts: 14.7 us -> none  [the longest x1 6 us: local(): lax.all_to_all(filtered_moved, 'lon', split_axis=3, concat_axis=2, tiled=...]
  transfers between devices with their start and end apart: 8 -> 8, of which waited for: 4 -> 4; matrix products, arithmetic and copies ran while one was open for 3% -> 2% of each run, Pallas kernels for 0% -> 5%
where the time goes in v1:
time: 164 us; the launch traced here: 163 us
  waiting for transfers between devices  50.9 us (31%)
  starting transfers between devices  45.9 us (28%)
  blocking collectives  37.4 us (23%)
  Pallas kernels  18.4 us (11%)
  local copies, waits for them, and re-layouts  6.99 us (4%)
  other arithmetic  2.17 us (1%)
    all_to_all x1, waiting for transfers between devices, local(): back = lax.all_to_all(send_back, 'lon', 0, 0, tiled=True)  24 us
    all_to_all x1, blocking collectives, local(): chunk = lax.all_to_all(chunk, ('ens', 'lat'), 0, 0, tiled=True)  19.2 us
    all_to_all x1, blocking collectives, local(): lat_parts = lax.all_to_all(send_lat, 'lon', 0, 0, tiled=True)  18.3 us
    all_to_all x1, waiting for transfers between devices, local(): filtered = lax.all_to_all(send_filtered, 'lon', 0, 0, tiled=True)  15.5 us
    all_to_all x1, starting transfers between devices, local(): chunk = lax.all_to_all(chunk, ('ens', 'lat'), 0, 0, tiled=True)  14.5 us
    ppermute x4, starting transfers between devices, shifted(): lax.ppermute(value, axis, [(source, source + steps) for source in range(l...  13.2 us
    all_to_all x1, starting transfers between devices, local(): own = lax.all_to_all(send_fields, 'lon', 0, 0, tiled=True)  11 us
    all_to_all x1, waiting for transfers between devices, local(): own = lax.all_to_all(send_fields, 'lon', 0, 0, tiled=True)  7.2 us
  transfers between devices with their start and end apart: 8, of which 4 were waited for; matrix products, arithmetic and copies ran while one was open for 2% of the time, Pallas kernels for 5%

profile of v1, /device:TPU:1, one launch (start us, length us, event | category | flops | bytes accessed | tf_op | source)
XLA Modules:
  0.0 162.8 jit_solution(11916407760838121900)
XLA Ops:
  0.6 0.0 copy-start
  0.6 1.2 copy-done
  1.9 0.0 copy-start.4
  1.9 0.9 copy-done.4
  2.8 1.0 shard_map.147
  3.8 0.0 copy-start.1
  3.8 0.0 copy-start.5
  3.8 11.0 %all-to-all-start = ((bf16[8,32,384]{2,1,0:T(8,128)(2,1)}), bf16[8,32,384]{2,1,0:T(8,128)(2,1)S(1)}, u32[]{:S(2)}, u32[]{:S(2)}) async-start(bf16[8,32,384]{2,1,0:T(8,128)(2,1)} %get-tuple-element.15), calls=%async_computation | async-start | bytes 393216 | tf_op jit(solution)/shard_map/all_to_all | solution.py:334
  14.8 0.7 convert_bitcast_fusion
  15.5 0.1 broadcast_in_dim.17
  15.6 0.1 convert_element_type.27
  15.7 0.8 multiply_bitcast_fusion.1
  16.5 7.2 %all-to-all-done.own_ref = bf16[8,32,384]{2,1,0:T(8,128)(2,1)S(1)} async-done(((bf16[8,32,384]{2,1,0:T(8,128)(2,1)}), bf16[8,32,384]{2,1,0:T(8,128)(2,1)S(1)}, u32[]{:S(2)}, u32[]{:S(2)}) %all-to-all-start) | async-done | bytes 196640 | tf_op jit(solution)/shard_map/all_to_all | solution.py:334
  23.7 5.7 %collective-permute-start = (bf16[8,32,384]{2,1,0:T(8,128)(2,1)S(1)}, bf16[8,32,384]{2,1,0:T(8,128)(2,1)S(1)}, u32[]{:S(2)}, u32[]{:S(2)}) collective-permute-start(bf16[8,32,384]{2,1,0:T(8,128)(2,1)S(1)} %all-to-all-done.own_ref), channel_id=1, source_target_pairs={{0,8},{8,16},{16,24},{24,32},{32,40},{40,48},{48,56},{56,64},{64,7... | collective-permute-start | bytes 589832 | tf_op jit(solution)/shard_map/ppermute | solution.py:310
  29.4 1.9 %collective-permute-start.1 = (bf16[8,32,384]{2,1,0:T(8,128)(2,1)S(1)}, bf16[8,32,384]{2,1,0:T(8,128)(2,1)S(1)}, u32[]{:S(2)}, u32[]{:S(2)}) collective-permute-start(bf16[8,32,384]{2,1,0:T(8,128)(2,1)S(1)} %all-to-all-done.own_ref), channel_id=1, source_target_pairs={{8,0},{16,8},{24,16},{32,24},{40,32},{48,40},{56,48},{64,56},{72,6... | collective-permute-start | bytes 589832 | tf_op jit(solution)/shard_map/ppermute | solution.py:310
  31.3 0.7 multiply_bitcast_fusion.2
  32.1 0.0 copy-start.6
  32.1 0.0 copy-start.7
  32.2 0.0 copy-start.8
  32.2 0.0 collective-permute-done.low_ref
  32.2 4.2 %collective-permute-done.1.high_ref = bf16[8,32,384]{2,1,0:T(8,128)(2,1)S(1)} collective-permute-done((bf16[8,32,384]{2,1,0:T(8,128)(2,1)S(1)}, bf16[8,32,384]{2,1,0:T(8,128)(2,1)S(1)}, u32[]{:S(2)}, u32[]{:S(2)}) %collective-permute-start.1) | collective-permute-done | bytes 196640 | tf_op jit(solution)/shard_map/ppermute | solution.py:310
  36.3 0.0 copy-start.9
  36.3 2.3 %copy-done.9 = bf16[1536,1536]{1,0:T(8,128)(2,1)S(1)} copy-done((bf16[1536,1536]{1,0:T(8,128)(2,1)S(1)}, bf16[1536,1536]{1,0:T(8,128)(2,1)}, u32[]{:S(2)}) %copy-start.9) | copy-done | bytes 4718616
  38.7 3.7 %shard_map.148 = bf16[8,96,384]{2,1,0:T(8,128)(2,1)} custom-call(bf16[8,32,384]{2,1,0:T(8,128)(2,1)S(1)} %collective-permute-done.low_ref, bf16[8,32,384]{2,1,0:T(8,128)(2,1)S(1)} %all-to-all-done.own_ref, bf16[8,32,384]{2,1,0:T(8,128)(2,1)S(1)} %collective-permute-done.1.high_ref, bf16[128,128]{1,0:T(8,128)(2,1)S(1)} %pad.11.weights_ref, ...), custom_call_target="tpu_custom_call" | custom-call | flops 1811939328 | bytes 1179648 | tf_op jit(solution)/shard_map/pallas_call | solution.py:356
  42.4 3.5 %all-to-all-start.1 = ((bf16[8,96,384]{2,1,0:T(8,128)(2,1)}), bf16[8,96,384]{2,1,0:T(8,128)(2,1)S(1)}, u32[]{:S(2)}, u32[]{:S(2)}) async-start(bf16[8,96,384]{2,1,0:T(8,128)(2,1)} %shard_map.148), calls=%async_computation.1 | async-start | bytes 1179648 | tf_op jit(solution)/shard_map/all_to_all | solution.py:359
  46.0 0.0 copy-done.1
  46.0 0.0 copy-done.5
  46.0 0.4 shard_map.149.cot_ref
  46.3 15.5 %all-to-all-done.1.recv_ref = bf16[8,96,384]{2,1,0:T(8,128)(2,1)S(1)} async-done(((bf16[8,96,384]{2,1,0:T(8,128)(2,1)}), bf16[8,96,384]{2,1,0:T(8,128)(2,1)S(1)}, u32[]{:S(2)}, u32[]{:S(2)}) %all-to-all-start.1) | async-done | bytes 589856 | tf_op jit(solution)/shard_map/all_to_all | solution.py:359
  61.9 0.0 copy-done.6
  61.9 0.0 copy-done.7
  61.9 0.0 copy-done.8
  61.9 3.1 %shard_map.150 = (bf16[8,144,384]{2,1,0:T(8,128)(2,1)}, f32[128,768]{1,0:T(8,128)S(1)}) custom-call(bf16[8,96,384]{2,1,0:T(8,128)(2,1)S(1)} %all-to-all-done.1.recv_ref, bf16[128,768]{1,0:T(8,128)(2,1)S(1)} %get-tuple-element.16.fields_ref, bf16[128,768]{1,0:T(8,128)(2,1)S(1)} %shard_map.149.cot_ref, bf16[3,128,128]{2,1,0:T(8,128)(2,1)S(1)} %copy-done.6, ...), custom_call_target="tpu_custom_call" | custom-call | flops 503316480 | bytes 2555904 | tf_op jit(solution)/shard_map/pallas_call | solution.py:361
  65.0 0.0 copy-start.10
  65.0 3.7 %all-to-all-start.2 = ((bf16[8,144,384]{2,1,0:T(8,128)(2,1)}), bf16[8,144,384]{2,1,0:T(8,128)(2,1)S(1)}, u32[]{:S(2)}, u32[]{:S(2)}) async-start(bf16[8,144,384]{2,1,0:T(8,128)(2,1)} %get-tuple-element.17), calls=%async_computation.2 | async-start | bytes 1769472 | tf_op jit(solution)/shard_map/all_to_all | solution.py:368
  68.7 0.1 copy.23
  68.8 24.0 %all-to-all-done.2.recv_ref = bf16[8,144,384]{2,1,0:T(8,128)(2,1)S(1)} async-done(((bf16[8,144,384]{2,1,0:T(8,128)(2,1)}), bf16[8,144,384]{2,1,0:T(8,128)(2,1)S(1)}, u32[]{:S(2)}, u32[]{:S(2)}) %all-to-all-start.2) | async-done | bytes 884768 | tf_op jit(solution)/shard_map/all_to_all | solution.py:368
  92.8 0.0 copy-start.2
  92.8 0.9 copy-done.2
  93.8 1.6 shard_map.152
  95.4 14.5 %all-to-all-start.3 = ((bf16[64,2,128]{2,1,0:T(2,128)(2,1)}), bf16[64,2,128]{2,1,0:T(2,128)(2,1)S(1)}, u32[]{:S(2)}, u32[]{:S(2)}) async-start(bf16[64,2,128]{2,1,0:T(2,128)(2,1)} %bitcast.36), calls=%async_computation.3 | async-start | bytes 65536 | tf_op jit(solution)/shard_map/all_to_all | solution.py:381
  109.9 0.0 copy-start.3
  109.9 1.2 copy-done.3
  111.1 7.1 %shard_map.151 = (bf16[8,32,384]{2,1,0:T(8,128)(2,1)S(1)}, f32[8,32,384]{2,1,0:T(8,128)S(1)}, bf16[8,32,384]{2,1,0:T(8,128)(2,1)S(1)}) custom-call(bf16[8,144,384]{2,1,0:T(8,128)(2,1)S(1)} %copy-done.3, bf16[128,128]{1,0:T(8,128)(2,1)S(1)} %pad.13.weights_ref, f32[24,768]{1,0:T(8,128)S(1)} %select_maximum_fusion.gain_ref, ...), custom_call_target="tpu_custom_call" | custom-call | flops 1811939328 | bytes 1572864 | tf_op jit(solution)/shard_map/pallas_call | solution.py:385
  118.2 2.4 %collective-permute-start.2 = (bf16[8,32,384]{2,1,0:T(8,128)(2,1)S(1)}, bf16[8,32,384]{2,1,0:T(8,128)(2,1)S(1)}, u32[]{:S(2)}, u32[]{:S(2)}) collective-permute-start(bf16[8,32,384]{2,1,0:T(8,128)(2,1)S(1)} %get-tuple-element.19), channel_id=1, source_target_pairs={{8,0},{16,8},{24,16},{32,24},{40,32},{48,40},{56,48},{64,56},{72,6... | collective-permute-start | bytes 589832 | tf_op jit(solution)/shard_map/ppermute | solution.py:310
  120.6 3.2 %collective-permute-start.3 = (bf16[8,32,384]{2,1,0:T(8,128)(2,1)S(1)}, bf16[8,32,384]{2,1,0:T(8,128)(2,1)S(1)}, u32[]{:S(2)}, u32[]{:S(2)}) collective-permute-start(bf16[8,32,384]{2,1,0:T(8,128)(2,1)S(1)} %get-tuple-element.20), channel_id=1, source_target_pairs={{0,8},{8,16},{16,24},{24,32},{32,40},{40,48},{48,56},{56,64},{64,7... | collective-permute-start | bytes 589832 | tf_op jit(solution)/shard_map/ppermute | solution.py:310
  123.8 0.0 all-to-all-done.3
  123.8 0.0 copy-done.10
  123.8 0.1 convolution_convert_fusion
  123.9 19.2 %all_to_all.43 = bf16[64,2,128]{2,1,0:T(2,128)(2,1)S(1)} all-to-all(bf16[64,2,128]{2,1,0:T(2,128)(2,1)S(1)} %bitcast.37), channel_id=1, replica_groups=mesh['ens'=2,'lat'=32,'lon'=8] {'ens','lat'}, dimensions={0} | all-to-all | bytes 65536 | tf_op jit(solution)/shard_map/all_to_all | solution.py:383
  143.1 0.0 collective-permute-done.2.from_high_ref
  143.1 0.0 collective-permute-done.3.from_low_ref
  143.1 0.1 shard_map.153
  143.2 18.3 %all_to_all.44.refs_0_ = bf16[8,80,384]{2,1,0:T(8,128)(2,1)S(1)} all-to-all(bf16[8,80,384]{2,1,0:T(8,128)(2,1)S(1)} %shard_map.153), channel_id=1, replica_groups=mesh['ens'=2,'lat'=32,'lon'=8] {'lon'}, dimensions={0} | all-to-all | bytes 983040 | tf_op jit(solution)/shard_map/all_to_all | solution.py:397
  161.5 1.3 shard_map.154
  (10 shorter events, 0.1 us)
Async XLA Ops:
  0.6 1.2 copy-start
  1.9 0.9 copy-start.4
  3.8 42.1 %copy-start.1 = (bf16[720,768]{1,0:T(8,128)(2,1)S(1)}, bf16[720,768]{1,0:T(8,128)(2,1)}, u32[]{:S(2)}) copy-start(bf16[720,768]{1,0:T(8,128)(2,1)} %constant.18.clone.select_ref.refs_2_) | copy-start | bytes 3317764
  3.8 42.1 %copy-start.5 = (bf16[1,4,180,128]{3,1,2,0:T(4,128)(2,1)S(1)}, bf16[1,4,180,128]{3,1,2,0:T(4,128)(2,1)}, u32[]{:S(2)}) copy-start(bf16[1,4,180,128]{3,1,2,0:T(4,128)(2,1)} %param.13) | copy-start | bytes 552964
  3.8 19.8 %all-to-all-start = ((bf16[8,32,384]{2,1,0:T(8,128)(2,1)}), bf16[8,32,384]{2,1,0:T(8,128)(2,1)S(1)}, u32[]{:S(2)}, u32[]{:S(2)}) async-start(bf16[8,32,384]{2,1,0:T(8,128)(2,1)} %get-tuple-element.15), calls=%async_computation | async-start | bytes 393216 | tf_op jit(solution)/shard_map/all_to_all | solution.py:334
  23.7 8.5 %collective-permute-start = (bf16[8,32,384]{2,1,0:T(8,128)(2,1)S(1)}, bf16[8,32,384]{2,1,0:T(8,128)(2,1)S(1)}, u32[]{:S(2)}, u32[]{:S(2)}) collective-permute-start(bf16[8,32,384]{2,1,0:T(8,128)(2,1)S(1)} %all-to-all-done.own_ref), channel_id=1, source_target_pairs={{0,8},{8,16},{16,24},{24,32},{32,40},{40,48},{48,56},{56,64},{64,7... | collective-permute-start | bytes 589832 | tf_op jit(solution)/shard_map/ppermute | solution.py:310
  29.4 7.0 %collective-permute-start.1 = (bf16[8,32,384]{2,1,0:T(8,128)(2,1)S(1)}, bf16[8,32,384]{2,1,0:T(8,128)(2,1)S(1)}, u32[]{:S(2)}, u32[]{:S(2)}) collective-permute-start(bf16[8,32,384]{2,1,0:T(8,128)(2,1)S(1)} %all-to-all-done.own_ref), channel_id=1, source_target_pairs={{8,0},{16,8},{24,16},{32,24},{40,32},{48,40},{56,48},{64,56},{72,6... | collective-permute-start | bytes 589832 | tf_op jit(solution)/shard_map/ppermute | solution.py:310
  32.1 29.7 %copy-start.6 = (bf16[3,128,128]{2,1,0:T(8,128)(2,1)S(1)}, bf16[3,128,128]{2,1,0:T(8,128)(2,1)}, u32[]{:S(2)}) copy-start(bf16[3,128,128]{2,1,0:T(8,128)(2,1)} %filter_ref.1) | copy-start | bytes 294916
  32.1 29.7 %copy-start.7 = (bf16[128,256]{1,0:T(8,128)(2,1)S(1)}, bf16[128,256]{1,0:T(8,128)(2,1)}, u32[]{:S(2)}) copy-start(bf16[128,256]{1,0:T(8,128)(2,1)} %inner_ref.1) | copy-start | bytes 196612
  32.2 29.7 %copy-start.8 = (bf16[256,128]{1,0:T(8,128)(2,1)S(1)}, bf16[256,128]{1,0:T(8,128)(2,1)}, u32[]{:S(2)}) copy-start(bf16[256,128]{1,0:T(8,128)(2,1)} %outer_ref.1) | copy-start | bytes 196612
  36.3 2.3 %copy-start.9 = (bf16[1536,1536]{1,0:T(8,128)(2,1)S(1)}, bf16[1536,1536]{1,0:T(8,128)(2,1)}, u32[]{:S(2)}) copy-start(bf16[1536,1536]{1,0:T(8,128)(2,1)} %constant.17.clone.table_ref) | copy-start | bytes 14155780
  42.4 19.5 %all-to-all-start.1 = ((bf16[8,96,384]{2,1,0:T(8,128)(2,1)}), bf16[8,96,384]{2,1,0:T(8,128)(2,1)S(1)}, u32[]{:S(2)}, u32[]{:S(2)}) async-start(bf16[8,96,384]{2,1,0:T(8,128)(2,1)} %shard_map.148), calls=%async_computation.1 | async-start | bytes 1179648 | tf_op jit(solution)/shard_map/all_to_all | solution.py:359
  65.0 58.8 %copy-start.10 = (bf16[128,128]{1,0:T(8,128)(2,1)S(1)}, bf16[128,128]{1,0:T(8,128)(2,1)}, u32[]{:S(2)}) copy-start(bf16[128,128]{1,0:T(8,128)(2,1)} %constant.19.clone) | copy-start | bytes 98308
  65.0 27.8 %all-to-all-start.2 = ((bf16[8,144,384]{2,1,0:T(8,128)(2,1)}), bf16[8,144,384]{2,1,0:T(8,128)(2,1)S(1)}, u32[]{:S(2)}, u32[]{:S(2)}) async-start(bf16[8,144,384]{2,1,0:T(8,128)(2,1)} %get-tuple-element.17), calls=%async_computation.2 | async-start | bytes 1769472 | tf_op jit(solution)/shard_map/all_to_all | solution.py:368
  92.8 0.9 copy-start.2
  95.4 28.4 %all-to-all-start.3 = ((bf16[64,2,128]{2,1,0:T(2,128)(2,1)}), bf16[64,2,128]{2,1,0:T(2,128)(2,1)S(1)}, u32[]{:S(2)}, u32[]{:S(2)}) async-start(bf16[64,2,128]{2,1,0:T(2,128)(2,1)} %bitcast.36), calls=%async_computation.3 | async-start | bytes 65536 | tf_op jit(solution)/shard_map/all_to_all | solution.py:381
  109.9 1.2 copy-start.3
  118.2 24.9 %collective-permute-start.2 = (bf16[8,32,384]{2,1,0:T(8,128)(2,1)S(1)}, bf16[8,32,384]{2,1,0:T(8,128)(2,1)S(1)}, u32[]{:S(2)}, u32[]{:S(2)}) collective-permute-start(bf16[8,32,384]{2,1,0:T(8,128)(2,1)S(1)} %get-tuple-element.19), channel_id=1, source_target_pairs={{8,0},{16,8},{24,16},{32,24},{40,32},{48,40},{56,48},{64,56},{72,6... | collective-permute-start | bytes 589832 | tf_op jit(solution)/shard_map/ppermute | solution.py:310
  120.6 22.5 %collective-permute-start.3 = (bf16[8,32,384]{2,1,0:T(8,128)(2,1)S(1)}, bf16[8,32,384]{2,1,0:T(8,128)(2,1)S(1)}, u32[]{:S(2)}, u32[]{:S(2)}) collective-permute-start(bf16[8,32,384]{2,1,0:T(8,128)(2,1)S(1)} %get-tuple-element.20), channel_id=1, source_target_pairs={{0,8},{8,16},{16,24},{24,32},{32,40},{40,48},{48,56},{56,64},{64,7... | collective-permute-start | bytes 589832 | tf_op jit(solution)/shard_map/ppermute | solution.py:310

commit v2 on v1

v2 whole, which is shorter than its diff:
```python
import math

import jax
import jax.numpy as jnp
import ml_dtypes
import numpy as np
from jax import lax
from jax.experimental import pallas as pl
from jax.experimental.pallas import tpu as pltpu
from jax.sharding import PartitionSpec as P

GELU_SCALE = 0.7978845608028654
CUBIC_TERM = 0.044715
BF = jnp.bfloat16
F32 = jnp.float32
NLON = 1440
NZ = 8
LON = 180
MODES = 720
MP = 384
KP = 768
CB = 16
NK = 3
NR = 4
WIDE = 1024
LIMIT = 24 * 1024 * 1024


def dft_table():
    lane = np.arange(KP)
    tail = lane >= 512
    owner = np.where(tail, 2 * ((lane - 512) // 128) + (lane % 128 >= 64), lane // 128)
    place = np.where(tail, 128 + lane % 64, lane % 128)
    column = owner * LON + place
    tables = []
    for parity in range(2):
        frequency = 2 * np.arange(MP) + parity
        phase = 2.0 * math.pi * ((column[:, None] * frequency[None, :]) % NLON) / NLON
        valid = (place < LON)[:, None] & (frequency < MODES)[None, :]
        cos = np.where(valid, np.cos(phase), 0.0)
        sin = np.where(valid, -np.sin(phase), 0.0)
        tables.append(np.concatenate([cos, sin], axis=1))
    return np.stack(tables).astype(ml_dtypes.bfloat16)


def dot(a, b):
    return jnp.dot(a, b, preferred_element_type=F32)


def dot_tn(a, b):
    return lax.dot_general(a, b, (((0,), (0,)), ((), ())), preferred_element_type=F32)


def dot_nt(a, b):
    return lax.dot_general(a, b, (((1,), (1,)), ((), ())), preferred_element_type=F32)


def low_halves(a, b):
    return jnp.concatenate([a[:, :64], b[:, :64]], axis=1)


def high_halves(a, b):
    return jnp.concatenate([a[:, 64:], b[:, 64:]], axis=1)


def iota(shape, dim):
    return lax.broadcasted_iota(jnp.int32, shape, dim)


def point_select():
    lane = iota((8, 2 * 384), 1)
    first = (lane >= 384).astype(jnp.int32)
    lane = lane - 384 * first
    middle = (lane >= 128) & (lane < 256)
    upper = ((lane >= 192)).astype(jnp.int32)
    place = jnp.where(middle, 128 + (lane & 63), lane & 127)
    point = jnp.where(place < LON, place * NR + 2 * upper + first, -1)
    return (iota((LON * NR, 2 * 384), 0) == point[0:1]).astype(F32).astype(BF)


def tile_of(z):
    return 6 * (z // 4) + z % 4


def tile_of_pair(pair):
    return 6 * (pair // 2) + 4 + pair % 2


def unpack(ref, x_ref, base, rows):
    for z in range(NZ):
        lanes = slice(128 * tile_of(z), 128 * tile_of(z) + 128)
        x_ref[base : base + rows, lanes] = ref[z, :, 0:128]
        x_ref[base + rows : base + 2 * rows, lanes] = ref[z, :, 256:384]
    for pair in range(NZ // 2):
        lanes = slice(128 * tile_of_pair(pair), 128 * tile_of_pair(pair) + 128)
        even = ref[2 * pair, :, 128:256]
        odd = ref[2 * pair + 1, :, 128:256]
        x_ref[base : base + rows, lanes] = low_halves(even, odd)
        x_ref[base + rows : base + 2 * rows, lanes] = high_halves(even, odd)


def pack(ref, half, value, rows):
    for t in range(4):
        lanes = slice(128 * t, 128 * t + 128)
        ref[4 * half + t, :, 0:128] = value[:rows, lanes]
        ref[4 * half + t, :, 256:384] = value[rows:, lanes]
    for t in range(2):
        lanes = slice(512 + 128 * t, 640 + 128 * t)
        lower, upper = value[:rows, lanes], value[rows:, lanes]
        ref[4 * half + 2 * t, :, 128:256] = low_halves(lower, upper)
        ref[4 * half + 2 * t + 1, :, 128:256] = high_halves(lower, upper)


def bring(pairs, sems):
    copies = [
        pltpu.make_async_copy(source, target, sems.at[n]) for n, (source, target) in enumerate(pairs)
    ]
    for copy in copies:
        copy.start()
    return copies


def pack_kernel(points_hbm, wide_ref, send_ref, points_ref, sems):
    copies = bring([(points_hbm, points_ref)], sems)
    select = point_select()
    copies[0].wait()
    wide = dot_tn(points_ref[...], select).astype(BF)
    wide_ref[...] = wide
    for s in range(NZ):
        for first in range(2):
            send_ref[s, CB * first : CB * first + CB, :] = wide[
                CB * s : CB * s + CB, 384 * first : 384 * first + 384
            ]


def prepare_kernel(
    points_hbm,
    weights_hbm,
    real_hbm,
    imag_hbm,
    support_hbm,
    wide_ref,
    coupling_ref,
    turned_hbm,
    gain_ref,
    turned_ref,
    points_ref,
    weights_ref,
    real_ref,
    imag_ref,
    support_ref,
    sems,
):
    copies = bring(
        (
            (points_hbm, points_ref),
            (weights_hbm, weights_ref),
            (real_hbm, real_ref),
            (imag_hbm, imag_ref),
            (support_hbm, support_ref),
        ),
        sems,
    )
    select = point_select()
    copies[0].wait()
    wide_ref[...] = dot_tn(points_ref[...], select).astype(BF)

    for copy in copies[1:]:
        copy.wait()
    flip = lax.rem(lax.axis_index("lat"), 2) == 0
    lane = iota((1, 12), 1)
    seen = support_ref[...]
    seen = jnp.where(lane < 4, seen[:, 0:1], jnp.where(lane < 8, seen[:, 1:2], seen[:, 2:3]))
    seen = seen.astype(F32)
    rows = [weights_ref[k].astype(F32) for k in range(NK)]
    masked = jnp.concatenate([rows[k][i : i + 1] * seen for i in range(NR) for k in range(NK)], axis=0)
    turned = jnp.concatenate([masked[:, 8:12], masked[:, 4:8], masked[:, 0:4]], axis=1)
    masked = jnp.where(flip, turned, masked).astype(BF)
    size = 12 * CB
    expand = (iota((size, 12), 0) // CB == iota((size, 12), 1)).astype(F32).astype(BF)
    same = (iota((size, size), 0) & 15) == (iota((size, size), 1) & 15)
    wide = dot_nt(dot(expand, masked).astype(BF), expand)
    coupling_ref[...] = jnp.where(same, wide, 0.0).astype(BF)
    wide = dot_nt(dot_nt(expand, masked).astype(BF), expand)
    turned_ref[...] = jnp.where(same, wide, 0.0).astype(BF)
    copies = bring([(turned_ref, turned_hbm)], sems)

    lane = iota((MODES, 2 * MP), 1)
    odd = (lane >= MP).astype(jnp.int32)
    split = (iota((MODES, 2 * MP), 0) == 2 * (lane - MP * odd) + odd).astype(F32).astype(BF)
    first_half = jnp.where(iota((1, 2 * MP), 1) == 0, 0.5, 1.0).astype(F32)
    for part, ref in enumerate((real_ref, imag_ref)):
        rows = [ref[k] for k in range(NK)]
        rest = jnp.concatenate([rows[k][i : i + 1] for i in range(NR) for k in range(NK)], axis=0)
        moved = None
        for step in range(3):
            piece = rest.astype(BF)
            rest = rest - piece.astype(F32)
            term = dot(piece, split)
            moved = term if moved is None else moved + term
        gain_ref[12 * part : 12 * part + 12, :] = moved * first_half
    copies[0].wait()


def spectral(value, parity, table_ref, gain_ref, filt_ref, sign):
    spec = dot(value, table_ref[parity])
    lanes = slice(MP * parity, MP * parity + MP)
    for g in range(12):
        rows = slice(CB * g, CB * g + CB)
        part_a, part_b = spec[rows, :MP], spec[rows, MP:]
        real = gain_ref[g : g + 1, lanes]
        imag = sign * gain_ref[12 + g : 13 + g, lanes]
        filt_ref[parity, rows, :MP] = (real * part_a - imag * part_b).astype(BF)
        filt_ref[parity, rows, MP:] = (real * part_b + imag * part_a).astype(BF)


def transform(lower, upper, table_ref, gain_ref, filt_ref, sign, copies):
    for parity, value in enumerate((lower + upper, lower - upper)):
        copies[parity].wait()
        spectral(value.astype(BF), parity, table_ref, gain_ref, filt_ref, sign)
    even = dot_nt(filt_ref[0], table_ref[0])
    odd = dot_nt(filt_ref[1], table_ref[1])
    scale = 2.0 / NLON
    return ((even + odd) * scale).astype(BF), ((even - odd) * scale).astype(BF)


def filter_kernel(
    first_ref,
    own_ref,
    second_ref,
    coupling_ref,
    gain_ref,
    table_hbm,
    send_ref,
    x_ref,
    filt_ref,
    table_ref,
    sems,
):
    copies = bring([(table_hbm.at[p], table_ref.at[p]) for p in range(2)], sems)
    for band, ref in enumerate((first_ref, own_ref, second_ref)):
        unpack(ref, x_ref, 64 * band, 32)
    coupling = coupling_ref[...]
    lower = dot(coupling, x_ref[:, :KP])
    upper = dot(coupling, x_ref[:, KP:])
    lower, upper = transform(lower, upper, table_ref, gain_ref, filt_ref, 1.0, copies)
    pack(send_ref, 0, lower, 96)
    pack(send_ref, 1, upper, 96)


def gelu_parts(hidden):
    inner_part = GELU_SCALE * (hidden + CUBIC_TERM * hidden * hidden * hidden)
    tangent = jnp.tanh(inner_part)
    gelu_value = 0.5 * hidden * (1.0 + tangent)
    gelu_slope = 0.5 * (1.0 + tangent) + 0.5 * hidden * (1.0 - tangent * tangent) * GELU_SCALE * (
        1.0 + 3.0 * CUBIC_TERM * hidden * hidden
    )
    return (gelu_value, gelu_slope)


def mlp_kernel(
    recv_ref,
    fields_ref,
    cot_ref,
    filter_ref,
    inner_ref,
    outer_ref,
    send_ref,
    state_grad_hbm,
    grads_hbm,
    state_grad_ref,
    grads_ref,
    sems,
):
    mix = jnp.concatenate(
        [filter_ref[k, CB * s : CB * s + CB, :] for s in range(NZ) for k in range(NK)], axis=0
    )
    inner = inner_ref[...]
    outer = outer_ref[...]
    sums = None
    for first in range(2):
        lanes = slice(384 * first, 384 * first + 384)
        filtered = jnp.concatenate(
            [recv_ref[s, 48 * first : 48 * first + 48, :] for s in range(NZ)], axis=0
        )
        cot = cot_ref[:, lanes]
        state = (fields_ref[:, lanes].astype(F32) + dot_tn(mix, filtered)).astype(BF)
        hidden = dot_tn(inner, state)
        value, slope = gelu_parts(hidden)
        active = value.astype(BF)
        d_hidden = (dot(outer, cot) * slope).astype(BF)
        d_state = cot.astype(F32) + dot(inner, d_hidden)
        state_grad_ref[:, lanes] = d_state
        d_state_b = d_state.astype(BF)
        d_filtered = dot(mix, d_state_b).astype(BF)
        for s in range(NZ):
            send_ref[s, 48 * first : 48 * first + 48, :] = d_filtered[48 * s : 48 * s + 48]
        parts = (dot_nt(filtered, d_state_b), dot_nt(active, cot), dot_nt(state, d_hidden))
        sums = parts if sums is None else tuple(a + b for a, b in zip(sums, parts))
    grads_ref[0:384, :] = sums[0].astype(BF)
    grads_ref[384:640, :] = sums[1].astype(BF)
    grads_ref[640:768, :] = sums[2][:, :128].astype(BF)
    grads_ref[768:896, :] = sums[2][:, 128:].astype(BF)
    grads_ref[896:WIDE, :] = jnp.zeros((WIDE - 896, 128), BF)
    for copy in bring(((grads_ref, grads_hbm), (state_grad_ref, state_grad_hbm)), sems):
        copy.wait()


def adjoint_kernel(
    recv_ref,
    coupling_hbm,
    gain_ref,
    table_hbm,
    first_ref,
    own_hbm,
    second_ref,
    coupling_ref,
    own_ref,
    x_ref,
    filt_ref,
    table_ref,
    sems,
):
    copies = bring(
        [(table_hbm.at[p], table_ref.at[p]) for p in range(2)] + [(coupling_hbm, coupling_ref)], sems
    )
    unpack(recv_ref, x_ref, 0, 96)
    lower = x_ref[:, :KP].astype(F32)
    upper = x_ref[:, KP:].astype(F32)
    halves = transform(lower, upper, table_ref, gain_ref, filt_ref, -1.0, copies)
    copies[2].wait()
    coupling = coupling_ref[...]
    for half, value in enumerate(halves):
        parts = dot(coupling, value)
        pack(first_ref, half, parts[0:64].astype(BF), 32)
        pack(own_ref, half, parts[64:128], 32)
        pack(second_ref, half, parts[128:192].astype(BF), 32)
    bring([(own_ref, own_hbm)], sems)[0].wait()


def halo_sum_kernel(own_hbm, first_ref, second_ref, chunks_ref, send_ref, own_ref, sems):
    copies = bring([(own_hbm, own_ref)], sems)
    chunk = chunks_ref[0].astype(F32)
    for n in range(1, chunks_ref.shape[0]):
        chunk = chunk + chunks_ref[n].astype(F32)
    chunk = chunk.astype(BF)
    size = chunk.shape[0]
    copies[0].wait()
    for z in range(NZ):
        total = own_ref[z] + first_ref[z].astype(F32) + second_ref[z].astype(F32)
        total = total.astype(BF)
        for tile in range(3):
            send_ref[z, 32 * tile : 32 * tile + 32, :] = total[:, 128 * tile : 128 * tile + 128]
        send_ref[z, 96 : 96 + size, :] = chunk


def chunk_sum_kernel(recv_ref, out_ref):
    size = recv_ref.shape[1] - 96
    total = recv_ref[0, 96:, :].astype(F32)
    for z in range(1, NZ):
        total = total + recv_ref[z, 96:, :].astype(F32)
    total = total.astype(BF)
    for n in range(WIDE // size):
        out_ref[size * n : size * n + size, :] = total


def field_kernel(recv_ref, state_grad_ref, grad_ref):
    totals = []
    for first in range(2):
        tiles = []
        for tile in range(3):
            base = 32 * tile + CB * first
            tiles.append(
                jnp.concatenate([recv_ref[s, base : base + CB, :] for s in range(NZ)], axis=0)
            )
        lat_part = jnp.concatenate(tiles, axis=1).astype(F32)
        total = state_grad_ref[:, 384 * first : 384 * first + 384] + lat_part
        totals.append(total.astype(BF))
    grad_ref[...] = dot_nt(point_select(), jnp.concatenate(totals, axis=1)).astype(BF)


def weights_kernel(scale, grads_ref, filter_ref, inner_ref, outer_ref):
    for s in range(NZ):
        for k in range(NK):
            base = 48 * s + CB * k
            filter_ref[k, CB * s : CB * s + CB, :] = grads_ref[base : base + CB, :].astype(F32) * scale
    outer_ref[...] = grads_ref[384:640, :].astype(F32) * scale
    inner_ref[:, :128] = grads_ref[640:768, :].astype(F32) * scale
    inner_ref[:, 128:] = grads_ref[768:896, :].astype(F32) * scale


def call(kernel, outs, flops, scratch=(), in_specs=None, out_specs=None):
    shapes = outs if isinstance(outs, tuple) else (outs,)
    moved = sum(math.prod(o.shape) * o.dtype.itemsize for o in shapes)
    if out_specs is None:
        out_specs = jax.tree.map(lambda _: pl.BlockSpec(memory_space=pltpu.VMEM), outs)
    return pl.pallas_call(
        kernel,
        out_shape=outs,
        in_specs=in_specs,
        out_specs=out_specs,
        scratch_shapes=scratch,
        compiler_params=pltpu.CompilerParams(vmem_limit_bytes=LIMIT),
        cost_estimate=pl.CostEstimate(flops=flops, bytes_accessed=2 * moved, transcendentals=0),
    )


def shaped(shape, dtype=BF):
    return jax.ShapeDtypeStruct(shape, dtype)


def in_hbm(shape, dtype=BF):
    return pltpu.HBM(shape, dtype)


def hold(value):
    return pltpu.with_memory_space_constraint(value, pltpu.HBM)


def vmem(count):
    return [pl.BlockSpec(memory_space=pltpu.VMEM)] * count


def hbm(count):
    return [pl.BlockSpec(memory_space=pltpu.HBM)] * count


def swapped(value, first):
    count = lax.axis_size("lat")
    pairs = []
    for low in range(first, count - 1, 2):
        pairs += [(low, low + 1), (low + 1, low)]
    return lax.ppermute(value, "lat", pairs)


def local(
    fields,
    cotangent,
    basis_weights,
    band_support,
    spectrum_real,
    spectrum_imag,
    filter_weights,
    inner_weights,
    outer_weights,
):
    group = lax.axis_size("lat")
    grad_scale = 1.0 / math.sqrt(lax.axis_size("ens") * group * NR * NLON)
    table = hold(jnp.asarray(dft_table()))

    field_points = fields[0].transpose(1, 0, 2).reshape(LON * NR, 128)
    cot_points = cotangent[0].transpose(1, 0, 2).reshape(LON * NR, 128)
    field_wide, send_fields = call(
        pack_kernel, (shaped((128, 768)), shaped((NZ, 32, 384))), 2 * 720 * 768 * 128,
        [pltpu.VMEM((720, 128), BF), pltpu.SemaphoreType.DMA((1,))], hbm(1)
    )(hold(field_points))
    own = lax.all_to_all(send_fields, "lon", 0, 0, tiled=True)

    cot_wide, coupling, turned, gains = call(
        prepare_kernel,
        (
            shaped((128, 768)),
            shaped((192, 192)),
            in_hbm((192, 192)),
            shaped((24, 2 * MP), F32),
        ),
        2 * 720 * 768 * 128,
        [
            pltpu.VMEM((192, 192), BF),
            pltpu.VMEM((720, 128), BF),
            pltpu.VMEM((NK, NR, 12), BF),
            pltpu.VMEM((NK, NR, MODES), F32),
            pltpu.VMEM((NK, NR, MODES), F32),
            pltpu.VMEM((1, 3), jnp.int32),
            pltpu.SemaphoreType.DMA((5,)),
        ],
        hbm(5),
        tuple(vmem(2) + hbm(1) + vmem(1)),
    )(
        hold(cot_points),
        hold(basis_weights),
        hold(spectrum_real),
        hold(spectrum_imag),
        hold(band_support),
    )

    first = swapped(own, 0)
    second = swapped(own, 1)
    work = [
        pltpu.VMEM((192, 2 * KP), BF),
        pltpu.VMEM((2, 192, 2 * MP), BF),
        pltpu.VMEM((2, KP, 2 * MP), BF),
        pltpu.SemaphoreType.DMA((3,)),
    ]
    send_filtered = call(
        filter_kernel, shaped((NZ, 96, 384)), 8 * 192 * KP * KP, work, vmem(5) + hbm(1)
    )(first, own, second, coupling, gains, table)
    filtered = lax.all_to_all(send_filtered, "lon", 0, 0, tiled=True)

    send_back, state_grad, grads = call(
        mlp_kernel,
        (shaped((NZ, 96, 384)), in_hbm((128, 768), F32), in_hbm((WIDE, 128))),
        2 * 768 * 128 * 256 * 10,
        [
            pltpu.VMEM((128, 768), F32),
            pltpu.VMEM((WIDE, 128), BF),
            pltpu.SemaphoreType.DMA((2,)),
        ],
        vmem(6),
        tuple(vmem(1) + hbm(2)),
    )(filtered, field_wide, cot_wide, filter_weights, inner_weights, outer_weights)
    back = lax.all_to_all(send_back, "lon", 0, 0, tiled=True)
    grads_other = lax.ppermute(grads, "ens", [(0, 1), (1, 0)])
    grads = (grads.astype(F32) + grads_other.astype(F32)).astype(BF)
    share = WIDE // group
    chunks = lax.all_to_all(grads.reshape(group, share, 128), "lat", 0, 0, tiled=True)

    pieces = (NZ, 32, 384)
    to_first, kept, to_second = call(
        adjoint_kernel,
        (shaped(pieces), in_hbm(pieces, F32), shaped(pieces)),
        8 * 192 * KP * KP,
        [pltpu.VMEM((192, 192), BF), pltpu.VMEM(pieces, F32)] + work,
        vmem(1) + hbm(1) + vmem(1) + hbm(1),
        tuple(vmem(1) + hbm(1) + vmem(1)),
    )(back, hold(turned), gains, table)
    from_first = swapped(to_first, 0)
    from_second = swapped(to_second, 1)
    send_lat = call(
        halo_sum_kernel,
        shaped((NZ, 96 + share, 128)),
        300000,
        [pltpu.VMEM(pieces, F32), pltpu.SemaphoreType.DMA((1,))],
        hbm(1) + vmem(3),
    )(hold(kept), from_first, from_second, chunks)
    lat_parts = lax.all_to_all(send_lat, "lon", 0, 0, tiled=True)

    spread = call(chunk_sum_kernel, shaped((WIDE, 128)), 40000, (), vmem(1))(lat_parts)
    gathered = lax.all_to_all(spread.reshape(group, share, 128), "lat", 0, 0, tiled=True)
    grad_points = call(field_kernel, shaped((LON * NR, 128)), 2 * 720 * 768 * 128, (), vmem(2))(
        lat_parts, hold(state_grad)
    )

    def weights(*refs):
        weights_kernel(grad_scale, *refs)

    filter_grad, inner_grad, outer_grad = call(
        weights,
        (shaped((NK, 128, 128), F32), shaped((128, 256), F32), shaped((256, 128), F32)),
        WIDE * 128,
        (),
        vmem(1),
    )(gathered.reshape(WIDE, 128))
    field_grad = grad_points.reshape(LON, NR, 128).transpose(1, 0, 2)[None]
    return (field_grad, filter_grad, inner_grad, outer_grad)


def solution(mesh):
    placed = (
        P("ens", "lat", "lon", None),
        P("ens", "lat", "lon", None),
        P(None, "lat", None),
        P("lat", None),
        P(None, "lat", None),
        P(None, "lat", None),
        P(),
        P(),
        P(),
    )
    return jax.shard_map(
        local,
        mesh=mesh,
        in_specs=placed,
        out_specs=(P("ens", "lat", "lon", None), P(), P(), P()),
        check_vma=False,
    )
```

time: 164 us -> 143 us (0.87)
  waiting for transfers between devices: 50.9 us -> 26.3 us
  blocking collectives: 37.4 us -> 55.3 us
  starting transfers between devices: 45.9 us -> 37.8 us
  local copies, waits for them, and re-layouts: 6.99 us -> 0.02 us
    all_to_all x1 -> x2, blocking collectives: 19.2 us -> 40.6 us  [the longest x1 21.1 us: local(): filtered = lax.all_to_all(send_filtered, 'lon', 0, 0, tiled=True)]
    all_to_all x1, waiting for transfers between devices: 24 us -> 7.3 us  [local(): back = lax.all_to_all(send_back, 'lon', 0, 0, tiled=True)]
    all_to_all x3 -> x2, starting transfers between devices: 29.1 us -> 16.4 us  [the longest x1 8.83 us: local(): lax.all_to_all(spread.reshape(group, share, 128), 'lat', 0, 0, tiled=True)]
    all_to_all x3 -> x2, waiting for transfers between devices: 22.7 us -> 12 us  [the longest x1 9.79 us: local(): lax.all_to_all(spread.reshape(group, share, 128), 'lat', 0, 0, tiled=True)]
    unnamed x22 -> x6, local copies, waits for them, and re-layouts: 6.63 us -> 0.02 us
    ppermute x4 -> x5, starting transfers between devices: 13.2 us -> 17.8 us  [the longest x4 13.2 us: swapped(): return lax.ppermute(value, 'lat', pairs)]
    all_to_all x1, blocking collectives: 18.3 us -> 14.8 us  [local(): lat_parts = lax.all_to_all(send_lat, 'lon', 0, 0, tiled=True)]
    ppermute x4 -> x5, waiting for transfers between devices: 4.17 us -> 6.94 us  [the longest x1 5.64 us: local(): grads_other = lax.ppermute(grads, 'ens', [(0, 1), (1, 0)])]
  transfers between devices with their start and end apart: 8 -> 8, of which waited for: 4 -> 5; matrix products, arithmetic and copies ran while one was open for 2% -> 1% of each run, Pallas kernels for 5% -> 6%
where the time goes in v2:
time: 143 us; the launch traced here: 142 us
  blocking collectives  55.3 us (39%)
  starting transfers between devices  37.8 us (26%)
  waiting for transfers between devices  26.3 us (18%)
  Pallas kernels  19.9 us (14%)
  other arithmetic  1.73 us (1%)
    all_to_all x1, blocking collectives, local(): filtered = lax.all_to_all(send_filtered, 'lon', 0, 0, tiled=True)  21.1 us
    all_to_all x1, blocking collectives, local(): own = lax.all_to_all(send_fields, 'lon', 0, 0, tiled=True)  19.5 us
    all_to_all x1, blocking collectives, local(): lat_parts = lax.all_to_all(send_lat, 'lon', 0, 0, tiled=True)  14.8 us
    ppermute x4, starting transfers between devices, swapped(): return lax.ppermute(value, 'lat', pairs)  13.2 us
    all_to_all x1, waiting for transfers between devices, local(): lax.all_to_all(spread.reshape(group, share, 128), 'lat', 0, 0, tiled=True)  9.79 us
    all_to_all x1, starting transfers between devices, local(): lax.all_to_all(spread.reshape(group, share, 128), 'lat', 0, 0, tiled=True)  8.83 us
    all_to_all x1, starting transfers between devices, local(): lax.all_to_all(grads.reshape(group, share, 128), 'lat', 0, 0, tiled=True)  7.6 us
    all_to_all x1, waiting for transfers between devices, local(): back = lax.all_to_all(send_back, 'lon', 0, 0, tiled=True)  7.3 us
  transfers between devices with their start and end apart: 8, of which 5 were waited for; matrix products, arithmetic and copies ran while one was open for 1% of the time, Pallas kernels for 6%

profile of v2, /device:TPU:1, one launch (start us, length us, event | category | flops | bytes accessed | tf_op | source)
XLA Modules:
  0.0 141.8 jit_solution(15127845189994499646)
XLA Ops:
  0.6 1.3 shard_map.129
  1.9 19.5 %all_to_all.30.own_ref = bf16[8,32,384]{2,1,0:T(8,128)(2,1)S(1)} all-to-all(bf16[8,32,384]{2,1,0:T(8,128)(2,1)S(1)} %get-tuple-element.19), channel_id=1, replica_groups=mesh['ens'=2,'lat'=32,'lon'=8] {'lon'}, dimensions={0} | all-to-all | bytes 393216 | tf_op jit(solution)/shard_map/all_to_all | solution.py:457
  21.4 5.7 %collective-permute-start.1 = (bf16[8,32,384]{2,1,0:T(8,128)(2,1)S(1)}, bf16[8,32,384]{2,1,0:T(8,128)(2,1)S(1)}, u32[]{:S(2)}, u32[]{:S(2)}) collective-permute-start(bf16[8,32,384]{2,1,0:T(8,128)(2,1)S(1)} %all_to_all.30.own_ref), channel_id=1, source_target_pairs={{8,16},{16,8},{24,32},{32,24},{40,48},{48,40},{56,64},{64,56},{72,... | collective-permute-start | bytes 589832 | tf_op jit(solution)/shard_map/ppermute | solution.py:433
  27.1 1.9 %collective-permute-start = (bf16[8,32,384]{2,1,0:T(8,128)(2,1)S(1)}, bf16[8,32,384]{2,1,0:T(8,128)(2,1)S(1)}, u32[]{:S(2)}, u32[]{:S(2)}) collective-permute-start(bf16[8,32,384]{2,1,0:T(8,128)(2,1)S(1)} %all_to_all.30.own_ref), channel_id=1, source_target_pairs={{0,8},{8,0},{16,24},{24,16},{32,40},{40,32},{48,56},{56,48},{64,72... | collective-permute-start | bytes 589832 | tf_op jit(solution)/shard_map/ppermute | solution.py:433
  29.0 2.9 %shard_map.130 = (bf16[128,768]{1,0:T(8,128)(2,1)S(1)}, bf16[192,192]{1,0:T(8,128)(2,1)S(1)}, bf16[192,192]{1,0:T(8,128)(2,1)}, f32[24,768]{1,0:T(8,128)S(1)}) custom-call(bf16[720,128]{1,0:T(8,128)(2,1)} %bitcast.21, bf16[3,4,12]{2,1,0:T(4,128)(2,1)} %weights_hbm.1, f32[3,4,720]{2,1,0:T(4,128)} %real_hbm.1, f32[3,4,720]{2,1,0:T(4,128)} %imag_hbm.1, ...), custom_call_target="tpu_custom_call" | custom-call | flops 141557760 | bytes 835584 | tf_op jit(solution)/shard_map/pallas_call | solution.py:459
  31.9 0.0 collective-permute-done.1.second_ref
  31.9 0.0 collective-permute-done.first_ref
  31.9 0.0 copy-start
  31.9 0.0 copy-start.1
  31.9 0.0 copy-start.2
  32.0 3.2 %shard_map.131 = bf16[8,96,384]{2,1,0:T(8,128)(2,1)S(1)} custom-call(bf16[8,32,384]{2,1,0:T(8,128)(2,1)S(1)} %collective-permute-done.first_ref, bf16[8,32,384]{2,1,0:T(8,128)(2,1)S(1)} %all_to_all.30.own_ref, bf16[8,32,384]{2,1,0:T(8,128)(2,1)S(1)} %collective-permute-done.1.second_ref, bf16[192,192]{1,0:T(8,128)(2,1)S(1)} %get-tuple-element.20.coupling_ref, ...), custom_call_target="tpu_custom_call" | custom-call | flops 905969664 | bytes 1179648 | tf_op jit(solution)/shard_map/pallas_call | solution.py:495
  35.1 21.1 %all_to_all.31.recv_ref = bf16[8,96,384]{2,1,0:T(8,128)(2,1)S(1)} all-to-all(bf16[8,96,384]{2,1,0:T(8,128)(2,1)S(1)} %shard_map.131), channel_id=1, replica_groups=mesh['ens'=2,'lat'=32,'lon'=8] {'lon'}, dimensions={0} | all-to-all | bytes 1179648 | tf_op jit(solution)/shard_map/all_to_all | solution.py:498
  56.2 0.0 copy-done
  56.2 0.0 copy-done.1
  56.2 0.0 copy-done.2
  56.2 3.8 %shard_map.132 = (bf16[8,96,384]{2,1,0:T(8,128)(2,1)}, f32[128,768]{1,0:T(8,128)}, bf16[1024,128]{1,0:T(8,128)(2,1)}) custom-call(bf16[8,96,384]{2,1,0:T(8,128)(2,1)S(1)} %all_to_all.31.recv_ref, bf16[128,768]{1,0:T(8,128)(2,1)S(1)} %get-tuple-element.22.fields_ref, bf16[128,768]{1,0:T(8,128)(2,1)S(1)} %get-tuple-element.23.cot_ref, ...), custom_call_target="tpu_custom_call" | custom-call | flops 503316480 | bytes 2490368 | tf_op jit(solution)/shard_map/pallas_call | solution.py:500
  60.0 3.5 %all-to-all-start.2 = ((bf16[8,96,384]{2,1,0:T(8,128)(2,1)}), bf16[8,96,384]{2,1,0:T(8,128)(2,1)S(1)}, u32[]{:S(2)}, u32[]{:S(2)}) async-start(bf16[8,96,384]{2,1,0:T(8,128)(2,1)} %get-tuple-element.24), calls=%async_computation.2 | async-start | bytes 1179648 | tf_op jit(solution)/shard_map/all_to_all | solution.py:512
  63.6 4.6 %collective-permute-start.4 = (bf16[1024,128]{1,0:T(8,128)(2,1)}, bf16[1024,128]{1,0:T(8,128)(2,1)S(1)}, u32[]{:S(2)}, u32[]{:S(2)}) collective-permute-start(bf16[1024,128]{1,0:T(8,128)(2,1)} %get-tuple-element.29), channel_id=1, source_target_pairs={{0,256},{256,0},{1,257},{257,1},{2,258},{258,2},{3,259},{259,3},{4... | collective-permute-start | bytes 786440 | tf_op jit(solution)/shard_map/ppermute | solution.py:513
  68.2 5.6 %collective-permute-done.4 = bf16[1024,128]{1,0:T(8,128)(2,1)S(1)} collective-permute-done((bf16[1024,128]{1,0:T(8,128)(2,1)}, bf16[1024,128]{1,0:T(8,128)(2,1)S(1)}, u32[]{:S(2)}, u32[]{:S(2)}) %collective-permute-start.4) | collective-permute-done | bytes 262176 | tf_op jit(solution)/shard_map/ppermute | solution.py:513
  73.8 1.7 %add_convert_fusion = bf16[1024,128]{1,0:T(8,128)(2,1)} fusion(bf16[1024,128]{1,0:T(8,128)(2,1)S(1)} %collective-permute-done.4, bf16[1024,128]{1,0:T(8,128)(2,1)} %get-tuple-element.29), kind=kLoop, calls=%fused_computation | loop fusion | flops 524288 | bytes 786432 | tf_op jit(solution)/shard_map/convert_element_type | solution.py:514
  75.6 7.3 %all-to-all-done.2.recv_ref = bf16[8,96,384]{2,1,0:T(8,128)(2,1)S(1)} async-done(((bf16[8,96,384]{2,1,0:T(8,128)(2,1)}), bf16[8,96,384]{2,1,0:T(8,128)(2,1)S(1)}, u32[]{:S(2)}, u32[]{:S(2)}) %all-to-all-start.2) | async-done | bytes 589856 | tf_op jit(solution)/shard_map/all_to_all | solution.py:512
  82.9 7.6 %all-to-all-start.3 = ((bf16[32,32,128]{2,1,0:T(8,128)(2,1)}), bf16[32,32,128]{2,1,0:T(8,128)(2,1)S(1)}, u32[]{:S(2)}, u32[]{:S(2)}) async-start(bf16[32,32,128]{2,1,0:T(8,128)(2,1)} %bitcast.6), calls=%async_computation.3 | async-start | bytes 524288 | tf_op jit(solution)/shard_map/all_to_all | solution.py:516
  90.5 4.1 %shard_map.133 = (bf16[8,32,384]{2,1,0:T(8,128)(2,1)S(1)}, f32[8,32,384]{2,1,0:T(8,128)}, bf16[8,32,384]{2,1,0:T(8,128)(2,1)S(1)}) custom-call(bf16[8,96,384]{2,1,0:T(8,128)(2,1)S(1)} %all-to-all-done.2.recv_ref, bf16[192,192]{1,0:T(8,128)(2,1)} %get-tuple-element.25.coupling_hbm, f32[24,768]{1,0:T(8,128)S(1)} %get-tuple-element.21.gain_ref, ...), custom_call_target="tpu_custom_call" | custom-call | flops 905969664 | bytes 1572864 | tf_op jit(solution)/shard_map/pallas_call | solution.py:519
  94.6 2.1 %collective-permute-start.2 = (bf16[8,32,384]{2,1,0:T(8,128)(2,1)S(1)}, bf16[8,32,384]{2,1,0:T(8,128)(2,1)S(1)}, u32[]{:S(2)}, u32[]{:S(2)}) collective-permute-start(bf16[8,32,384]{2,1,0:T(8,128)(2,1)S(1)} %get-tuple-element.27), channel_id=1, source_target_pairs={{0,8},{8,0},{16,24},{24,16},{32,40},{40,32},{48,56},{56,48},{64,72... | collective-permute-start | bytes 589832 | tf_op jit(solution)/shard_map/ppermute | solution.py:433
  96.7 3.4 %collective-permute-start.3 = (bf16[8,32,384]{2,1,0:T(8,128)(2,1)S(1)}, bf16[8,32,384]{2,1,0:T(8,128)(2,1)S(1)}, u32[]{:S(2)}, u32[]{:S(2)}) collective-permute-start(bf16[8,32,384]{2,1,0:T(8,128)(2,1)S(1)} %get-tuple-element.28), channel_id=1, source_target_pairs={{8,16},{16,8},{24,32},{32,24},{40,48},{48,40},{56,64},{64,56},{72,... | collective-permute-start | bytes 589832 | tf_op jit(solution)/shard_map/ppermute | solution.py:433
  100.2 2.2 %all-to-all-done.3.chunks_ref = bf16[32,32,128]{2,1,0:T(8,128)(2,1)S(1)} async-done(((bf16[32,32,128]{2,1,0:T(8,128)(2,1)}), bf16[32,32,128]{2,1,0:T(8,128)(2,1)S(1)}, u32[]{:S(2)}, u32[]{:S(2)}) %all-to-all-start.3) | async-done | bytes 262176 | tf_op jit(solution)/shard_map/all_to_all | solution.py:516
  102.4 0.0 collective-permute-done.2.first_ref
  102.4 1.3 collective-permute-done.3.second_ref
  103.7 1.1 shard_map.134
  104.8 14.8 %all_to_all.32.recv_ref = bf16[8,128,128]{2,1,0:T(8,128)(2,1)S(1)} all-to-all(bf16[8,128,128]{2,1,0:T(8,128)(2,1)S(1)} %shard_map.134), channel_id=1, replica_groups=mesh['ens'=2,'lat'=32,'lon'=8] {'lon'}, dimensions={0} | all-to-all | bytes 524288 | tf_op jit(solution)/shard_map/all_to_all | solution.py:536
  119.5 0.7 shard_map.136
  120.3 8.8 %all-to-all-start.5 = ((bf16[32,32,128]{2,1,0:T(8,128)(2,1)}), bf16[32,32,128]{2,1,0:T(8,128)(2,1)S(1)}, u32[]{:S(2)}, u32[]{:S(2)}) async-start(bf16[32,32,128]{2,1,0:T(8,128)(2,1)} %bitcast.10), calls=%async_computation.5 | async-start | bytes 524288 | tf_op jit(solution)/shard_map/all_to_all | solution.py:539
  129.1 2.1 %shard_map.135 = bf16[720,128]{1,0:T(8,128)(2,1)} custom-call(bf16[8,128,128]{2,1,0:T(8,128)(2,1)S(1)} %all_to_all.32.recv_ref, f32[128,768]{1,0:T(8,128)} %get-tuple-element.30.state_grad_ref), custom_call_target="tpu_custom_call" | custom-call | flops 141557760 | bytes 368640 | tf_op jit(solution)/shard_map/pallas_call | solution.py:540
  131.2 9.8 %all-to-all-done.5 = bf16[32,32,128]{2,1,0:T(8,128)(2,1)S(1)} async-done(((bf16[32,32,128]{2,1,0:T(8,128)(2,1)}), bf16[32,32,128]{2,1,0:T(8,128)(2,1)S(1)}, u32[]{:S(2)}, u32[]{:S(2)}) %all-to-all-start.5) | async-done | bytes 262176 | tf_op jit(solution)/shard_map/all_to_all | solution.py:539
  141.0 0.8 shard_map.137
Async XLA Ops:
  21.4 10.5 %collective-permute-start.1 = (bf16[8,32,384]{2,1,0:T(8,128)(2,1)S(1)}, bf16[8,32,384]{2,1,0:T(8,128)(2,1)S(1)}, u32[]{:S(2)}, u32[]{:S(2)}) collective-permute-start(bf16[8,32,384]{2,1,0:T(8,128)(2,1)S(1)} %all_to_all.30.own_ref), channel_id=1, source_target_pairs={{8,16},{16,8},{24,32},{32,24},{40,48},{48,40},{56,64},{64,56},{72,... | collective-permute-start | bytes 589832 | tf_op jit(solution)/shard_map/ppermute | solution.py:433
  27.1 4.8 %collective-permute-start = (bf16[8,32,384]{2,1,0:T(8,128)(2,1)S(1)}, bf16[8,32,384]{2,1,0:T(8,128)(2,1)S(1)}, u32[]{:S(2)}, u32[]{:S(2)}) collective-permute-start(bf16[8,32,384]{2,1,0:T(8,128)(2,1)S(1)} %all_to_all.30.own_ref), channel_id=1, source_target_pairs={{0,8},{8,0},{16,24},{24,16},{32,40},{40,32},{48,56},{56,48},{64,72... | collective-permute-start | bytes 589832 | tf_op jit(solution)/shard_map/ppermute | solution.py:433
  31.9 24.3 %copy-start = (bf16[3,128,128]{2,1,0:T(8,128)(2,1)S(1)}, bf16[3,128,128]{2,1,0:T(8,128)(2,1)}, u32[]{:S(2)}) copy-start(bf16[3,128,128]{2,1,0:T(8,128)(2,1)} %filter_ref.1) | copy-start | bytes 294916
  31.9 24.3 %copy-start.1 = (bf16[128,256]{1,0:T(8,128)(2,1)S(1)}, bf16[128,256]{1,0:T(8,128)(2,1)}, u32[]{:S(2)}) copy-start(bf16[128,256]{1,0:T(8,128)(2,1)} %inner_ref.1) | copy-start | bytes 196612
  31.9 24.3 %copy-start.2 = (bf16[256,128]{1,0:T(8,128)(2,1)S(1)}, bf16[256,128]{1,0:T(8,128)(2,1)}, u32[]{:S(2)}) copy-start(bf16[256,128]{1,0:T(8,128)(2,1)} %outer_ref.1) | copy-start | bytes 196612
  60.0 22.8 %all-to-all-start.2 = ((bf16[8,96,384]{2,1,0:T(8,128)(2,1)}), bf16[8,96,384]{2,1,0:T(8,128)(2,1)S(1)}, u32[]{:S(2)}, u32[]{:S(2)}) async-start(bf16[8,96,384]{2,1,0:T(8,128)(2,1)} %get-tuple-element.24), calls=%async_computation.2 | async-start | bytes 1179648 | tf_op jit(solution)/shard_map/all_to_all | solution.py:512
  63.6 10.2 %collective-permute-start.4 = (bf16[1024,128]{1,0:T(8,128)(2,1)}, bf16[1024,128]{1,0:T(8,128)(2,1)S(1)}, u32[]{:S(2)}, u32[]{:S(2)}) collective-permute-start(bf16[1024,128]{1,0:T(8,128)(2,1)} %get-tuple-element.29), channel_id=1, source_target_pairs={{0,256},{256,0},{1,257},{257,1},{2,258},{258,2},{3,259},{259,3},{4... | collective-permute-start | bytes 786440 | tf_op jit(solution)/shard_map/ppermute | solution.py:513
  82.9 19.5 %all-to-all-start.3 = ((bf16[32,32,128]{2,1,0:T(8,128)(2,1)}), bf16[32,32,128]{2,1,0:T(8,128)(2,1)S(1)}, u32[]{:S(2)}, u32[]{:S(2)}) async-start(bf16[32,32,128]{2,1,0:T(8,128)(2,1)} %bitcast.6), calls=%async_computation.3 | async-start | bytes 524288 | tf_op jit(solution)/shard_map/all_to_all | solution.py:516
  94.6 7.8 %collective-permute-start.2 = (bf16[8,32,384]{2,1,0:T(8,128)(2,1)S(1)}, bf16[8,32,384]{2,1,0:T(8,128)(2,1)S(1)}, u32[]{:S(2)}, u32[]{:S(2)}) collective-permute-start(bf16[8,32,384]{2,1,0:T(8,128)(2,1)S(1)} %get-tuple-element.27), channel_id=1, source_target_pairs={{0,8},{8,0},{16,24},{24,16},{32,40},{40,32},{48,56},{56,48},{64,72... | collective-permute-start | bytes 589832 | tf_op jit(solution)/shard_map/ppermute | solution.py:433
  96.7 7.0 %collective-permute-start.3 = (bf16[8,32,384]{2,1,0:T(8,128)(2,1)S(1)}, bf16[8,32,384]{2,1,0:T(8,128)(2,1)S(1)}, u32[]{:S(2)}, u32[]{:S(2)}) collective-permute-start(bf16[8,32,384]{2,1,0:T(8,128)(2,1)S(1)} %get-tuple-element.28), channel_id=1, source_target_pairs={{8,16},{16,8},{24,32},{32,24},{40,48},{48,40},{56,64},{64,56},{72,... | collective-permute-start | bytes 589832 | tf_op jit(solution)/shard_map/ppermute | solution.py:433
  120.3 20.8 %all-to-all-start.5 = ((bf16[32,32,128]{2,1,0:T(8,128)(2,1)}), bf16[32,32,128]{2,1,0:T(8,128)(2,1)S(1)}, u32[]{:S(2)}, u32[]{:S(2)}) async-start(bf16[32,32,128]{2,1,0:T(8,128)(2,1)} %bitcast.10), calls=%async_computation.5 | async-start | bytes 524288 | tf_op jit(solution)/shard_map/all_to_all | solution.py:539

commit v3 on v2

--- a/solution.py
+++ b/solution.py
@@ -1,3 +1,4 @@
+import functools
 import math
 
 import jax
@@ -141,9 +142,9 @@
     support_hbm,
     wide_ref,
     coupling_ref,
-    turned_hbm,
+    masked_hbm,
     gain_ref,
-    turned_ref,
+    masked_ref,
     points_ref,
     weights_ref,
     real_ref,
@@ -175,15 +176,15 @@
     rows = [weights_ref[k].astype(F32) for k in range(NK)]
     masked = jnp.concatenate([rows[k][i : i + 1] * seen for i in range(NR) for k in range(NK)], axis=0)
     turned = jnp.concatenate([masked[:, 8:12], masked[:, 4:8], masked[:, 0:4]], axis=1)
-    masked = jnp.where(flip, turned, masked).astype(BF)
+    masked = jnp.where(flip, turned, masked)
+    masked_ref[...] = masked
+    copies = bring([(masked_ref, masked_hbm)], sems)
+    masked = masked.astype(BF)
     size = 12 * CB
     expand = (iota((size, 12), 0) // CB == iota((size, 12), 1)).astype(F32).astype(BF)
     same = (iota((size, size), 0) & 15) == (iota((size, size), 1) & 15)
     wide = dot_nt(dot(expand, masked).astype(BF), expand)
     coupling_ref[...] = jnp.where(same, wide, 0.0).astype(BF)
-    wide = dot_nt(dot_nt(expand, masked).astype(BF), expand)
-    turned_ref[...] = jnp.where(same, wide, 0.0).astype(BF)
-    copies = bring([(turned_ref, turned_hbm)], sems)
 
     lane = iota((MODES, 2 * MP), 1)
     odd = (lane >= MP).astype(jnp.int32)
@@ -265,11 +266,12 @@
     filter_ref,
     inner_ref,
     outer_ref,
-    send_ref,
+    back_hbm,
+    grads_hbm,
     state_grad_hbm,
-    grads_hbm,
+    back_ref,
+    grads_ref,
     state_grad_ref,
-    grads_ref,
     sems,
 ):
     mix = jnp.concatenate(
@@ -277,7 +279,7 @@
     )
     inner = inner_ref[...]
     outer = outer_ref[...]
-    sums = None
+    held = []
     for first in range(2):
         lanes = slice(384 * first, 384 * first + 384)
         filtered = jnp.concatenate(
@@ -292,9 +294,11 @@
         d_state = cot.astype(F32) + dot(inner, d_hidden)
         state_grad_ref[:, lanes] = d_state
         d_state_b = d_state.astype(BF)
-        d_filtered = dot(mix, d_state_b).astype(BF)
-        for s in range(NZ):
-            send_ref[s, 48 * first : 48 * first + 48, :] = d_filtered[48 * s : 48 * s + 48]
+        back_ref[128 * first : 128 * first + 128, :] = d_state_b
+        held.append((filtered, d_state_b, active, cot, state, d_hidden))
+    copies = bring(((back_ref, back_hbm), (state_grad_ref, state_grad_hbm)), sems)
+    sums = None
+    for filtered, d_state_b, active, cot, state, d_hidden in held:
         parts = (dot_nt(filtered, d_state_b), dot_nt(active, cot), dot_nt(state, d_hidden))
         sums = parts if sums is None else tuple(a + b for a, b in zip(sums, parts))
     grads_ref[0:384, :] = sums[0].astype(BF)
@@ -302,81 +306,106 @@
     grads_ref[640:768, :] = sums[2][:, :128].astype(BF)
     grads_ref[768:896, :] = sums[2][:, 128:].astype(BF)
     grads_ref[896:WIDE, :] = jnp.zeros((WIDE - 896, 128), BF)
-    for copy in bring(((grads_ref, grads_hbm), (state_grad_ref, state_grad_hbm)), sems):
+    last = pltpu.make_async_copy(grads_ref, grads_hbm, sems.at[2])
+    last.start()
+    for copy in copies + [last]:
         copy.wait()
 
 
 def adjoint_kernel(
-    recv_ref,
-    coupling_hbm,
+    recv_hbm,
+    weights_ref,
     gain_ref,
-    table_hbm,
+    table_ref,
+    filter_ref,
     first_ref,
     own_hbm,
     second_ref,
-    coupling_ref,
+    x_ref,
+    middle_ref,
+    spec_ref,
+    filt_ref,
+    total_ref,
     own_ref,
-    x_ref,
-    filt_ref,
-    table_ref,
     sems,
 ):
-    copies = bring(
-        [(table_hbm.at[p], table_ref.at[p]) for p in range(2)] + [(coupling_hbm, coupling_ref)], sems
-    )
-    unpack(recv_ref, x_ref, 0, 96)
-    lower = x_ref[:, :KP].astype(F32)
-    upper = x_ref[:, KP:].astype(F32)
-    halves = transform(lower, upper, table_ref, gain_ref, filt_ref, -1.0, copies)
-    copies[2].wait()
-    coupling = coupling_ref[...]
-    for half, value in enumerate(halves):
-        parts = dot(coupling, value)
-        pack(first_ref, half, parts[0:64].astype(BF), 32)
-        pack(own_ref, half, parts[64:128], 32)
-        pack(second_ref, half, parts[128:192].astype(BF), 32)
+    pairs = []
+    for n in range(NZ):
+        lanes = pl.ds(128 * tile_of(n), 128)
+        pairs.append((recv_hbm.at[n, :, pl.ds(0, 128)], x_ref.at[pl.ds(0, 256), lanes]))
+        pairs.append((recv_hbm.at[n, :, pl.ds(256, 128)], x_ref.at[pl.ds(256, 256), lanes]))
+        pairs.append((recv_hbm.at[n, :, pl.ds(128, 128)], middle_ref.at[n]))
+    copies = bring(pairs, sems)
+    z = lax.axis_index("lon")
+    quarter = lax.rem(z, 4)
+    sign = jnp.where(z < 4, 1.0, -1.0)
+    main = pl.ds(pl.multiple_of(128 * quarter, 128), 128)
+    tail = pl.ds(pl.multiple_of(512 + 64 * quarter, 64), 64)
+    places = [
+        jnp.concatenate([table_ref[p, main, :], table_ref[p, tail, :]], axis=0) for p in range(2)
+    ]
+    for copy in copies:
+        copy.wait()
+    for pair in range(NZ // 2):
+        lanes = slice(128 * tile_of_pair(pair), 128 * tile_of_pair(pair) + 128)
+        even, odd = middle_ref[2 * pair], middle_ref[2 * pair + 1]
+        x_ref[0:256, lanes] = low_halves(even, odd)
+        x_ref[256:512, lanes] = high_halves(even, odd)
+    for i in range(NR):
+        rows = slice(128 * i, 128 * i + 128)
+        lower = x_ref[rows, :KP].astype(F32)
+        upper = x_ref[rows, KP:].astype(F32)
+        spec_ref[0, rows, :] = dot((lower + upper).astype(BF), table_ref[0])
+        spec_ref[1, rows, :] = dot((lower - upper).astype(BF), table_ref[1])
+    for i in range(NR):
+        rows = slice(128 * i, 128 * i + 128)
+        for parity in range(2):
+            lanes = slice(MP * parity, MP * parity + MP)
+            part_a, part_b = spec_ref[parity, rows, :MP], spec_ref[parity, rows, MP:]
+            for k in range(NK):
+                g = NK * i + k
+                real = gain_ref[g : g + 1, lanes]
+                imag = gain_ref[12 + g : 13 + g, lanes]
+                block = slice(128 * k, 128 * k + 128)
+                filt_ref[i, parity, block, :MP] = (real * part_a + imag * part_b).astype(BF)
+                filt_ref[i, parity, block, MP:] = (real * part_b - imag * part_a).astype(BF)
+        result = dot_nt(filt_ref[i, 0], places[0]) + sign * dot_nt(filt_ref[i, 1], places[1])
+        result = (result * (2.0 / NLON)).astype(BF)
+        parts = [dot(filter_ref[k], result[128 * k : 128 * k + 128]) for k in range(NK)]
+        for q in range(12):
+            total = weights_ref[NK * i, q] * parts[0]
+            for k in range(1, NK):
+                total = total + weights_ref[NK * i + k, q] * parts[k]
+            total_ref[q] = total if i == 0 else total_ref[q] + total
+    for band, ref in enumerate((first_ref, own_ref, second_ref)):
+        for first in range(2):
+            lower, upper = total_ref[4 * band + first], total_ref[4 * band + 2 + first]
+            base = 384 * first
+            dtype = ref.dtype
+            ref[:, base : base + 128] = lower[:, :128].astype(dtype)
+            middle = jnp.concatenate([lower[:, 128:], upper[:, 128:]], axis=1)
+            ref[:, base + 128 : base + 256] = middle.astype(dtype)
+            ref[:, base + 256 : base + 384] = upper[:, :128].astype(dtype)
     bring([(own_ref, own_hbm)], sems)[0].wait()
 
 
-def halo_sum_kernel(own_hbm, first_ref, second_ref, chunks_ref, send_ref, own_ref, sems):
-    copies = bring([(own_hbm, own_ref)], sems)
-    chunk = chunks_ref[0].astype(F32)
-    for n in range(1, chunks_ref.shape[0]):
-        chunk = chunk + chunks_ref[n].astype(F32)
-    chunk = chunk.astype(BF)
-    size = chunk.shape[0]
-    copies[0].wait()
-    for z in range(NZ):
-        total = own_ref[z] + first_ref[z].astype(F32) + second_ref[z].astype(F32)
-        total = total.astype(BF)
-        for tile in range(3):
-            send_ref[z, 32 * tile : 32 * tile + 32, :] = total[:, 128 * tile : 128 * tile + 128]
-        send_ref[z, 96 : 96 + size, :] = chunk
-
-
-def chunk_sum_kernel(recv_ref, out_ref):
-    size = recv_ref.shape[1] - 96
-    total = recv_ref[0, 96:, :].astype(F32)
-    for z in range(1, NZ):
-        total = total + recv_ref[z, 96:, :].astype(F32)
+def sum_kernel(copies, recv_ref, out_ref):
+    total = recv_ref[0].astype(F32)
+    for n in range(1, recv_ref.shape[0]):
+        total = total + recv_ref[n].astype(F32)
     total = total.astype(BF)
-    for n in range(WIDE // size):
-        out_ref[size * n : size * n + size, :] = total
-
-
-def field_kernel(recv_ref, state_grad_ref, grad_ref):
-    totals = []
-    for first in range(2):
-        tiles = []
-        for tile in range(3):
-            base = 32 * tile + CB * first
-            tiles.append(
-                jnp.concatenate([recv_ref[s, base : base + CB, :] for s in range(NZ)], axis=0)
-            )
-        lat_part = jnp.concatenate(tiles, axis=1).astype(F32)
-        total = state_grad_ref[:, 384 * first : 384 * first + 384] + lat_part
-        totals.append(total.astype(BF))
-    grad_ref[...] = dot_nt(point_select(), jnp.concatenate(totals, axis=1)).astype(BF)
+    for n in range(copies):
+        out_ref[n] = total
+
+
+def field_kernel(own_hbm, state_grad_hbm, first_ref, second_ref, grad_ref, own_ref, state_grad_ref, sems):
+    copies = bring(((own_hbm, own_ref), (state_grad_hbm, state_grad_ref)), sems)
+    select = point_select()
+    for copy in copies:
+        copy.wait()
+    lat_part = own_ref[...] + first_ref[...].astype(F32) + second_ref[...].astype(F32)
+    total = state_grad_ref[...] + lat_part.astype(BF).astype(F32)
+    grad_ref[...] = dot_nt(select, total.astype(BF)).astype(BF)
 
 
 def weights_kernel(scale, grads_ref, filter_ref, inner_ref, outer_ref):
@@ -444,9 +473,9 @@
     inner_weights,
     outer_weights,
 ):
-    group = lax.axis_size("lat")
-    grad_scale = 1.0 / math.sqrt(lax.axis_size("ens") * group * NR * NLON)
-    table = hold(jnp.asarray(dft_table()))
+    group = lax.axis_size("ens") * lax.axis_size("lat")
+    grad_scale = 1.0 / math.sqrt(group * NR * NLON)
+    table = jnp.asarray(dft_table())
 
     field_points = fields[0].transpose(1, 0, 2).reshape(LON * NR, 128)
     cot_points = cotangent[0].transpose(1, 0, 2).reshape(LON * NR, 128)
@@ -456,17 +485,17 @@
     )(hold(field_points))
     own = lax.all_to_all(send_fields, "lon", 0, 0, tiled=True)
 
-    cot_wide, coupling, turned, gains = call(
+    cot_wide, coupling, masked, gains = call(
         prepare_kernel,
         (
             shaped((128, 768)),
             shaped((192, 192)),
-            in_hbm((192, 192)),
+            in_hbm((12, 12), F32),
             shaped((24, 2 * MP), F32),
         ),
         2 * 720 * 768 * 128,
         [
-            pltpu.VMEM((192, 192), BF),
+            pltpu.VMEM((12, 12), F32),
             pltpu.VMEM((720, 128), BF),
             pltpu.VMEM((NK, NR, 12), BF),
             pltpu.VMEM((NK, NR, MODES), F32),
@@ -494,58 +523,70 @@
     ]
     send_filtered = call(
         filter_kernel, shaped((NZ, 96, 384)), 8 * 192 * KP * KP, work, vmem(5) + hbm(1)
-    )(first, own, second, coupling, gains, table)
+    )(first, own, second, coupling, gains, hold(table))
     filtered = lax.all_to_all(send_filtered, "lon", 0, 0, tiled=True)
 
-    send_back, state_grad, grads = call(
+    back, grads, state_grad = call(
         mlp_kernel,
-        (shaped((NZ, 96, 384)), in_hbm((128, 768), F32), in_hbm((WIDE, 128))),
+        (in_hbm((256, 384)), in_hbm((WIDE, 128)), in_hbm((128, 768), F32)),
         2 * 768 * 128 * 256 * 10,
         [
+            pltpu.VMEM((256, 384), BF),
+            pltpu.VMEM((WIDE, 128), BF),
             pltpu.VMEM((128, 768), F32),
-            pltpu.VMEM((WIDE, 128), BF),
+            pltpu.SemaphoreType.DMA((3,)),
+        ],
+        vmem(6),
+        tuple(hbm(3)),
+    )(filtered, field_wide, cot_wide, filter_weights, inner_weights, outer_weights)
+    back = lax.all_gather(back, "lon", tiled=True).reshape(NZ, 256, 384)
+
+    def summed(value, copies):
+        return call(
+            functools.partial(sum_kernel, copies),
+            shaped((copies,) + value.shape[1:]),
+            value.size,
+            (),
+            vmem(1),
+        )(value)
+
+    share = WIDE // group
+    chunks = lax.all_to_all(grads.reshape(group, share, 128), ("ens", "lat"), 0, 0, tiled=True)
+    chunks = lax.all_to_all(summed(chunks, NZ), "lon", 0, 0, tiled=True)
+    gathered = lax.all_to_all(summed(chunks, group), ("ens", "lat"), 0, 0, tiled=True)
+
+    to_first, kept, to_second = call(
+        adjoint_kernel,
+        (shaped((128, 768)), in_hbm((128, 768), F32), shaped((128, 768))),
+        4 * 512 * KP * KP + 4 * 1536 * KP * 192,
+        [
+            pltpu.VMEM((512, 2 * KP), BF),
+            pltpu.VMEM((NZ, 256, 128), BF),
+            pltpu.VMEM((2, 512, 2 * MP), F32),
+            pltpu.VMEM((NR, 2, 384, 2 * MP), BF),
+            pltpu.VMEM((12, 128, 192), F32),
+            pltpu.VMEM((128, 768), F32),
+            pltpu.SemaphoreType.DMA((3 * NZ,)),
+        ],
+        hbm(1) + [pl.BlockSpec(memory_space=pltpu.SMEM)] + vmem(3),
+        tuple(vmem(1) + hbm(1) + vmem(1)),
+    )(hold(back), masked, gains, table, filter_weights)
+    from_first = swapped(to_first, 0)
+    from_second = swapped(to_second, 1)
+    grad_points = call(
+        field_kernel,
+        shaped((LON * NR, 128)),
+        2 * 720 * 768 * 128,
+        [
+            pltpu.VMEM((128, 768), F32),
+            pltpu.VMEM((128, 768), F32),
             pltpu.SemaphoreType.DMA((2,)),
         ],
-        vmem(6),
-        tuple(vmem(1) + hbm(2)),
-    )(filtered, field_wide, cot_wide, filter_weights, inner_weights, outer_weights)
-    back = lax.all_to_all(send_back, "lon", 0, 0, tiled=True)
-    grads_other = lax.ppermute(grads, "ens", [(0, 1), (1, 0)])
-    grads = (grads.astype(F32) + grads_other.astype(F32)).astype(BF)
-    share = WIDE // group
-    chunks = lax.all_to_all(grads.reshape(group, share, 128), "lat", 0, 0, tiled=True)
-
-    pieces = (NZ, 32, 384)
-    to_first, kept, to_second = call(
-        adjoint_kernel,
-        (shaped(pieces), in_hbm(pieces, F32), shaped(pieces)),
-        8 * 192 * KP * KP,
-        [pltpu.VMEM((192, 192), BF), pltpu.VMEM(pieces, F32)] + work,
-        vmem(1) + hbm(1) + vmem(1) + hbm(1),
-        tuple(vmem(1) + hbm(1) + vmem(1)),
-    )(back, hold(turned), gains, table)
-    from_first = swapped(to_first, 0)
-    from_second = swapped(to_second, 1)
-    send_lat = call(
-        halo_sum_kernel,
-        shaped((NZ, 96 + share, 128)),
-        300000,
-        [pltpu.VMEM(pieces, F32), pltpu.SemaphoreType.DMA((1,))],
-        hbm(1) + vmem(3),
-    )(hold(kept), from_first, from_second, chunks)
-    lat_parts = lax.all_to_all(send_lat, "lon", 0, 0, tiled=True)
-
-    spread = call(chunk_sum_kernel, shaped((WIDE, 128)), 40000, (), vmem(1))(lat_parts)
-    gathered = lax.all_to_all(spread.reshape(group, share, 128), "lat", 0, 0, tiled=True)
-    grad_points = call(field_kernel, shaped((LON * NR, 128)), 2 * 720 * 768 * 128, (), vmem(2))(
-        lat_parts, hold(state_grad)
-    )
-
-    def weights(*refs):
-        weights_kernel(grad_scale, *refs)
+        hbm(2) + vmem(2),
+    )(hold(kept), hold(state_grad), from_first, from_second)
 
     filter_grad, inner_grad, outer_grad = call(
-        weights,
+        functools.partial(weights_kernel, grad_scale),
         (shaped((NK, 128, 128), F32), shaped((128, 256), F32), shaped((256, 128), F32)),
         WIDE * 128,
         (),

time: 143 us -> 133 us (0.930)
  waiting for transfers between devices: 26.3 us -> 3.16 us
  starting transfers between devices: 37.8 us -> 20.3 us
  blocking collectives: 55.3 us -> 72.5 us
  between operations: 0.79 us -> 14.2 us
  Pallas kernels: 19.9 us -> 21.8 us
  other arithmetic: 1.73 us -> 0 us
    all_to_all x3 -> x1, waiting for transfers between devices: 19.3 us -> 0.01 us  [local(): lax.all_to_all(summed(chunks, group), ('ens', 'lat'), 0, 0, tiled=True)]
    all_to_all x1 -> x2, blocking collectives: 14.8 us -> 31.8 us  [the longest x1 22.4 us: local(): lax.all_to_all(grads.reshape(group, share, 128), ('ens', 'lat'), 0, 0, ti...]
    all_to_all x3 -> x1, starting transfers between devices: 20 us -> 7.07 us  [local(): lax.all_to_all(summed(chunks, group), ('ens', 'lat'), 0, 0, tiled=True)]
    ppermute x1 -> x0, waiting for transfers between devices: 5.64 us -> none  [local(): grads_other = lax.ppermute(grads, 'ens', [(0, 1), (1, 0)])]
    ppermute x1 -> x0, starting transfers between devices: 4.59 us -> none  [local(): grads_other = lax.ppermute(grads, 'ens', [(0, 1), (1, 0)])]
    pallas_call x7, Pallas kernels: 15.5 us -> 17.3 us  [the longest x1 8.03 us: local(): call(adjoint_kernel, (shaped((128, 768)), in_hbm((128, 768), F32), shaped...]
    ppermute x4, waiting for transfers between devices: 1.3 us -> 3.12 us  [swapped(): return lax.ppermute(value, 'lat', pairs)]
    convert_element_type x1 -> x0, other arithmetic: 1.73 us -> none  [local(): grads = (grads.astype(F32) + grads_other.astype(F32)).astype(BF)]
  transfers between devices with their start and end apart: 8 -> 6, of which waited for: 5 -> 1; matrix products, arithmetic and copies ran while one was open for 1% -> 0% of each run, Pallas kernels for 6% -> 9%
where the time goes in v3:
time: 133 us; the launch traced here: 132 us
  blocking collectives  72.5 us (55%)
  Pallas kernels  21.8 us (16%)
  starting transfers between devices  20.3 us (15%)
  between operations  14.2 us (11%)
  waiting for transfers between devices  3.16 us (2%)
    all_to_all x1, blocking collectives, local(): lax.all_to_all(grads.reshape(group, share, 128), ('ens', 'lat'), 0, 0, ti...  22.4 us
    all_to_all x1, blocking collectives, local(): filtered = lax.all_to_all(send_filtered, 'lon', 0, 0, tiled=True)  21.2 us
    all_to_all x1, blocking collectives, local(): own = lax.all_to_all(send_fields, 'lon', 0, 0, tiled=True)  19.5 us
    ppermute x4, starting transfers between devices, swapped(): return lax.ppermute(value, 'lat', pairs)  13.2 us
    all_to_all x1, blocking collectives, local(): chunks = lax.all_to_all(summed(chunks, NZ), 'lon', 0, 0, tiled=True)  9.42 us
    pallas_call x1, Pallas kernels, local(): call(adjoint_kernel, (shaped((128, 768)), in_hbm((128, 768), F32), shaped...  8.03 us
    all_to_all x1, starting transfers between devices, local(): lax.all_to_all(summed(chunks, group), ('ens', 'lat'), 0, 0, tiled=True)  7.07 us
    pallas_call x1, Pallas kernels, local(): call(filter_kernel, shaped((NZ, 96, 384)), 8 * 192 * KP * KP, work, vmem(...  3.18 us
  transfers between devices with their start and end apart: 6, of which 1 were waited for; matrix products, arithmetic and copies ran while one was open for 0% of the time, Pallas kernels for 9%

profile of v3, /device:TPU:1, one launch (start us, length us, event | category | flops | bytes accessed | tf_op | source)
XLA Modules:
  0.0 132.0 jit_solution(16052273085747002949)
XLA Ops:
  7.2 0.0 all-gather.2.cloned.1.call-start
  7.2 1.3 shard_map.129
  8.5 19.5 %all_to_all.25.own_ref = bf16[8,32,384]{2,1,0:T(8,128)(2,1)S(1)} all-to-all(bf16[8,32,384]{2,1,0:T(8,128)(2,1)S(1)} %get-tuple-element.19), channel_id=1, replica_groups=mesh['ens'=2,'lat'=32,'lon'=8] {'lon'}, dimensions={0} | all-to-all | bytes 393216 | tf_op jit(solution)/shard_map/all_to_all | solution.py:486
  28.0 5.7 %collective-permute-start.1 = (bf16[8,32,384]{2,1,0:T(8,128)(2,1)S(1)}, bf16[8,32,384]{2,1,0:T(8,128)(2,1)S(1)}, u32[]{:S(2)}, u32[]{:S(2)}) collective-permute-start(bf16[8,32,384]{2,1,0:T(8,128)(2,1)S(1)} %all_to_all.25.own_ref), channel_id=1, source_target_pairs={{8,16},{16,8},{24,32},{32,24},{40,48},{48,40},{56,64},{64,56},{72,... | collective-permute-start | bytes 589832 | tf_op jit(solution)/shard_map/ppermute | solution.py:462
  33.7 1.9 %collective-permute-start = (bf16[8,32,384]{2,1,0:T(8,128)(2,1)S(1)}, bf16[8,32,384]{2,1,0:T(8,128)(2,1)S(1)}, u32[]{:S(2)}, u32[]{:S(2)}) collective-permute-start(bf16[8,32,384]{2,1,0:T(8,128)(2,1)S(1)} %all_to_all.25.own_ref), channel_id=1, source_target_pairs={{0,8},{8,0},{16,24},{24,16},{32,40},{40,32},{48,56},{56,48},{64,72... | collective-permute-start | bytes 589832 | tf_op jit(solution)/shard_map/ppermute | solution.py:462
  35.6 2.8 %shard_map.130 = (bf16[128,768]{1,0:T(8,128)(2,1)S(1)}, bf16[192,192]{1,0:T(8,128)(2,1)S(1)}, f32[12,12]{1,0:T(8,128)}, f32[24,768]{1,0:T(8,128)S(1)}) custom-call(bf16[720,128]{1,0:T(8,128)(2,1)} %bitcast.23, bf16[3,4,12]{2,1,0:T(4,128)(2,1)} %weights_hbm.1, f32[3,4,720]{2,1,0:T(4,128)} %real_hbm.1, f32[3,4,720]{2,1,0:T(4,128)} %imag_hbm.1, s32[1,3]{1,0:T(1,128)} %support_hbm.1), custom_call_target="tpu_custom_call" | custom-call | flops 141557760 | bytes 689280 | tf_op jit(solution)/shard_map/pallas_call | solution.py:488
  38.4 0.0 collective-permute-done.1.second_ref
  38.4 0.0 collective-permute-done.first_ref
  38.4 0.0 copy-start.1
  38.4 0.0 copy-start.2
  38.5 0.0 copy-start.3
  38.5 3.2 %shard_map.131 = bf16[8,96,384]{2,1,0:T(8,128)(2,1)S(1)} custom-call(bf16[8,32,384]{2,1,0:T(8,128)(2,1)S(1)} %collective-permute-done.first_ref, bf16[8,32,384]{2,1,0:T(8,128)(2,1)S(1)} %all_to_all.25.own_ref, bf16[8,32,384]{2,1,0:T(8,128)(2,1)S(1)} %collective-permute-done.1.second_ref, bf16[192,192]{1,0:T(8,128)(2,1)S(1)} %get-tuple-element.20.coupling_ref, ...), custom_call_target="tpu_custom_call" | custom-call | flops 905969664 | bytes 1179648 | tf_op jit(solution)/shard_map/pallas_call | solution.py:524
  41.7 0.0 copy-start
  41.7 0.0 copy-start.4
  41.7 21.2 %all_to_all.26.recv_ref = bf16[8,96,384]{2,1,0:T(8,128)(2,1)S(1)} all-to-all(bf16[8,96,384]{2,1,0:T(8,128)(2,1)S(1)} %shard_map.131), channel_id=1, replica_groups=mesh['ens'=2,'lat'=32,'lon'=8] {'lon'}, dimensions={0} | all-to-all | bytes 1179648 | tf_op jit(solution)/shard_map/all_to_all | solution.py:527
  62.9 0.0 copy-done.1
  62.9 0.0 copy-done.2
  62.9 0.0 copy-done.3
  62.9 2.6 %shard_map.132 = (bf16[256,384]{1,0:T(8,128)(2,1)}, bf16[1024,128]{1,0:T(8,128)(2,1)}, f32[128,768]{1,0:T(8,128)}) custom-call(bf16[8,96,384]{2,1,0:T(8,128)(2,1)S(1)} %all_to_all.26.recv_ref, bf16[128,768]{1,0:T(8,128)(2,1)S(1)} %get-tuple-element.22.fields_ref, bf16[128,768]{1,0:T(8,128)(2,1)S(1)} %get-tuple-element.23.cot_ref, ...), custom_call_target="tpu_custom_call" | custom-call | flops 503316480 | bytes 1703936 | tf_op jit(solution)/shard_map/pallas_call | solution.py:529
  65.5 0.0 all-gather.2.cloned.1.call-update
  65.5 22.4 %all_to_all.27.recv_ref = bf16[64,16,128]{2,1,0:T(8,128)(2,1)S(1)} all-to-all(bf16[64,16,128]{2,1,0:T(8,128)(2,1)} %bitcast.19), channel_id=1, replica_groups=mesh['ens'=2,'lat'=32,'lon'=8] {'ens','lat'}, dimensions={0} | all-to-all | bytes 524288 | tf_op jit(solution)/shard_map/all_to_all | solution.py:554
  87.9 0.1 shard_map.135
  88.0 9.4 %all_to_all.28.recv_ref = bf16[8,16,128]{2,1,0:T(8,128)(2,1)S(1)} all-to-all(bf16[8,16,128]{2,1,0:T(8,128)(2,1)S(1)} %shard_map.135), channel_id=1, replica_groups=mesh['ens'=2,'lat'=32,'lon'=8] {'lon'}, dimensions={0} | all-to-all | bytes 65536 | tf_op jit(solution)/shard_map/all_to_all | solution.py:555
  97.4 0.7 shard_map.136
  98.1 7.1 %all-to-all-start.4 = ((bf16[64,16,128]{2,1,0:T(8,128)(2,1)}), bf16[64,16,128]{2,1,0:T(8,128)(2,1)S(1)}, u32[]{:S(2)}, u32[]{:S(2)}) async-start(bf16[64,16,128]{2,1,0:T(8,128)(2,1)} %shard_map.136), calls=%async_computation.4 | async-start | bytes 524288 | tf_op jit(solution)/shard_map/all_to_all | solution.py:556
  105.2 0.0 all-gather.2.cloned.1.call-done
  105.2 0.0 copy-done
  105.3 0.0 copy-done.4
  105.3 8.0 %shard_map.133 = (bf16[128,768]{1,0:T(8,128)(2,1)S(1)}, f32[128,768]{1,0:T(8,128)}, bf16[128,768]{1,0:T(8,128)(2,1)S(1)}) custom-call(bf16[8,256,384]{2,1,0:T(8,128)(2,1)} %bitcast.21, f32[12,12]{1,0:T(8,128)S(1)} %copy-done.4, f32[24,768]{1,0:T(8,128)S(1)} %get-tuple-element.21.gain_ref, bf16[2,768,768]{2,1,0:T(8,128)(2,1)S(1)} %copy-done, ...), custom_call_target="tpu_custom_call" | custom-call | flops 2113929216 | bytes 1572864 | tf_op jit(solution)/shard_map/pallas_call | solution.py:558
  113.3 2.5 %collective-permute-start.2 = (bf16[128,768]{1,0:T(8,128)(2,1)S(1)}, bf16[128,768]{1,0:T(8,128)(2,1)S(1)}, u32[]{:S(2)}, u32[]{:S(2)}) collective-permute-start(bf16[128,768]{1,0:T(8,128)(2,1)S(1)} %get-tuple-element.28), channel_id=1, source_target_pairs={{0,8},{8,0},{16,24},{24,16},{32,40},{40,32},{48,56},{56,48},{64,72... | collective-permute-start | bytes 589832 | tf_op jit(solution)/shard_map/ppermute | solution.py:462
  115.8 3.1 %collective-permute-start.3 = (bf16[128,768]{1,0:T(8,128)(2,1)S(1)}, bf16[128,768]{1,0:T(8,128)(2,1)S(1)}, u32[]{:S(2)}, u32[]{:S(2)}) collective-permute-start(bf16[128,768]{1,0:T(8,128)(2,1)S(1)} %get-tuple-element.29), channel_id=1, source_target_pairs={{8,16},{16,8},{24,32},{32,24},{40,48},{48,40},{56,64},{64,56},{72,... | collective-permute-start | bytes 589832 | tf_op jit(solution)/shard_map/ppermute | solution.py:462
  118.9 0.0 all-to-all-done.4
  118.9 0.8 shard_map.137
  119.7 0.0 collective-permute-done.2.first_ref
  119.7 3.1 %collective-permute-done.3.second_ref = bf16[128,768]{1,0:T(8,128)(2,1)S(1)} collective-permute-done((bf16[128,768]{1,0:T(8,128)(2,1)S(1)}, bf16[128,768]{1,0:T(8,128)(2,1)S(1)}, u32[]{:S(2)}, u32[]{:S(2)}) %collective-permute-start.3) | collective-permute-done | bytes 196640 | tf_op jit(solution)/shard_map/ppermute | solution.py:462
  122.8 2.3 %shard_map.134 = bf16[720,128]{1,0:T(8,128)(2,1)} custom-call(f32[128,768]{1,0:T(8,128)} %get-tuple-element.26.own_hbm, f32[128,768]{1,0:T(8,128)} %get-tuple-element.27.state_grad_hbm, bf16[128,768]{1,0:T(8,128)(2,1)S(1)} %collective-permute-done.2.first_ref, bf16[128,768]{1,0:T(8,128)(2,1)S(1)} %collective-permute-done.3.second_ref), custom_call_target="tpu_custom_call" | custom-call | flops 141557760 | bytes 368640 | tf_op jit(solution)/shard_map/pallas_call | solution.py:576
Async XLA Ops:
  7.2 98.1 %all-gather.2.cloned.1.call-start = ((), (), s32[]{:S(2)}) async-start(), calls=%async_computation.5 | async-start | bytes 1769472 | tf_op jit(solution)/shard_map/all_gather | solution.py:542
  28.0 10.4 %collective-permute-start.1 = (bf16[8,32,384]{2,1,0:T(8,128)(2,1)S(1)}, bf16[8,32,384]{2,1,0:T(8,128)(2,1)S(1)}, u32[]{:S(2)}, u32[]{:S(2)}) collective-permute-start(bf16[8,32,384]{2,1,0:T(8,128)(2,1)S(1)} %all_to_all.25.own_ref), channel_id=1, source_target_pairs={{8,16},{16,8},{24,32},{32,24},{40,48},{48,40},{56,64},{64,56},{72,... | collective-permute-start | bytes 589832 | tf_op jit(solution)/shard_map/ppermute | solution.py:462
  33.7 4.7 %collective-permute-start = (bf16[8,32,384]{2,1,0:T(8,128)(2,1)S(1)}, bf16[8,32,384]{2,1,0:T(8,128)(2,1)S(1)}, u32[]{:S(2)}, u32[]{:S(2)}) collective-permute-start(bf16[8,32,384]{2,1,0:T(8,128)(2,1)S(1)} %all_to_all.25.own_ref), channel_id=1, source_target_pairs={{0,8},{8,0},{16,24},{24,16},{32,40},{40,32},{48,56},{56,48},{64,72... | collective-permute-start | bytes 589832 | tf_op jit(solution)/shard_map/ppermute | solution.py:462
  38.4 24.4 %copy-start.1 = (bf16[3,128,128]{2,1,0:T(8,128)(2,1)S(1)}, bf16[3,128,128]{2,1,0:T(8,128)(2,1)}, u32[]{:S(2)}) copy-start(bf16[3,128,128]{2,1,0:T(8,128)(2,1)} %filter_ref.3) | copy-start | bytes 294916
  38.4 24.4 %copy-start.2 = (bf16[128,256]{1,0:T(8,128)(2,1)S(1)}, bf16[128,256]{1,0:T(8,128)(2,1)}, u32[]{:S(2)}) copy-start(bf16[128,256]{1,0:T(8,128)(2,1)} %inner_ref.1) | copy-start | bytes 196612
  38.5 24.4 %copy-start.3 = (bf16[256,128]{1,0:T(8,128)(2,1)S(1)}, bf16[256,128]{1,0:T(8,128)(2,1)}, u32[]{:S(2)}) copy-start(bf16[256,128]{1,0:T(8,128)(2,1)} %outer_ref.1) | copy-start | bytes 196612
  41.7 63.6 %copy-start = (bf16[2,768,768]{2,1,0:T(8,128)(2,1)S(1)}, bf16[2,768,768]{2,1,0:T(8,128)(2,1)}, u32[]{:S(2)}) copy-start(bf16[2,768,768]{2,1,0:T(8,128)(2,1)} %constant.2.clone.table_hbm.table_ref) | copy-start | bytes 7077892
  41.7 63.6 %copy-start.4 = (f32[12,12]{1,0:T(8,128)S(1)}, f32[12,12]{1,0:T(8,128)}, u32[]{:S(2)}) copy-start(f32[12,12]{1,0:T(8,128)} %get-tuple-element.25.weights_ref) | copy-start | bytes 1732
  98.1 20.8 %all-to-all-start.4 = ((bf16[64,16,128]{2,1,0:T(8,128)(2,1)}), bf16[64,16,128]{2,1,0:T(8,128)(2,1)S(1)}, u32[]{:S(2)}, u32[]{:S(2)}) async-start(bf16[64,16,128]{2,1,0:T(8,128)(2,1)} %shard_map.136), calls=%async_computation.4 | async-start | bytes 524288 | tf_op jit(solution)/shard_map/all_to_all | solution.py:556
  113.3 6.4 %collective-permute-start.2 = (bf16[128,768]{1,0:T(8,128)(2,1)S(1)}, bf16[128,768]{1,0:T(8,128)(2,1)S(1)}, u32[]{:S(2)}, u32[]{:S(2)}) collective-permute-start(bf16[128,768]{1,0:T(8,128)(2,1)S(1)} %get-tuple-element.28), channel_id=1, source_target_pairs={{0,8},{8,0},{16,24},{24,16},{32,40},{40,32},{48,56},{56,48},{64,72... | collective-permute-start | bytes 589832 | tf_op jit(solution)/shard_map/ppermute | solution.py:462
  115.8 7.0 %collective-permute-start.3 = (bf16[128,768]{1,0:T(8,128)(2,1)S(1)}, bf16[128,768]{1,0:T(8,128)(2,1)S(1)}, u32[]{:S(2)}, u32[]{:S(2)}) collective-permute-start(bf16[128,768]{1,0:T(8,128)(2,1)S(1)} %get-tuple-element.29), channel_id=1, source_target_pairs={{8,16},{16,8},{24,32},{32,24},{40,48},{48,40},{56,64},{64,56},{72,... | collective-permute-start | bytes 589832 | tf_op jit(solution)/shard_map/ppermute | solution.py:462
Sparse Core Ops, SparseCore 0:
  65.6 35.3 all-gather.1

commit v4 on v3

--- a/solution.py
+++ b/solution.py
@@ -142,9 +142,9 @@
     support_hbm,
     wide_ref,
     coupling_ref,
-    masked_hbm,
+    turned_hbm,
     gain_ref,
-    masked_ref,
+    turned_ref,
     points_ref,
     weights_ref,
     real_ref,
@@ -176,15 +176,15 @@
     rows = [weights_ref[k].astype(F32) for k in range(NK)]
     masked = jnp.concatenate([rows[k][i : i + 1] * seen for i in range(NR) for k in range(NK)], axis=0)
     turned = jnp.concatenate([masked[:, 8:12], masked[:, 4:8], masked[:, 0:4]], axis=1)
-    masked = jnp.where(flip, turned, masked)
-    masked_ref[...] = masked
-    copies = bring([(masked_ref, masked_hbm)], sems)
-    masked = masked.astype(BF)
+    masked = jnp.where(flip, turned, masked).astype(BF)
     size = 12 * CB
     expand = (iota((size, 12), 0) // CB == iota((size, 12), 1)).astype(F32).astype(BF)
     same = (iota((size, size), 0) & 15) == (iota((size, size), 1) & 15)
     wide = dot_nt(dot(expand, masked).astype(BF), expand)
     coupling_ref[...] = jnp.where(same, wide, 0.0).astype(BF)
+    wide = dot_nt(dot_nt(expand, masked).astype(BF), expand)
+    turned_ref[...] = jnp.where(same, wide, 0.0).astype(BF)
+    copies = bring([(turned_ref, turned_hbm)], sems)
 
     lane = iota((MODES, 2 * MP), 1)
     odd = (lane >= MP).astype(jnp.int32)
@@ -314,27 +314,31 @@
 
 def adjoint_kernel(
     recv_hbm,
-    weights_ref,
+    turned_hbm,
+    state_grad_hbm,
     gain_ref,
     table_ref,
     filter_ref,
     first_ref,
-    own_hbm,
+    base_hbm,
     second_ref,
     x_ref,
     middle_ref,
     spec_ref,
     filt_ref,
-    total_ref,
-    own_ref,
+    part_ref,
+    turned_ref,
+    state_grad_ref,
+    base_ref,
     sems,
 ):
-    pairs = []
-    for n in range(NZ):
-        lanes = pl.ds(128 * tile_of(n), 128)
-        pairs.append((recv_hbm.at[n, :, pl.ds(0, 128)], x_ref.at[pl.ds(0, 256), lanes]))
-        pairs.append((recv_hbm.at[n, :, pl.ds(256, 128)], x_ref.at[pl.ds(256, 256), lanes]))
-        pairs.append((recv_hbm.at[n, :, pl.ds(128, 128)], middle_ref.at[n]))
+    pairs = [(recv_hbm.at[n, :, pl.ds(128, 128)], middle_ref.at[n]) for n in range(NZ)]
+    for half in range(2):
+        for n in range(NZ):
+            lanes = pl.ds(128 * tile_of(n), 128)
+            rows = pl.ds(256 * half, 256)
+            pairs.append((recv_hbm.at[n, :, pl.ds(256 * half, 128)], x_ref.at[rows, lanes]))
+    pairs += [(turned_hbm, turned_ref), (state_grad_hbm, state_grad_ref)]
     copies = bring(pairs, sems)
     z = lax.axis_index("lon")
     quarter = lax.rem(z, 4)
@@ -344,49 +348,51 @@
     places = [
         jnp.concatenate([table_ref[p, main, :], table_ref[p, tail, :]], axis=0) for p in range(2)
     ]
-    for copy in copies:
-        copy.wait()
-    for pair in range(NZ // 2):
-        lanes = slice(128 * tile_of_pair(pair), 128 * tile_of_pair(pair) + 128)
-        even, odd = middle_ref[2 * pair], middle_ref[2 * pair + 1]
-        x_ref[0:256, lanes] = low_halves(even, odd)
-        x_ref[256:512, lanes] = high_halves(even, odd)
-    for i in range(NR):
-        rows = slice(128 * i, 128 * i + 128)
-        lower = x_ref[rows, :KP].astype(F32)
-        upper = x_ref[rows, KP:].astype(F32)
-        spec_ref[0, rows, :] = dot((lower + upper).astype(BF), table_ref[0])
-        spec_ref[1, rows, :] = dot((lower - upper).astype(BF), table_ref[1])
-    for i in range(NR):
-        rows = slice(128 * i, 128 * i + 128)
-        for parity in range(2):
-            lanes = slice(MP * parity, MP * parity + MP)
-            part_a, part_b = spec_ref[parity, rows, :MP], spec_ref[parity, rows, MP:]
+    for half in range(2):
+        for copy in copies[0 : 2 * NZ] if half == 0 else copies[2 * NZ :]:
+            copy.wait()
+        block = slice(256 * half, 256 * half + 256)
+        for pair in range(NZ // 2):
+            lanes = slice(128 * tile_of_pair(pair), 128 * tile_of_pair(pair) + 128)
+            even, odd = middle_ref[2 * pair], middle_ref[2 * pair + 1]
+            x_ref[block, lanes] = low_halves(even, odd) if half == 0 else high_halves(even, odd)
+        lower = x_ref[block, :KP].astype(F32)
+        upper = x_ref[block, KP:].astype(F32)
+        spec_ref[0, block, :] = dot((lower + upper).astype(BF), table_ref[0])
+        spec_ref[1, block, :] = dot((lower - upper).astype(BF), table_ref[1])
+        for i in (2 * half, 2 * half + 1):
+            rows = slice(128 * i, 128 * i + 128)
+            for parity in range(2):
+                lanes = slice(MP * parity, MP * parity + MP)
+                part_a, part_b = spec_ref[parity, rows, :MP], spec_ref[parity, rows, MP:]
+                for k in range(NK):
+                    g = NK * i + k
+                    real = gain_ref[g : g + 1, lanes]
+                    imag = gain_ref[12 + g : 13 + g, lanes]
+                    out = slice(128 * k, 128 * k + 128)
+                    filt_ref[i, parity, out, :MP] = (real * part_a + imag * part_b).astype(BF)
+                    filt_ref[i, parity, out, MP:] = (real * part_b - imag * part_a).astype(BF)
+            result = dot_nt(filt_ref[i, 0], places[0]) + sign * dot_nt(filt_ref[i, 1], places[1])
+            result = (result * (2.0 / NLON)).astype(BF)
             for k in range(NK):
-                g = NK * i + k
-                real = gain_ref[g : g + 1, lanes]
-                imag = gain_ref[12 + g : 13 + g, lanes]
-                block = slice(128 * k, 128 * k + 128)
-                filt_ref[i, parity, block, :MP] = (real * part_a + imag * part_b).astype(BF)
-                filt_ref[i, parity, block, MP:] = (real * part_b - imag * part_a).astype(BF)
-        result = dot_nt(filt_ref[i, 0], places[0]) + sign * dot_nt(filt_ref[i, 1], places[1])
-        result = (result * (2.0 / NLON)).astype(BF)
-        parts = [dot(filter_ref[k], result[128 * k : 128 * k + 128]) for k in range(NK)]
-        for q in range(12):
-            total = weights_ref[NK * i, q] * parts[0]
-            for k in range(1, NK):
-                total = total + weights_ref[NK * i + k, q] * parts[k]
-            total_ref[q] = total if i == 0 else total_ref[q] + total
-    for band, ref in enumerate((first_ref, own_ref, second_ref)):
-        for first in range(2):
-            lower, upper = total_ref[4 * band + first], total_ref[4 * band + 2 + first]
-            base = 384 * first
-            dtype = ref.dtype
-            ref[:, base : base + 128] = lower[:, :128].astype(dtype)
-            middle = jnp.concatenate([lower[:, 128:], upper[:, 128:]], axis=1)
-            ref[:, base + 128 : base + 256] = middle.astype(dtype)
-            ref[:, base + 256 : base + 384] = upper[:, :128].astype(dtype)
-    bring([(own_ref, own_hbm)], sems)[0].wait()
+                part = dot(filter_ref[k], result[128 * k : 128 * k + 128])
+                part_ref[NK * i + k] = part.astype(BF)
+    for s in range(NZ):
+        rows = slice(CB * s, CB * s + CB)
+        parts = jnp.concatenate([part_ref[g, rows, :] for g in range(12)], axis=0)
+        total = dot(turned_ref[...], parts)
+        for band, ref in enumerate((first_ref, base_ref, second_ref)):
+            for first in range(2):
+                base = 64 * band + CB * first
+                lower, upper = total[base : base + CB], total[base + 32 : base + 32 + CB]
+                middle = jnp.concatenate([lower[:, 128:], upper[:, 128:]], axis=1)
+                for tile, value in enumerate((lower[:, :128], middle, upper[:, :128])):
+                    lanes = slice(384 * first + 128 * tile, 384 * first + 128 * tile + 128)
+                    if band == 1:
+                        ref[rows, lanes] = value + state_grad_ref[rows, lanes]
+                    else:
+                        ref[rows, lanes] = value.astype(BF)
+    bring([(base_ref, base_hbm)], sems)[0].wait()
 
 
 def sum_kernel(copies, recv_ref, out_ref):
@@ -398,14 +404,12 @@
         out_ref[n] = total
 
 
-def field_kernel(own_hbm, state_grad_hbm, first_ref, second_ref, grad_ref, own_ref, state_grad_ref, sems):
-    copies = bring(((own_hbm, own_ref), (state_grad_hbm, state_grad_ref)), sems)
+def field_kernel(base_hbm, first_ref, second_ref, grad_ref, base_ref, sems):
+    copies = bring([(base_hbm, base_ref)], sems)
     select = point_select()
-    for copy in copies:
-        copy.wait()
-    lat_part = own_ref[...] + first_ref[...].astype(F32) + second_ref[...].astype(F32)
-    total = state_grad_ref[...] + lat_part.astype(BF).astype(F32)
-    grad_ref[...] = dot_nt(select, total.astype(BF)).astype(BF)
+    halo = first_ref[...].astype(F32) + second_ref[...].astype(F32)
+    copies[0].wait()
+    grad_ref[...] = dot_nt(select, (base_ref[...] + halo).astype(BF)).astype(BF)
 
 
 def weights_kernel(scale, grads_ref, filter_ref, inner_ref, outer_ref):
@@ -485,17 +489,17 @@
     )(hold(field_points))
     own = lax.all_to_all(send_fields, "lon", 0, 0, tiled=True)
 
-    cot_wide, coupling, masked, gains = call(
+    cot_wide, coupling, turned, gains = call(
         prepare_kernel,
         (
             shaped((128, 768)),
             shaped((192, 192)),
-            in_hbm((12, 12), F32),
+            in_hbm((192, 192)),
             shaped((24, 2 * MP), F32),
         ),
         2 * 720 * 768 * 128,
         [
-            pltpu.VMEM((12, 12), F32),
+            pltpu.VMEM((192, 192), BF),
             pltpu.VMEM((720, 128), BF),
             pltpu.VMEM((NK, NR, 12), BF),
             pltpu.VMEM((NK, NR, MODES), F32),
@@ -564,26 +568,24 @@
             pltpu.VMEM((NZ, 256, 128), BF),
             pltpu.VMEM((2, 512, 2 * MP), F32),
             pltpu.VMEM((NR, 2, 384, 2 * MP), BF),
-            pltpu.VMEM((12, 128, 192), F32),
+            pltpu.VMEM((12, 128, 192), BF),
+            pltpu.VMEM((192, 192), BF),
             pltpu.VMEM((128, 768), F32),
-            pltpu.SemaphoreType.DMA((3 * NZ,)),
+            pltpu.VMEM((128, 768), F32),
+            pltpu.SemaphoreType.DMA((3 * NZ + 2,)),
         ],
-        hbm(1) + [pl.BlockSpec(memory_space=pltpu.SMEM)] + vmem(3),
+        hbm(3) + vmem(3),
         tuple(vmem(1) + hbm(1) + vmem(1)),
-    )(hold(back), masked, gains, table, filter_weights)
+    )(hold(back), hold(turned), hold(state_grad), gains, table, filter_weights)
+    from_second = swapped(to_second, 1)
     from_first = swapped(to_first, 0)
-    from_second = swapped(to_second, 1)
     grad_points = call(
         field_kernel,
         shaped((LON * NR, 128)),
         2 * 720 * 768 * 128,
-        [
-            pltpu.VMEM((128, 768), F32),
-            pltpu.VMEM((128, 768), F32),
-            pltpu.SemaphoreType.DMA((2,)),
-        ],
-        hbm(2) + vmem(2),
-    )(hold(kept), hold(state_grad), from_first, from_second)
+        [pltpu.VMEM((128, 768), F32), pltpu.SemaphoreType.DMA((1,))],
+        hbm(1) + vmem(2),
+    )(hold(kept), from_second, from_first)
 
     filter_grad, inner_grad, outer_grad = call(
         functools.partial(weights_kernel, grad_scale),

time: 133 us -> 130 us (0.977)
  waiting for transfers between devices: 3.16 us -> 0.76 us
    ppermute x4, waiting for transfers between devices: 3.12 us -> 0.72 us  [swapped(): return lax.ppermute(value, 'lat', pairs)]
where the time goes in v4:
time: 130 us; the launch traced here: 128 us
  blocking collectives  72.5 us (56%)
  Pallas kernels  20.5 us (16%)
  starting transfers between devices  20.2 us (16%)
  between operations  14.2 us (11%)
    all_to_all x1, blocking collectives, local(): lax.all_to_all(grads.reshape(group, share, 128), ('ens', 'lat'), 0, 0, ti...  22.5 us
    all_to_all x1, blocking collectives, local(): filtered = lax.all_to_all(send_filtered, 'lon', 0, 0, tiled=True)  21.1 us
    all_to_all x1, blocking collectives, local(): own = lax.all_to_all(send_fields, 'lon', 0, 0, tiled=True)  19.5 us
    ppermute x4, starting transfers between devices, swapped(): return lax.ppermute(value, 'lat', pairs)  13.1 us
    all_to_all x1, blocking collectives, local(): chunks = lax.all_to_all(summed(chunks, NZ), 'lon', 0, 0, tiled=True)  9.41 us
    all_to_all x1, starting transfers between devices, local(): lax.all_to_all(summed(chunks, group), ('ens', 'lat'), 0, 0, tiled=True)  7.09 us
    pallas_call x1, Pallas kernels, local(): call(adjoint_kernel, (shaped((128, 768)), in_hbm((128, 768), F32), shaped...  6.83 us
    pallas_call x1, Pallas kernels, local(): call(filter_kernel, shaped((NZ, 96, 384)), 8 * 192 * KP * KP, work, vmem(...  3.17 us
  transfers between devices with their start and end apart: 6, of which 1 were waited for; matrix products, arithmetic and copies ran while one was open for 0% of the time, Pallas kernels for 9%

profile of v4, /device:TPU:1, one launch (start us, length us, event | category | flops | bytes accessed | tf_op | source)
XLA Modules:
  0.0 128.1 jit_solution(14944957143475161916)
XLA Ops:
  7.2 0.0 all-gather.2.cloned.1.call-start
  7.2 1.3 %shard_map.129 = (bf16[128,768]{1,0:T(8,128)(2,1)S(1)}, bf16[8,32,384]{2,1,0:T(8,128)(2,1)S(1)}) custom-call(bf16[720,128]{1,0:T(8,128)(2,1)} %bitcast.22), custom_call_target="tpu_custom_call" | custom-call | flops 141557760 | bytes 786432 | tf_op jit(solution)/shard_map/pallas_call | solution.py:486
  8.5 19.5 %all_to_all.25.own_ref = bf16[8,32,384]{2,1,0:T(8,128)(2,1)S(1)} all-to-all(bf16[8,32,384]{2,1,0:T(8,128)(2,1)S(1)} %get-tuple-element.19), channel_id=1, replica_groups=mesh['ens'=2,'lat'=32,'lon'=8] {'lon'}, dimensions={0} | all-to-all | bytes 393216 | tf_op jit(solution)/shard_map/all_to_all | solution.py:490
  28.0 5.7 %collective-permute-start.1 = (bf16[8,32,384]{2,1,0:T(8,128)(2,1)S(1)}, bf16[8,32,384]{2,1,0:T(8,128)(2,1)S(1)}, u32[]{:S(2)}, u32[]{:S(2)}) collective-permute-start(bf16[8,32,384]{2,1,0:T(8,128)(2,1)S(1)} %all_to_all.25.own_ref), channel_id=1, source_target_pairs={{8,16},{16,8},{24,32},{32,24},{40,48},{48,40},{56,64},{64,56},{72,... | collective-permute-start | bytes 589832 | tf_op jit(solution)/shard_map/ppermute | solution.py:466
  33.7 1.9 %collective-permute-start = (bf16[8,32,384]{2,1,0:T(8,128)(2,1)S(1)}, bf16[8,32,384]{2,1,0:T(8,128)(2,1)S(1)}, u32[]{:S(2)}, u32[]{:S(2)}) collective-permute-start(bf16[8,32,384]{2,1,0:T(8,128)(2,1)S(1)} %all_to_all.25.own_ref), channel_id=1, source_target_pairs={{0,8},{8,0},{16,24},{24,16},{32,40},{40,32},{48,56},{56,48},{64,72... | collective-permute-start | bytes 589832 | tf_op jit(solution)/shard_map/ppermute | solution.py:466
  35.6 2.9 %shard_map.130 = (bf16[128,768]{1,0:T(8,128)(2,1)S(1)}, bf16[192,192]{1,0:T(8,128)(2,1)S(1)}, bf16[192,192]{1,0:T(8,128)(2,1)}, f32[24,768]{1,0:T(8,128)S(1)}) custom-call(bf16[720,128]{1,0:T(8,128)(2,1)} %bitcast.23, bf16[3,4,12]{2,1,0:T(4,128)(2,1)} %weights_hbm.1, f32[3,4,720]{2,1,0:T(4,128)} %real_hbm.1, f32[3,4,720]{2,1,0:T(4,128)} %imag_hbm.1, ...), custom_call_target="tpu_custom_call" | custom-call | flops 141557760 | bytes 835584 | tf_op jit(solution)/shard_map/pallas_call | solution.py:492
  38.5 0.0 collective-permute-done.1.second_ref
  38.5 0.0 collective-permute-done.first_ref
  38.5 0.0 copy-start.1
  38.5 0.0 copy-start.2
  38.5 0.0 copy-start.3
  38.5 3.2 %shard_map.131 = bf16[8,96,384]{2,1,0:T(8,128)(2,1)S(1)} custom-call(bf16[8,32,384]{2,1,0:T(8,128)(2,1)S(1)} %collective-permute-done.first_ref, bf16[8,32,384]{2,1,0:T(8,128)(2,1)S(1)} %all_to_all.25.own_ref, bf16[8,32,384]{2,1,0:T(8,128)(2,1)S(1)} %collective-permute-done.1.second_ref, bf16[192,192]{1,0:T(8,128)(2,1)S(1)} %get-tuple-element.20.coupling_ref, ...), custom_call_target="tpu_custom_call" | custom-call | flops 905969664 | bytes 1179648 | tf_op jit(solution)/shard_map/pallas_call | solution.py:528
  41.7 0.0 copy-start
  41.7 21.1 %all_to_all.26.recv_ref = bf16[8,96,384]{2,1,0:T(8,128)(2,1)S(1)} all-to-all(bf16[8,96,384]{2,1,0:T(8,128)(2,1)S(1)} %shard_map.131), channel_id=1, replica_groups=mesh['ens'=2,'lat'=32,'lon'=8] {'lon'}, dimensions={0} | all-to-all | bytes 1179648 | tf_op jit(solution)/shard_map/all_to_all | solution.py:531
  62.9 0.0 copy-done.1
  62.9 0.0 copy-done.2
  62.9 0.0 copy-done.3
  62.9 2.6 %shard_map.132 = (bf16[256,384]{1,0:T(8,128)(2,1)}, bf16[1024,128]{1,0:T(8,128)(2,1)}, f32[128,768]{1,0:T(8,128)}) custom-call(bf16[8,96,384]{2,1,0:T(8,128)(2,1)S(1)} %all_to_all.26.recv_ref, bf16[128,768]{1,0:T(8,128)(2,1)S(1)} %get-tuple-element.22.fields_ref, bf16[128,768]{1,0:T(8,128)(2,1)S(1)} %get-tuple-element.23.cot_ref, ...), custom_call_target="tpu_custom_call" | custom-call | flops 503316480 | bytes 1703936 | tf_op jit(solution)/shard_map/pallas_call | solution.py:533
  65.5 0.0 all-gather.2.cloned.1.call-update
  65.5 22.5 %all_to_all.27.recv_ref = bf16[64,16,128]{2,1,0:T(8,128)(2,1)S(1)} all-to-all(bf16[64,16,128]{2,1,0:T(8,128)(2,1)} %bitcast.19), channel_id=1, replica_groups=mesh['ens'=2,'lat'=32,'lon'=8] {'ens','lat'}, dimensions={0} | all-to-all | bytes 524288 | tf_op jit(solution)/shard_map/all_to_all | solution.py:558
  88.0 0.1 shard_map.135
  88.0 9.4 %all_to_all.28.recv_ref = bf16[8,16,128]{2,1,0:T(8,128)(2,1)S(1)} all-to-all(bf16[8,16,128]{2,1,0:T(8,128)(2,1)S(1)} %shard_map.135), channel_id=1, replica_groups=mesh['ens'=2,'lat'=32,'lon'=8] {'lon'}, dimensions={0} | all-to-all | bytes 65536 | tf_op jit(solution)/shard_map/all_to_all | solution.py:559
  97.4 0.7 shard_map.136
  98.2 7.1 %all-to-all-start.4 = ((bf16[64,16,128]{2,1,0:T(8,128)(2,1)}), bf16[64,16,128]{2,1,0:T(8,128)(2,1)S(1)}, u32[]{:S(2)}, u32[]{:S(2)}) async-start(bf16[64,16,128]{2,1,0:T(8,128)(2,1)} %shard_map.136), calls=%async_computation.4 | async-start | bytes 524288 | tf_op jit(solution)/shard_map/all_to_all | solution.py:560
  105.3 0.0 all-gather.2.cloned.1.call-done
  105.3 0.0 copy-done
  105.3 6.8 %shard_map.133 = (bf16[128,768]{1,0:T(8,128)(2,1)S(1)}, f32[128,768]{1,0:T(8,128)}, bf16[128,768]{1,0:T(8,128)(2,1)S(1)}) custom-call(bf16[8,256,384]{2,1,0:T(8,128)(2,1)} %bitcast.21, bf16[192,192]{1,0:T(8,128)(2,1)} %get-tuple-element.25.turned_hbm, f32[128,768]{1,0:T(8,128)} %get-tuple-element.26.state_grad_hbm, ...), custom_call_target="tpu_custom_call" | custom-call | flops 2113929216 | bytes 1572864 | tf_op jit(solution)/shard_map/pallas_call | solution.py:562
  112.1 3.5 %collective-permute-start.2 = (bf16[128,768]{1,0:T(8,128)(2,1)S(1)}, bf16[128,768]{1,0:T(8,128)(2,1)S(1)}, u32[]{:S(2)}, u32[]{:S(2)}) collective-permute-start(bf16[128,768]{1,0:T(8,128)(2,1)S(1)} %get-tuple-element.28), channel_id=1, source_target_pairs={{8,16},{16,8},{24,32},{32,24},{40,48},{48,40},{56,64},{64,56},{72,... | collective-permute-start | bytes 589832 | tf_op jit(solution)/shard_map/ppermute | solution.py:466
  115.7 1.9 %collective-permute-start.3 = (bf16[128,768]{1,0:T(8,128)(2,1)S(1)}, bf16[128,768]{1,0:T(8,128)(2,1)S(1)}, u32[]{:S(2)}, u32[]{:S(2)}) collective-permute-start(bf16[128,768]{1,0:T(8,128)(2,1)S(1)} %get-tuple-element.29), channel_id=1, source_target_pairs={{0,8},{8,0},{16,24},{24,16},{32,40},{40,32},{48,56},{56,48},{64,72... | collective-permute-start | bytes 589832 | tf_op jit(solution)/shard_map/ppermute | solution.py:466
  117.6 0.0 all-to-all-done.4
  117.6 0.8 shard_map.137
  118.4 0.7 collective-permute-done.2.first_ref
  119.1 0.0 collective-permute-done.3.second_ref
  119.1 2.1 %shard_map.134 = bf16[720,128]{1,0:T(8,128)(2,1)} custom-call(f32[128,768]{1,0:T(8,128)} %get-tuple-element.27.base_hbm, bf16[128,768]{1,0:T(8,128)(2,1)S(1)} %collective-permute-done.2.first_ref, bf16[128,768]{1,0:T(8,128)(2,1)S(1)} %collective-permute-done.3.second_ref), custom_call_target="tpu_custom_call" | custom-call | flops 141557760 | bytes 368640 | tf_op jit(solution)/shard_map/pallas_call | solution.py:582
Async XLA Ops:
  7.2 98.1 %all-gather.2.cloned.1.call-start = ((), (), s32[]{:S(2)}) async-start(), calls=%async_computation.5 | async-start | bytes 1769472 | tf_op jit(solution)/shard_map/all_gather | solution.py:546
  28.0 10.5 %collective-permute-start.1 = (bf16[8,32,384]{2,1,0:T(8,128)(2,1)S(1)}, bf16[8,32,384]{2,1,0:T(8,128)(2,1)S(1)}, u32[]{:S(2)}, u32[]{:S(2)}) collective-permute-start(bf16[8,32,384]{2,1,0:T(8,128)(2,1)S(1)} %all_to_all.25.own_ref), channel_id=1, source_target_pairs={{8,16},{16,8},{24,32},{32,24},{40,48},{48,40},{56,64},{64,56},{72,... | collective-permute-start | bytes 589832 | tf_op jit(solution)/shard_map/ppermute | solution.py:466
  33.7 4.8 %collective-permute-start = (bf16[8,32,384]{2,1,0:T(8,128)(2,1)S(1)}, bf16[8,32,384]{2,1,0:T(8,128)(2,1)S(1)}, u32[]{:S(2)}, u32[]{:S(2)}) collective-permute-start(bf16[8,32,384]{2,1,0:T(8,128)(2,1)S(1)} %all_to_all.25.own_ref), channel_id=1, source_target_pairs={{0,8},{8,0},{16,24},{24,16},{32,40},{40,32},{48,56},{56,48},{64,72... | collective-permute-start | bytes 589832 | tf_op jit(solution)/shard_map/ppermute | solution.py:466
  38.5 24.4 %copy-start.1 = (bf16[3,128,128]{2,1,0:T(8,128)(2,1)S(1)}, bf16[3,128,128]{2,1,0:T(8,128)(2,1)}, u32[]{:S(2)}) copy-start(bf16[3,128,128]{2,1,0:T(8,128)(2,1)} %filter_ref.3) | copy-start | bytes 294916
  38.5 24.4 %copy-start.2 = (bf16[128,256]{1,0:T(8,128)(2,1)S(1)}, bf16[128,256]{1,0:T(8,128)(2,1)}, u32[]{:S(2)}) copy-start(bf16[128,256]{1,0:T(8,128)(2,1)} %inner_ref.1) | copy-start | bytes 196612
  38.5 24.4 %copy-start.3 = (bf16[256,128]{1,0:T(8,128)(2,1)S(1)}, bf16[256,128]{1,0:T(8,128)(2,1)}, u32[]{:S(2)}) copy-start(bf16[256,128]{1,0:T(8,128)(2,1)} %outer_ref.1) | copy-start | bytes 196612
  41.7 63.6 %copy-start = (bf16[2,768,768]{2,1,0:T(8,128)(2,1)S(1)}, bf16[2,768,768]{2,1,0:T(8,128)(2,1)}, u32[]{:S(2)}) copy-start(bf16[2,768,768]{2,1,0:T(8,128)(2,1)} %constant.2.clone.table_hbm.table_ref) | copy-start | bytes 7077892
  98.2 19.4 %all-to-all-start.4 = ((bf16[64,16,128]{2,1,0:T(8,128)(2,1)}), bf16[64,16,128]{2,1,0:T(8,128)(2,1)S(1)}, u32[]{:S(2)}, u32[]{:S(2)}) async-start(bf16[64,16,128]{2,1,0:T(8,128)(2,1)} %shard_map.136), calls=%async_computation.4 | async-start | bytes 524288 | tf_op jit(solution)/shard_map/all_to_all | solution.py:560
  112.1 7.0 %collective-permute-start.2 = (bf16[128,768]{1,0:T(8,128)(2,1)S(1)}, bf16[128,768]{1,0:T(8,128)(2,1)S(1)}, u32[]{:S(2)}, u32[]{:S(2)}) collective-permute-start(bf16[128,768]{1,0:T(8,128)(2,1)S(1)} %get-tuple-element.28), channel_id=1, source_target_pairs={{8,16},{16,8},{24,32},{32,24},{40,48},{48,40},{56,64},{64,56},{72,... | collective-permute-start | bytes 589832 | tf_op jit(solution)/shard_map/ppermute | solution.py:466
  115.7 3.4 %collective-permute-start.3 = (bf16[128,768]{1,0:T(8,128)(2,1)S(1)}, bf16[128,768]{1,0:T(8,128)(2,1)S(1)}, u32[]{:S(2)}, u32[]{:S(2)}) collective-permute-start(bf16[128,768]{1,0:T(8,128)(2,1)S(1)} %get-tuple-element.29), channel_id=1, source_target_pairs={{0,8},{8,0},{16,24},{24,16},{32,40},{40,32},{48,56},{56,48},{64,72... | collective-permute-start | bytes 589832 | tf_op jit(solution)/shard_map/ppermute | solution.py:466
Sparse Core Ops, SparseCore 0:
  65.6 34.9 all-gather.1

commit v5 on v4

--- a/solution.py
+++ b/solution.py
@@ -23,7 +23,7 @@
 CB = 16
 NK = 3
 NR = 4
-WIDE = 1024
+WIDE = 896
 LIMIT = 24 * 1024 * 1024
 
 
@@ -190,16 +190,18 @@
     odd = (lane >= MP).astype(jnp.int32)
     split = (iota((MODES, 2 * MP), 0) == 2 * (lane - MP * odd) + odd).astype(F32).astype(BF)
     first_half = jnp.where(iota((1, 2 * MP), 1) == 0, 0.5, 1.0).astype(F32)
-    for part, ref in enumerate((real_ref, imag_ref)):
+    rest = []
+    for ref in (real_ref, imag_ref):
         rows = [ref[k] for k in range(NK)]
-        rest = jnp.concatenate([rows[k][i : i + 1] for i in range(NR) for k in range(NK)], axis=0)
-        moved = None
-        for step in range(3):
-            piece = rest.astype(BF)
-            rest = rest - piece.astype(F32)
-            term = dot(piece, split)
-            moved = term if moved is None else moved + term
-        gain_ref[12 * part : 12 * part + 12, :] = moved * first_half
+        rest += [rows[k][i : i + 1] for i in range(NR) for k in range(NK)]
+    rest = jnp.concatenate(rest, axis=0)
+    pieces = []
+    for step in range(3):
+        piece = rest.astype(BF)
+        rest = rest - piece.astype(F32)
+        pieces.append(piece.astype(F32))
+    moved = dot(jnp.concatenate(pieces, axis=0).astype(BF), split)
+    gain_ref[...] = (moved[0:24] + moved[24:48] + moved[48:72]) * first_half
     copies[0].wait()
 
 
@@ -294,7 +296,9 @@
         d_state = cot.astype(F32) + dot(inner, d_hidden)
         state_grad_ref[:, lanes] = d_state
         d_state_b = d_state.astype(BF)
-        back_ref[128 * first : 128 * first + 128, :] = d_state_b
+        for tile in range(3):
+            base = 256 * tile + 128 * first
+            back_ref[base : base + 128, :] = d_state_b[:, 128 * tile : 128 * tile + 128]
         held.append((filtered, d_state_b, active, cot, state, d_hidden))
     copies = bring(((back_ref, back_hbm), (state_grad_ref, state_grad_hbm)), sems)
     sums = None
@@ -305,7 +309,6 @@
     grads_ref[384:640, :] = sums[1].astype(BF)
     grads_ref[640:768, :] = sums[2][:, :128].astype(BF)
     grads_ref[768:896, :] = sums[2][:, 128:].astype(BF)
-    grads_ref[896:WIDE, :] = jnp.zeros((WIDE - 896, 128), BF)
     last = pltpu.make_async_copy(grads_ref, grads_hbm, sems.at[2])
     last.start()
     for copy in copies + [last]:
@@ -326,18 +329,19 @@
     middle_ref,
     spec_ref,
     filt_ref,
+    held_ref,
     part_ref,
     turned_ref,
     state_grad_ref,
     base_ref,
     sems,
 ):
-    pairs = [(recv_hbm.at[n, :, pl.ds(128, 128)], middle_ref.at[n]) for n in range(NZ)]
+    pairs = [(recv_hbm.at[n, pl.ds(256, 256), :], middle_ref.at[n]) for n in range(NZ)]
     for half in range(2):
         for n in range(NZ):
             lanes = pl.ds(128 * tile_of(n), 128)
             rows = pl.ds(256 * half, 256)
-            pairs.append((recv_hbm.at[n, :, pl.ds(256 * half, 128)], x_ref.at[rows, lanes]))
+            pairs.append((recv_hbm.at[n, pl.ds(512 * half, 256), :], x_ref.at[rows, lanes]))
     pairs += [(turned_hbm, turned_ref), (state_grad_hbm, state_grad_ref)]
     copies = bring(pairs, sems)
     z = lax.axis_index("lon")
@@ -374,9 +378,12 @@
                     filt_ref[i, parity, out, MP:] = (real * part_b - imag * part_a).astype(BF)
             result = dot_nt(filt_ref[i, 0], places[0]) + sign * dot_nt(filt_ref[i, 1], places[1])
             result = (result * (2.0 / NLON)).astype(BF)
-            for k in range(NK):
-                part = dot(filter_ref[k], result[128 * k : 128 * k + 128])
-                part_ref[NK * i + k] = part.astype(BF)
+            held_ref[:, 192 * i : 192 * i + 192] = result
+    for k in range(NK):
+        mixed = dot(filter_ref[k], held_ref[128 * k : 128 * k + 128, :]).astype(BF)
+        for i in range(NR):
+            part_ref[NK * i + k] = mixed[:, 192 * i : 192 * i + 192]
+    copies = []
     for s in range(NZ):
         rows = slice(CB * s, CB * s + CB)
         parts = jnp.concatenate([part_ref[g, rows, :] for g in range(12)], axis=0)
@@ -392,16 +399,19 @@
                         ref[rows, lanes] = value + state_grad_ref[rows, lanes]
                     else:
                         ref[rows, lanes] = value.astype(BF)
-    bring([(base_ref, base_hbm)], sems)[0].wait()
-
-
-def sum_kernel(copies, recv_ref, out_ref):
-    total = recv_ref[0].astype(F32)
-    for n in range(1, recv_ref.shape[0]):
-        total = total + recv_ref[n].astype(F32)
-    total = total.astype(BF)
-    for n in range(copies):
-        out_ref[n] = total
+        piece = pl.ds(CB * s, CB)
+        copies.append(
+            pltpu.make_async_copy(base_ref.at[piece], base_hbm.at[piece], sems.at[s])
+        )
+        copies[-1].start()
+    for copy in copies:
+        copy.wait()
+
+
+def sum_kernel(share, recv_ref, out_ref):
+    rows, columns = out_ref.shape[0], recv_ref.shape[0]
+    same = lax.rem(iota((rows, columns), 0), share) == lax.rem(iota((rows, columns), 1), share)
+    out_ref[...] = dot(same.astype(F32).astype(BF), recv_ref[...]).astype(BF)
 
 
 def field_kernel(base_hbm, first_ref, second_ref, grad_ref, base_ref, sems):
@@ -532,10 +542,10 @@
 
     back, grads, state_grad = call(
         mlp_kernel,
-        (in_hbm((256, 384)), in_hbm((WIDE, 128)), in_hbm((128, 768), F32)),
+        (in_hbm((768, 128)), in_hbm((WIDE, 128)), in_hbm((128, 768), F32)),
         2 * 768 * 128 * 256 * 10,
         [
-            pltpu.VMEM((256, 384), BF),
+            pltpu.VMEM((768, 128), BF),
             pltpu.VMEM((WIDE, 128), BF),
             pltpu.VMEM((128, 768), F32),
             pltpu.SemaphoreType.DMA((3,)),
@@ -543,21 +553,26 @@
         vmem(6),
         tuple(hbm(3)),
     )(filtered, field_wide, cot_wide, filter_weights, inner_weights, outer_weights)
-    back = lax.all_gather(back, "lon", tiled=True).reshape(NZ, 256, 384)
+    back = lax.all_gather(back, "lon", tiled=True).reshape(NZ, 768, 128)
+
+    share = WIDE // group
+
+    def exchanged(value, axes):
+        value = value.reshape(value.shape[0] // 2, 2, 128)
+        return lax.all_to_all(value, axes, 0, 0, tiled=True).reshape(-1, 128)
 
     def summed(value, copies):
         return call(
-            functools.partial(sum_kernel, copies),
-            shaped((copies,) + value.shape[1:]),
-            value.size,
+            functools.partial(sum_kernel, share),
+            shaped((copies * share, 128)),
+            2 * copies * share * value.size,
             (),
             vmem(1),
         )(value)
 
-    share = WIDE // group
-    chunks = lax.all_to_all(grads.reshape(group, share, 128), ("ens", "lat"), 0, 0, tiled=True)
-    chunks = lax.all_to_all(summed(chunks, NZ), "lon", 0, 0, tiled=True)
-    gathered = lax.all_to_all(summed(chunks, group), ("ens", "lat"), 0, 0, tiled=True)
+    chunks = exchanged(grads, ("ens", "lat"))
+    chunks = exchanged(summed(chunks, NZ), "lon")
+    gathered = exchanged(summed(chunks, group), ("ens", "lat"))
 
     to_first, kept, to_second = call(
         adjoint_kernel,
@@ -568,6 +583,7 @@
             pltpu.VMEM((NZ, 256, 128), BF),
             pltpu.VMEM((2, 512, 2 * MP), F32),
             pltpu.VMEM((NR, 2, 384, 2 * MP), BF),
+            pltpu.VMEM((384, 768), BF),
             pltpu.VMEM((12, 128, 192), BF),
             pltpu.VMEM((192, 192), BF),
             pltpu.VMEM((128, 768), F32),
@@ -593,7 +609,7 @@
         WIDE * 128,
         (),
         vmem(1),
-    )(gathered.reshape(WIDE, 128))
+    )(gathered)
     field_grad = grad_points.reshape(LON, NR, 128).transpose(1, 0, 2)[None]
     return (field_grad, filter_grad, inner_grad, outer_grad)
 

time: 130 us -> 129 us (level)
  no operation moved by 1% of the time
where the time goes in v5:
time: 129 us; the launch traced here: 127 us
  blocking collectives  71.4 us (55%)
  starting transfers between devices  20.9 us (16%)
  Pallas kernels  20.2 us (16%)
  between operations  14.2 us (11%)
    all_to_all x2, blocking collectives, exchanged(): return lax.all_to_all(value, axes, 0, 0, tiled=True).reshape(-1, 128)  30.8 us
    all_to_all x1, blocking collectives, local(): filtered = lax.all_to_all(send_filtered, 'lon', 0, 0, tiled=True)  21.1 us
    all_to_all x1, blocking collectives, local(): own = lax.all_to_all(send_fields, 'lon', 0, 0, tiled=True)  19.5 us
    ppermute x4, starting transfers between devices, swapped(): return lax.ppermute(value, 'lat', pairs)  13.4 us
    all_to_all x1, starting transfers between devices, exchanged(): return lax.all_to_all(value, axes, 0, 0, tiled=True).reshape(-1, 128)  7.47 us
    pallas_call x1, Pallas kernels, local(): call(adjoint_kernel, (shaped((128, 768)), in_hbm((128, 768), F32), shaped...  6.55 us
    pallas_call x1, Pallas kernels, local(): call(filter_kernel, shaped((NZ, 96, 384)), 8 * 192 * KP * KP, work, vmem(...  3.18 us
  transfers between devices with their start and end apart: 6, of which 1 were waited for; matrix products, arithmetic and copies ran while one was open for 0% of the time, Pallas kernels for 9%

profile of v5, /device:TPU:1, one launch (start us, length us, event | category | flops | bytes accessed | tf_op | source)
XLA Modules:
  0.0 127.4 jit_solution(10911965401499020649)
XLA Ops:
  7.2 0.0 all-gather.2.cloned.1.call-start
  7.2 1.3 %shard_map.129 = (bf16[128,768]{1,0:T(8,128)(2,1)S(1)}, bf16[8,32,384]{2,1,0:T(8,128)(2,1)S(1)}) custom-call(bf16[720,128]{1,0:T(8,128)(2,1)} %bitcast.29), custom_call_target="tpu_custom_call" | custom-call | flops 141557760 | bytes 786432 | tf_op jit(solution)/shard_map/pallas_call | solution.py:496
  8.5 19.5 %all_to_all.25.own_ref = bf16[8,32,384]{2,1,0:T(8,128)(2,1)S(1)} all-to-all(bf16[8,32,384]{2,1,0:T(8,128)(2,1)S(1)} %get-tuple-element.19), channel_id=1, replica_groups=mesh['ens'=2,'lat'=32,'lon'=8] {'lon'}, dimensions={0} | all-to-all | bytes 393216 | tf_op jit(solution)/shard_map/all_to_all | solution.py:500
  28.0 5.7 %collective-permute-start.1 = (bf16[8,32,384]{2,1,0:T(8,128)(2,1)S(1)}, bf16[8,32,384]{2,1,0:T(8,128)(2,1)S(1)}, u32[]{:S(2)}, u32[]{:S(2)}) collective-permute-start(bf16[8,32,384]{2,1,0:T(8,128)(2,1)S(1)} %all_to_all.25.own_ref), channel_id=1, source_target_pairs={{8,16},{16,8},{24,32},{32,24},{40,48},{48,40},{56,64},{64,56},{72,... | collective-permute-start | bytes 589832 | tf_op jit(solution)/shard_map/ppermute | solution.py:476
  33.7 1.9 %collective-permute-start = (bf16[8,32,384]{2,1,0:T(8,128)(2,1)S(1)}, bf16[8,32,384]{2,1,0:T(8,128)(2,1)S(1)}, u32[]{:S(2)}, u32[]{:S(2)}) collective-permute-start(bf16[8,32,384]{2,1,0:T(8,128)(2,1)S(1)} %all_to_all.25.own_ref), channel_id=1, source_target_pairs={{0,8},{8,0},{16,24},{24,16},{32,40},{40,32},{48,56},{56,48},{64,72... | collective-permute-start | bytes 589832 | tf_op jit(solution)/shard_map/ppermute | solution.py:476
  35.6 2.5 %shard_map.130 = (bf16[128,768]{1,0:T(8,128)(2,1)S(1)}, bf16[192,192]{1,0:T(8,128)(2,1)S(1)}, bf16[192,192]{1,0:T(8,128)(2,1)}, f32[24,768]{1,0:T(8,128)S(1)}) custom-call(bf16[720,128]{1,0:T(8,128)(2,1)} %bitcast.30, bf16[3,4,12]{2,1,0:T(4,128)(2,1)} %weights_hbm.1, f32[3,4,720]{2,1,0:T(4,128)} %real_hbm.1, f32[3,4,720]{2,1,0:T(4,128)} %imag_hbm.1, ...), custom_call_target="tpu_custom_call" | custom-call | flops 141557760 | bytes 835584 | tf_op jit(solution)/shard_map/pallas_call | solution.py:502
  38.1 0.0 collective-permute-done.1.second_ref
  38.1 0.0 collective-permute-done.first_ref
  38.1 0.0 copy-start.1
  38.1 0.0 copy-start.2
  38.1 0.0 copy-start.3
  38.2 3.2 %shard_map.131 = bf16[8,96,384]{2,1,0:T(8,128)(2,1)S(1)} custom-call(bf16[8,32,384]{2,1,0:T(8,128)(2,1)S(1)} %collective-permute-done.first_ref, bf16[8,32,384]{2,1,0:T(8,128)(2,1)S(1)} %all_to_all.25.own_ref, bf16[8,32,384]{2,1,0:T(8,128)(2,1)S(1)} %collective-permute-done.1.second_ref, bf16[192,192]{1,0:T(8,128)(2,1)S(1)} %get-tuple-element.20.coupling_ref, ...), custom_call_target="tpu_custom_call" | custom-call | flops 905969664 | bytes 1179648 | tf_op jit(solution)/shard_map/pallas_call | solution.py:538
  41.3 0.0 copy-start
  41.4 21.1 %all_to_all.26.recv_ref = bf16[8,96,384]{2,1,0:T(8,128)(2,1)S(1)} all-to-all(bf16[8,96,384]{2,1,0:T(8,128)(2,1)S(1)} %shard_map.131), channel_id=1, replica_groups=mesh['ens'=2,'lat'=32,'lon'=8] {'lon'}, dimensions={0} | all-to-all | bytes 1179648 | tf_op jit(solution)/shard_map/all_to_all | solution.py:541
  62.4 0.0 copy-done.1
  62.4 0.0 copy-done.2
  62.4 0.0 copy-done.3
  62.5 2.6 %shard_map.132 = (bf16[768,128]{1,0:T(8,128)(2,1)}, bf16[896,128]{1,0:T(8,128)(2,1)}, f32[128,768]{1,0:T(8,128)}) custom-call(bf16[8,96,384]{2,1,0:T(8,128)(2,1)S(1)} %all_to_all.26.recv_ref, bf16[128,768]{1,0:T(8,128)(2,1)S(1)} %get-tuple-element.22.fields_ref, bf16[128,768]{1,0:T(8,128)(2,1)S(1)} %get-tuple-element.23.cot_ref, ...), custom_call_target="tpu_custom_call" | custom-call | flops 503316480 | bytes 1638400 | tf_op jit(solution)/shard_map/pallas_call | solution.py:543
  65.0 0.0 all-gather.2.cloned.1.call-update
  65.1 21.7 %all_to_all.27 = bf16[448,2,128]{2,1,0:T(2,128)(2,1)S(1)} all-to-all(bf16[448,2,128]{2,1,0:T(2,128)(2,1)} %bitcast.26), channel_id=1, replica_groups=mesh['ens'=2,'lat'=32,'lon'=8] {'ens','lat'}, dimensions={0} | all-to-all | bytes 458752 | tf_op jit(solution)/shard_map/all_to_all | solution.py:562
  86.7 0.2 shard_map.135
  86.9 9.2 %all_to_all.28 = bf16[56,2,128]{2,1,0:T(2,128)(2,1)S(1)} all-to-all(bf16[56,2,128]{2,1,0:T(2,128)(2,1)S(1)} %bitcast.24), channel_id=1, replica_groups=mesh['ens'=2,'lat'=32,'lon'=8] {'lon'}, dimensions={0} | all-to-all | bytes 57344 | tf_op jit(solution)/shard_map/all_to_all | solution.py:562
  96.1 1.0 shard_map.136
  97.1 7.5 %all-to-all-start.4 = ((bf16[448,2,128]{2,1,0:T(2,128)(2,1)}), bf16[448,2,128]{2,1,0:T(2,128)(2,1)S(1)}, u32[]{:S(2)}, u32[]{:S(2)}) async-start(bf16[448,2,128]{2,1,0:T(2,128)(2,1)} %bitcast.14), calls=%async_computation.4 | async-start | bytes 458752 | tf_op jit(solution)/shard_map/all_to_all | solution.py:562
  104.6 0.0 all-gather.2.cloned.1.call-done
  104.6 0.0 copy-done
  104.6 6.6 %shard_map.133 = (bf16[128,768]{1,0:T(8,128)(2,1)S(1)}, f32[128,768]{1,0:T(8,128)}, bf16[128,768]{1,0:T(8,128)(2,1)S(1)}) custom-call(bf16[8,768,128]{2,1,0:T(8,128)(2,1)} %bitcast.28, bf16[192,192]{1,0:T(8,128)(2,1)} %get-tuple-element.25.turned_hbm, f32[128,768]{1,0:T(8,128)} %get-tuple-element.26.state_grad_hbm, ...), custom_call_target="tpu_custom_call" | custom-call | flops 2113929216 | bytes 1572864 | tf_op jit(solution)/shard_map/pallas_call | solution.py:577
  111.2 3.8 %collective-permute-start.2 = (bf16[128,768]{1,0:T(8,128)(2,1)S(1)}, bf16[128,768]{1,0:T(8,128)(2,1)S(1)}, u32[]{:S(2)}, u32[]{:S(2)}) collective-permute-start(bf16[128,768]{1,0:T(8,128)(2,1)S(1)} %get-tuple-element.28), channel_id=1, source_target_pairs={{8,16},{16,8},{24,32},{32,24},{40,48},{48,40},{56,64},{64,56},{72,... | collective-permute-start | bytes 589832 | tf_op jit(solution)/shard_map/ppermute | solution.py:476
  115.0 1.9 %collective-permute-start.3 = (bf16[128,768]{1,0:T(8,128)(2,1)S(1)}, bf16[128,768]{1,0:T(8,128)(2,1)S(1)}, u32[]{:S(2)}, u32[]{:S(2)}) collective-permute-start(bf16[128,768]{1,0:T(8,128)(2,1)S(1)} %get-tuple-element.29), channel_id=1, source_target_pairs={{0,8},{8,0},{16,24},{24,16},{32,40},{40,32},{48,56},{56,48},{64,72... | collective-permute-start | bytes 589832 | tf_op jit(solution)/shard_map/ppermute | solution.py:476
  117.0 0.0 all-to-all-done.4
  117.0 0.8 shard_map.137
  117.8 0.6 collective-permute-done.2.first_ref
  118.4 0.0 collective-permute-done.3.second_ref
  118.4 2.1 %shard_map.134 = bf16[720,128]{1,0:T(8,128)(2,1)} custom-call(f32[128,768]{1,0:T(8,128)} %get-tuple-element.27.base_hbm, bf16[128,768]{1,0:T(8,128)(2,1)S(1)} %collective-permute-done.2.first_ref, bf16[128,768]{1,0:T(8,128)(2,1)S(1)} %collective-permute-done.3.second_ref), custom_call_target="tpu_custom_call" | custom-call | flops 141557760 | bytes 368640 | tf_op jit(solution)/shard_map/pallas_call | solution.py:598
Async XLA Ops:
  7.2 97.4 %all-gather.2.cloned.1.call-start = ((), (), s32[]{:S(2)}) async-start(), calls=%async_computation.5 | async-start | bytes 1769472 | tf_op jit(solution)/shard_map/all_gather | solution.py:556
  28.0 10.1 %collective-permute-start.1 = (bf16[8,32,384]{2,1,0:T(8,128)(2,1)S(1)}, bf16[8,32,384]{2,1,0:T(8,128)(2,1)S(1)}, u32[]{:S(2)}, u32[]{:S(2)}) collective-permute-start(bf16[8,32,384]{2,1,0:T(8,128)(2,1)S(1)} %all_to_all.25.own_ref), channel_id=1, source_target_pairs={{8,16},{16,8},{24,32},{32,24},{40,48},{48,40},{56,64},{64,56},{72,... | collective-permute-start | bytes 589832 | tf_op jit(solution)/shard_map/ppermute | solution.py:476
  33.7 4.4 %collective-permute-start = (bf16[8,32,384]{2,1,0:T(8,128)(2,1)S(1)}, bf16[8,32,384]{2,1,0:T(8,128)(2,1)S(1)}, u32[]{:S(2)}, u32[]{:S(2)}) collective-permute-start(bf16[8,32,384]{2,1,0:T(8,128)(2,1)S(1)} %all_to_all.25.own_ref), channel_id=1, source_target_pairs={{0,8},{8,0},{16,24},{24,16},{32,40},{40,32},{48,56},{56,48},{64,72... | collective-permute-start | bytes 589832 | tf_op jit(solution)/shard_map/ppermute | solution.py:476
  38.1 24.3 %copy-start.1 = (bf16[3,128,128]{2,1,0:T(8,128)(2,1)S(1)}, bf16[3,128,128]{2,1,0:T(8,128)(2,1)}, u32[]{:S(2)}) copy-start(bf16[3,128,128]{2,1,0:T(8,128)(2,1)} %filter_ref.3) | copy-start | bytes 294916
  38.1 24.3 %copy-start.2 = (bf16[128,256]{1,0:T(8,128)(2,1)S(1)}, bf16[128,256]{1,0:T(8,128)(2,1)}, u32[]{:S(2)}) copy-start(bf16[128,256]{1,0:T(8,128)(2,1)} %inner_ref.1) | copy-start | bytes 196612
  38.1 24.3 %copy-start.3 = (bf16[256,128]{1,0:T(8,128)(2,1)S(1)}, bf16[256,128]{1,0:T(8,128)(2,1)}, u32[]{:S(2)}) copy-start(bf16[256,128]{1,0:T(8,128)(2,1)} %outer_ref.1) | copy-start | bytes 196612
  41.3 63.3 %copy-start = (bf16[2,768,768]{2,1,0:T(8,128)(2,1)S(1)}, bf16[2,768,768]{2,1,0:T(8,128)(2,1)}, u32[]{:S(2)}) copy-start(bf16[2,768,768]{2,1,0:T(8,128)(2,1)} %constant.2.clone.table_hbm.table_ref) | copy-start | bytes 7077892
  97.1 19.9 %all-to-all-start.4 = ((bf16[448,2,128]{2,1,0:T(2,128)(2,1)}), bf16[448,2,128]{2,1,0:T(2,128)(2,1)S(1)}, u32[]{:S(2)}, u32[]{:S(2)}) async-start(bf16[448,2,128]{2,1,0:T(2,128)(2,1)} %bitcast.14), calls=%async_computation.4 | async-start | bytes 458752 | tf_op jit(solution)/shard_map/all_to_all | solution.py:562
  111.2 7.2 %collective-permute-start.2 = (bf16[128,768]{1,0:T(8,128)(2,1)S(1)}, bf16[128,768]{1,0:T(8,128)(2,1)S(1)}, u32[]{:S(2)}, u32[]{:S(2)}) collective-permute-start(bf16[128,768]{1,0:T(8,128)(2,1)S(1)} %get-tuple-element.28), channel_id=1, source_target_pairs={{8,16},{16,8},{24,32},{32,24},{40,48},{48,40},{56,64},{64,56},{72,... | collective-permute-start | bytes 589832 | tf_op jit(solution)/shard_map/ppermute | solution.py:476
  115.0 3.3 %collective-permute-start.3 = (bf16[128,768]{1,0:T(8,128)(2,1)S(1)}, bf16[128,768]{1,0:T(8,128)(2,1)S(1)}, u32[]{:S(2)}, u32[]{:S(2)}) collective-permute-start(bf16[128,768]{1,0:T(8,128)(2,1)S(1)} %get-tuple-element.29), channel_id=1, source_target_pairs={{0,8},{8,0},{16,24},{24,16},{32,40},{40,32},{48,56},{56,48},{64,72... | collective-permute-start | bytes 589832 | tf_op jit(solution)/shard_map/ppermute | solution.py:476
Sparse Core Ops, SparseCore 0:
  65.2 35.4 all-gather.1

commit v6 on v5

--- a/solution.py
+++ b/solution.py
@@ -378,34 +378,42 @@
                     filt_ref[i, parity, out, MP:] = (real * part_b - imag * part_a).astype(BF)
             result = dot_nt(filt_ref[i, 0], places[0]) + sign * dot_nt(filt_ref[i, 1], places[1])
             result = (result * (2.0 / NLON)).astype(BF)
-            held_ref[:, 192 * i : 192 * i + 192] = result
+            held_ref[:, 256 * i + 192 : 256 * i + 256] = jnp.zeros((384, 64), BF)
+            held_ref[:, 256 * i : 256 * i + 192] = result
     for k in range(NK):
         mixed = dot(filter_ref[k], held_ref[128 * k : 128 * k + 128, :]).astype(BF)
         for i in range(NR):
-            part_ref[NK * i + k] = mixed[:, 192 * i : 192 * i + 192]
+            part_ref[NK * i + k] = mixed[:, 256 * i : 256 * i + 192]
     copies = []
+    totals = []
     for s in range(NZ):
         rows = slice(CB * s, CB * s + CB)
         parts = jnp.concatenate([part_ref[g, rows, :] for g in range(12)], axis=0)
-        total = dot(turned_ref[...], parts)
-        for band, ref in enumerate((first_ref, base_ref, second_ref)):
-            for first in range(2):
-                base = 64 * band + CB * first
-                lower, upper = total[base : base + CB], total[base + 32 : base + 32 + CB]
-                middle = jnp.concatenate([lower[:, 128:], upper[:, 128:]], axis=1)
-                for tile, value in enumerate((lower[:, :128], middle, upper[:, :128])):
-                    lanes = slice(384 * first + 128 * tile, 384 * first + 128 * tile + 128)
-                    if band == 1:
-                        ref[rows, lanes] = value + state_grad_ref[rows, lanes]
-                    else:
-                        ref[rows, lanes] = value.astype(BF)
+        totals.append(dot(turned_ref[...], parts))
+        spread_band(totals[s], 1, rows, base_ref, state_grad_ref)
         piece = pl.ds(CB * s, CB)
         copies.append(
             pltpu.make_async_copy(base_ref.at[piece], base_hbm.at[piece], sems.at[s])
         )
         copies[-1].start()
+    for s in range(NZ):
+        rows = slice(CB * s, CB * s + CB)
+        spread_band(totals[s], 0, rows, first_ref, None)
+        spread_band(totals[s], 2, rows, second_ref, None)
     for copy in copies:
         copy.wait()
+
+
+def spread_band(total, band, rows, ref, added_ref):
+    for first in range(2):
+        base = 64 * band + CB * first
+        lower, upper = total[base : base + CB], total[base + 32 : base + 32 + CB]
+        middle = jnp.concatenate([lower[:, 128:], upper[:, 128:]], axis=1)
+        for tile, value in enumerate((lower[:, :128], middle, upper[:, :128])):
+            lanes = slice(384 * first + 128 * tile, 384 * first + 128 * tile + 128)
+            if added_ref is not None:
+                value = value + added_ref[rows, lanes]
+            ref[rows, lanes] = value.astype(ref.dtype)
 
 
 def sum_kernel(share, recv_ref, out_ref):
@@ -414,12 +422,22 @@
     out_ref[...] = dot(same.astype(F32).astype(BF), recv_ref[...]).astype(BF)
 
 
-def field_kernel(base_hbm, first_ref, second_ref, grad_ref, base_ref, sems):
+def field_kernel(base_hbm, first_ref, second_ref, grad_hbm, base_ref, grad_ref, sems):
     copies = bring([(base_hbm, base_ref)], sems)
     select = point_select()
     halo = first_ref[...].astype(F32) + second_ref[...].astype(F32)
     copies[0].wait()
-    grad_ref[...] = dot_nt(select, (base_ref[...] + halo).astype(BF)).astype(BF)
+    total = (base_ref[...] + halo).astype(BF)
+    copies = []
+    for n, (start, size) in enumerate(((0, 368), (368, 352))):
+        rows = pl.ds(start, size)
+        grad_ref[start : start + size, :] = dot_nt(select[start : start + size], total).astype(BF)
+        copies.append(
+            pltpu.make_async_copy(grad_ref.at[rows, :], grad_hbm.at[rows, :], sems.at[n])
+        )
+        copies[-1].start()
+    for copy in copies:
+        copy.wait()
 
 
 def weights_kernel(scale, grads_ref, filter_ref, inner_ref, outer_ref):
@@ -583,7 +601,7 @@
             pltpu.VMEM((NZ, 256, 128), BF),
             pltpu.VMEM((2, 512, 2 * MP), F32),
             pltpu.VMEM((NR, 2, 384, 2 * MP), BF),
-            pltpu.VMEM((384, 768), BF),
+            pltpu.VMEM((384, 1024), BF),
             pltpu.VMEM((12, 128, 192), BF),
             pltpu.VMEM((192, 192), BF),
             pltpu.VMEM((128, 768), F32),
@@ -597,10 +615,15 @@
     from_first = swapped(to_first, 0)
     grad_points = call(
         field_kernel,
-        shaped((LON * NR, 128)),
+        in_hbm((LON * NR, 128)),
         2 * 720 * 768 * 128,
-        [pltpu.VMEM((128, 768), F32), pltpu.SemaphoreType.DMA((1,))],
+        [
+            pltpu.VMEM((128, 768), F32),
+            pltpu.VMEM((LON * NR, 128), BF),
+            pltpu.SemaphoreType.DMA((2,)),
+        ],
         hbm(1) + vmem(2),
+        hbm(1)[0],
     )(hold(kept), from_second, from_first)
 
     filter_grad, inner_grad, outer_grad = call(

time: 129 us -> 129 us (level)
  no operation moved by 1% of the time
where the time goes in v6:
time: 129 us; the launch traced here: 127 us
  blocking collectives  71.4 us (55%)
  starting transfers between devices  20.9 us (16%)
  Pallas kernels  20.1 us (16%)
  between operations  14.2 us (11%)
    all_to_all x2, blocking collectives, exchanged(): return lax.all_to_all(value, axes, 0, 0, tiled=True).reshape(-1, 128)  30.8 us
    all_to_all x1, blocking collectives, local(): filtered = lax.all_to_all(send_filtered, 'lon', 0, 0, tiled=True)  21.1 us
    all_to_all x1, blocking collectives, local(): own = lax.all_to_all(send_fields, 'lon', 0, 0, tiled=True)  19.5 us
    ppermute x4, starting transfers between devices, swapped(): return lax.ppermute(value, 'lat', pairs)  13.4 us
    all_to_all x1, starting transfers between devices, exchanged(): return lax.all_to_all(value, axes, 0, 0, tiled=True).reshape(-1, 128)  7.47 us
    pallas_call x1, Pallas kernels, local(): call(adjoint_kernel, (shaped((128, 768)), in_hbm((128, 768), F32), shaped...  6.43 us
    pallas_call x1, Pallas kernels, local(): call(filter_kernel, shaped((NZ, 96, 384)), 8 * 192 * KP * KP, work, vmem(...  3.18 us
  transfers between devices with their start and end apart: 6, of which 1 were waited for; matrix products, arithmetic and copies ran while one was open for 0% of the time, Pallas kernels for 9%

profile of v6, /device:TPU:1, one launch (start us, length us, event | category | flops | bytes accessed | tf_op | source)
XLA Modules:
  0.0 127.2 jit_solution(4505866408003807863)
XLA Ops:
  7.2 0.0 all-gather.2.cloned.1.call-start
  7.2 1.3 %shard_map.129 = (bf16[128,768]{1,0:T(8,128)(2,1)S(1)}, bf16[8,32,384]{2,1,0:T(8,128)(2,1)S(1)}) custom-call(bf16[720,128]{1,0:T(8,128)(2,1)} %bitcast.29), custom_call_target="tpu_custom_call" | custom-call | flops 141557760 | bytes 786432 | tf_op jit(solution)/shard_map/pallas_call | solution.py:514
  8.5 19.5 %all_to_all.25.own_ref = bf16[8,32,384]{2,1,0:T(8,128)(2,1)S(1)} all-to-all(bf16[8,32,384]{2,1,0:T(8,128)(2,1)S(1)} %get-tuple-element.19), channel_id=1, replica_groups=mesh['ens'=2,'lat'=32,'lon'=8] {'lon'}, dimensions={0} | all-to-all | bytes 393216 | tf_op jit(solution)/shard_map/all_to_all | solution.py:518
  28.0 5.7 %collective-permute-start.1 = (bf16[8,32,384]{2,1,0:T(8,128)(2,1)S(1)}, bf16[8,32,384]{2,1,0:T(8,128)(2,1)S(1)}, u32[]{:S(2)}, u32[]{:S(2)}) collective-permute-start(bf16[8,32,384]{2,1,0:T(8,128)(2,1)S(1)} %all_to_all.25.own_ref), channel_id=1, source_target_pairs={{8,16},{16,8},{24,32},{32,24},{40,48},{48,40},{56,64},{64,56},{72,... | collective-permute-start | bytes 589832 | tf_op jit(solution)/shard_map/ppermute | solution.py:494
  33.7 1.9 %collective-permute-start = (bf16[8,32,384]{2,1,0:T(8,128)(2,1)S(1)}, bf16[8,32,384]{2,1,0:T(8,128)(2,1)S(1)}, u32[]{:S(2)}, u32[]{:S(2)}) collective-permute-start(bf16[8,32,384]{2,1,0:T(8,128)(2,1)S(1)} %all_to_all.25.own_ref), channel_id=1, source_target_pairs={{0,8},{8,0},{16,24},{24,16},{32,40},{40,32},{48,56},{56,48},{64,72... | collective-permute-start | bytes 589832 | tf_op jit(solution)/shard_map/ppermute | solution.py:494
  35.6 2.5 %shard_map.130 = (bf16[128,768]{1,0:T(8,128)(2,1)S(1)}, bf16[192,192]{1,0:T(8,128)(2,1)S(1)}, bf16[192,192]{1,0:T(8,128)(2,1)}, f32[24,768]{1,0:T(8,128)S(1)}) custom-call(bf16[720,128]{1,0:T(8,128)(2,1)} %bitcast.30, bf16[3,4,12]{2,1,0:T(4,128)(2,1)} %weights_hbm.1, f32[3,4,720]{2,1,0:T(4,128)} %real_hbm.1, f32[3,4,720]{2,1,0:T(4,128)} %imag_hbm.1, ...), custom_call_target="tpu_custom_call" | custom-call | flops 141557760 | bytes 835584 | tf_op jit(solution)/shard_map/pallas_call | solution.py:520
  38.1 0.0 collective-permute-done.1.second_ref
  38.1 0.0 collective-permute-done.first_ref
  38.1 0.0 copy-start.1
  38.1 0.0 copy-start.2
  38.1 0.0 copy-start.3
  38.2 3.2 %shard_map.131 = bf16[8,96,384]{2,1,0:T(8,128)(2,1)S(1)} custom-call(bf16[8,32,384]{2,1,0:T(8,128)(2,1)S(1)} %collective-permute-done.first_ref, bf16[8,32,384]{2,1,0:T(8,128)(2,1)S(1)} %all_to_all.25.own_ref, bf16[8,32,384]{2,1,0:T(8,128)(2,1)S(1)} %collective-permute-done.1.second_ref, bf16[192,192]{1,0:T(8,128)(2,1)S(1)} %get-tuple-element.20.coupling_ref, ...), custom_call_target="tpu_custom_call" | custom-call | flops 905969664 | bytes 1179648 | tf_op jit(solution)/shard_map/pallas_call | solution.py:556
  41.3 0.0 copy-start
  41.4 21.1 %all_to_all.26.recv_ref = bf16[8,96,384]{2,1,0:T(8,128)(2,1)S(1)} all-to-all(bf16[8,96,384]{2,1,0:T(8,128)(2,1)S(1)} %shard_map.131), channel_id=1, replica_groups=mesh['ens'=2,'lat'=32,'lon'=8] {'lon'}, dimensions={0} | all-to-all | bytes 1179648 | tf_op jit(solution)/shard_map/all_to_all | solution.py:559
  62.4 0.0 copy-done.1
  62.4 0.0 copy-done.2
  62.4 0.0 copy-done.3
  62.5 2.6 %shard_map.132 = (bf16[768,128]{1,0:T(8,128)(2,1)}, bf16[896,128]{1,0:T(8,128)(2,1)}, f32[128,768]{1,0:T(8,128)}) custom-call(bf16[8,96,384]{2,1,0:T(8,128)(2,1)S(1)} %all_to_all.26.recv_ref, bf16[128,768]{1,0:T(8,128)(2,1)S(1)} %get-tuple-element.22.fields_ref, bf16[128,768]{1,0:T(8,128)(2,1)S(1)} %get-tuple-element.23.cot_ref, ...), custom_call_target="tpu_custom_call" | custom-call | flops 503316480 | bytes 1638400 | tf_op jit(solution)/shard_map/pallas_call | solution.py:561
  65.0 0.0 all-gather.2.cloned.1.call-update
  65.1 21.7 %all_to_all.27 = bf16[448,2,128]{2,1,0:T(2,128)(2,1)S(1)} all-to-all(bf16[448,2,128]{2,1,0:T(2,128)(2,1)} %bitcast.26), channel_id=1, replica_groups=mesh['ens'=2,'lat'=32,'lon'=8] {'ens','lat'}, dimensions={0} | all-to-all | bytes 458752 | tf_op jit(solution)/shard_map/all_to_all | solution.py:580
  86.7 0.2 shard_map.135
  86.9 9.2 %all_to_all.28 = bf16[56,2,128]{2,1,0:T(2,128)(2,1)S(1)} all-to-all(bf16[56,2,128]{2,1,0:T(2,128)(2,1)S(1)} %bitcast.24), channel_id=1, replica_groups=mesh['ens'=2,'lat'=32,'lon'=8] {'lon'}, dimensions={0} | all-to-all | bytes 57344 | tf_op jit(solution)/shard_map/all_to_all | solution.py:580
  96.1 1.0 shard_map.136
  97.1 7.5 %all-to-all-start.4 = ((bf16[448,2,128]{2,1,0:T(2,128)(2,1)}), bf16[448,2,128]{2,1,0:T(2,128)(2,1)S(1)}, u32[]{:S(2)}, u32[]{:S(2)}) async-start(bf16[448,2,128]{2,1,0:T(2,128)(2,1)} %bitcast.14), calls=%async_computation.4 | async-start | bytes 458752 | tf_op jit(solution)/shard_map/all_to_all | solution.py:580
  104.6 0.0 all-gather.2.cloned.1.call-done
  104.6 0.0 copy-done
  104.6 6.4 %shard_map.133 = (bf16[128,768]{1,0:T(8,128)(2,1)S(1)}, f32[128,768]{1,0:T(8,128)}, bf16[128,768]{1,0:T(8,128)(2,1)S(1)}) custom-call(bf16[8,768,128]{2,1,0:T(8,128)(2,1)} %bitcast.28, bf16[192,192]{1,0:T(8,128)(2,1)} %get-tuple-element.25.turned_hbm, f32[128,768]{1,0:T(8,128)} %get-tuple-element.26.state_grad_hbm, ...), custom_call_target="tpu_custom_call" | custom-call | flops 2113929216 | bytes 1572864 | tf_op jit(solution)/shard_map/pallas_call | solution.py:595
  111.1 3.8 %collective-permute-start.2 = (bf16[128,768]{1,0:T(8,128)(2,1)S(1)}, bf16[128,768]{1,0:T(8,128)(2,1)S(1)}, u32[]{:S(2)}, u32[]{:S(2)}) collective-permute-start(bf16[128,768]{1,0:T(8,128)(2,1)S(1)} %get-tuple-element.28), channel_id=1, source_target_pairs={{8,16},{16,8},{24,32},{32,24},{40,48},{48,40},{56,64},{64,56},{72,... | collective-permute-start | bytes 589832 | tf_op jit(solution)/shard_map/ppermute | solution.py:494
  114.9 1.9 %collective-permute-start.3 = (bf16[128,768]{1,0:T(8,128)(2,1)S(1)}, bf16[128,768]{1,0:T(8,128)(2,1)S(1)}, u32[]{:S(2)}, u32[]{:S(2)}) collective-permute-start(bf16[128,768]{1,0:T(8,128)(2,1)S(1)} %get-tuple-element.29), channel_id=1, source_target_pairs={{0,8},{8,0},{16,24},{24,16},{32,40},{40,32},{48,56},{56,48},{64,72... | collective-permute-start | bytes 589832 | tf_op jit(solution)/shard_map/ppermute | solution.py:494
  116.8 0.0 all-to-all-done.4
  116.8 0.8 shard_map.137
  117.6 0.6 collective-permute-done.2.first_ref
  118.2 0.0 collective-permute-done.3.second_ref
  118.2 2.1 %shard_map.134 = bf16[720,128]{1,0:T(8,128)(2,1)} custom-call(f32[128,768]{1,0:T(8,128)} %get-tuple-element.27.base_hbm, bf16[128,768]{1,0:T(8,128)(2,1)S(1)} %collective-permute-done.2.first_ref, bf16[128,768]{1,0:T(8,128)(2,1)S(1)} %collective-permute-done.3.second_ref), custom_call_target="tpu_custom_call" | custom-call | flops 141557760 | bytes 368640 | tf_op jit(solution)/shard_map/pallas_call | solution.py:616
Async XLA Ops:
  7.2 97.4 %all-gather.2.cloned.1.call-start = ((), (), s32[]{:S(2)}) async-start(), calls=%async_computation.5 | async-start | bytes 1769472 | tf_op jit(solution)/shard_map/all_gather | solution.py:574
  28.0 10.1 %collective-permute-start.1 = (bf16[8,32,384]{2,1,0:T(8,128)(2,1)S(1)}, bf16[8,32,384]{2,1,0:T(8,128)(2,1)S(1)}, u32[]{:S(2)}, u32[]{:S(2)}) collective-permute-start(bf16[8,32,384]{2,1,0:T(8,128)(2,1)S(1)} %all_to_all.25.own_ref), channel_id=1, source_target_pairs={{8,16},{16,8},{24,32},{32,24},{40,48},{48,40},{56,64},{64,56},{72,... | collective-permute-start | bytes 589832 | tf_op jit(solution)/shard_map/ppermute | solution.py:494
  33.7 4.4 %collective-permute-start = (bf16[8,32,384]{2,1,0:T(8,128)(2,1)S(1)}, bf16[8,32,384]{2,1,0:T(8,128)(2,1)S(1)}, u32[]{:S(2)}, u32[]{:S(2)}) collective-permute-start(bf16[8,32,384]{2,1,0:T(8,128)(2,1)S(1)} %all_to_all.25.own_ref), channel_id=1, source_target_pairs={{0,8},{8,0},{16,24},{24,16},{32,40},{40,32},{48,56},{56,48},{64,72... | collective-permute-start | bytes 589832 | tf_op jit(solution)/shard_map/ppermute | solution.py:494
  38.1 24.3 %copy-start.1 = (bf16[3,128,128]{2,1,0:T(8,128)(2,1)S(1)}, bf16[3,128,128]{2,1,0:T(8,128)(2,1)}, u32[]{:S(2)}) copy-start(bf16[3,128,128]{2,1,0:T(8,128)(2,1)} %filter_ref.3) | copy-start | bytes 294916
  38.1 24.3 %copy-start.2 = (bf16[128,256]{1,0:T(8,128)(2,1)S(1)}, bf16[128,256]{1,0:T(8,128)(2,1)}, u32[]{:S(2)}) copy-start(bf16[128,256]{1,0:T(8,128)(2,1)} %inner_ref.1) | copy-start | bytes 196612
  38.1 24.3 %copy-start.3 = (bf16[256,128]{1,0:T(8,128)(2,1)S(1)}, bf16[256,128]{1,0:T(8,128)(2,1)}, u32[]{:S(2)}) copy-start(bf16[256,128]{1,0:T(8,128)(2,1)} %outer_ref.1) | copy-start | bytes 196612
  41.3 63.3 %copy-start = (bf16[2,768,768]{2,1,0:T(8,128)(2,1)S(1)}, bf16[2,768,768]{2,1,0:T(8,128)(2,1)}, u32[]{:S(2)}) copy-start(bf16[2,768,768]{2,1,0:T(8,128)(2,1)} %constant.2.clone.table_hbm.table_ref) | copy-start | bytes 7077892
  97.1 19.7 %all-to-all-start.4 = ((bf16[448,2,128]{2,1,0:T(2,128)(2,1)}), bf16[448,2,128]{2,1,0:T(2,128)(2,1)S(1)}, u32[]{:S(2)}, u32[]{:S(2)}) async-start(bf16[448,2,128]{2,1,0:T(2,128)(2,1)} %bitcast.14), calls=%async_computation.4 | async-start | bytes 458752 | tf_op jit(solution)/shard_map/all_to_all | solution.py:580
  111.1 7.2 %collective-permute-start.2 = (bf16[128,768]{1,0:T(8,128)(2,1)S(1)}, bf16[128,768]{1,0:T(8,128)(2,1)S(1)}, u32[]{:S(2)}, u32[]{:S(2)}) collective-permute-start(bf16[128,768]{1,0:T(8,128)(2,1)S(1)} %get-tuple-element.28), channel_id=1, source_target_pairs={{8,16},{16,8},{24,32},{32,24},{40,48},{48,40},{56,64},{64,56},{72,... | collective-permute-start | bytes 589832 | tf_op jit(solution)/shard_map/ppermute | solution.py:494
  114.9 3.3 %collective-permute-start.3 = (bf16[128,768]{1,0:T(8,128)(2,1)S(1)}, bf16[128,768]{1,0:T(8,128)(2,1)S(1)}, u32[]{:S(2)}, u32[]{:S(2)}) collective-permute-start(bf16[128,768]{1,0:T(8,128)(2,1)S(1)} %get-tuple-element.29), channel_id=1, source_target_pairs={{0,8},{8,0},{16,24},{24,16},{32,40},{40,32},{48,56},{56,48},{64,72... | collective-permute-start | bytes 589832 | tf_op jit(solution)/shard_map/ppermute | solution.py:494
Sparse Core Ops, SparseCore 0:
  65.2 35.4 all-gather.1

commit v7 on v6

--- a/solution.py
+++ b/solution.py
@@ -269,10 +269,9 @@
     inner_ref,
     outer_ref,
     back_hbm,
-    grads_hbm,
+    grads_ref,
     state_grad_hbm,
     back_ref,
-    grads_ref,
     state_grad_ref,
     sems,
 ):
@@ -309,9 +308,7 @@
     grads_ref[384:640, :] = sums[1].astype(BF)
     grads_ref[640:768, :] = sums[2][:, :128].astype(BF)
     grads_ref[768:896, :] = sums[2][:, 128:].astype(BF)
-    last = pltpu.make_async_copy(grads_ref, grads_hbm, sems.at[2])
-    last.start()
-    for copy in copies + [last]:
+    for copy in copies:
         copy.wait()
 
 
@@ -560,16 +557,15 @@
 
     back, grads, state_grad = call(
         mlp_kernel,
-        (in_hbm((768, 128)), in_hbm((WIDE, 128)), in_hbm((128, 768), F32)),
+        (in_hbm((768, 128)), shaped((WIDE, 128)), in_hbm((128, 768), F32)),
         2 * 768 * 128 * 256 * 10,
         [
             pltpu.VMEM((768, 128), BF),
-            pltpu.VMEM((WIDE, 128), BF),
             pltpu.VMEM((128, 768), F32),
-            pltpu.SemaphoreType.DMA((3,)),
+            pltpu.SemaphoreType.DMA((2,)),
         ],
         vmem(6),
-        tuple(hbm(3)),
+        tuple(hbm(1) + vmem(1) + hbm(1)),
     )(filtered, field_wide, cot_wide, filter_weights, inner_weights, outer_weights)
     back = lax.all_gather(back, "lon", tiled=True).reshape(NZ, 768, 128)
 

time: 129 us -> 129 us (level)
  no operation moved by 1% of the time
where the time goes in v7:
time: 129 us; the launch traced here: 127 us
  blocking collectives  71.3 us (55%)
  starting transfers between devices  21 us (16%)
  Pallas kernels  19.7 us (15%)
  between operations  14.2 us (11%)
    all_to_all x2, blocking collectives, exchanged(): return lax.all_to_all(value, axes, 0, 0, tiled=True).reshape(-1, 128)  30.7 us
    all_to_all x1, blocking collectives, local(): filtered = lax.all_to_all(send_filtered, 'lon', 0, 0, tiled=True)  21.1 us
    all_to_all x1, blocking collectives, local(): own = lax.all_to_all(send_fields, 'lon', 0, 0, tiled=True)  19.5 us
    ppermute x4, starting transfers between devices, swapped(): return lax.ppermute(value, 'lat', pairs)  13.5 us
    all_to_all x1, starting transfers between devices, exchanged(): return lax.all_to_all(value, axes, 0, 0, tiled=True).reshape(-1, 128)  7.47 us
    pallas_call x1, Pallas kernels, local(): call(adjoint_kernel, (shaped((128, 768)), in_hbm((128, 768), F32), shaped...  6.44 us
    pallas_call x1, Pallas kernels, local(): call(filter_kernel, shaped((NZ, 96, 384)), 8 * 192 * KP * KP, work, vmem(...  3.18 us
  transfers between devices with their start and end apart: 6, of which 1 were waited for; matrix products, arithmetic and copies ran while one was open for 0% of the time, Pallas kernels for 9%

profile of v7, /device:TPU:1, one launch (start us, length us, event | category | flops | bytes accessed | tf_op | source)
XLA Modules:
  0.0 126.9 jit_solution(2779604357041655825)
XLA Ops:
  7.2 0.0 all-gather.2.cloned.1.call-start
  7.2 1.3 %shard_map.129 = (bf16[128,768]{1,0:T(8,128)(2,1)S(1)}, bf16[8,32,384]{2,1,0:T(8,128)(2,1)S(1)}) custom-call(bf16[720,128]{1,0:T(8,128)(2,1)} %bitcast.29), custom_call_target="tpu_custom_call" | custom-call | flops 141557760 | bytes 786432 | tf_op jit(solution)/shard_map/pallas_call | solution.py:511
  8.5 19.5 %all_to_all.25.own_ref = bf16[8,32,384]{2,1,0:T(8,128)(2,1)S(1)} all-to-all(bf16[8,32,384]{2,1,0:T(8,128)(2,1)S(1)} %get-tuple-element.19), channel_id=1, replica_groups=mesh['ens'=2,'lat'=32,'lon'=8] {'lon'}, dimensions={0} | all-to-all | bytes 393216 | tf_op jit(solution)/shard_map/all_to_all | solution.py:515
  28.0 5.7 %collective-permute-start.1 = (bf16[8,32,384]{2,1,0:T(8,128)(2,1)S(1)}, bf16[8,32,384]{2,1,0:T(8,128)(2,1)S(1)}, u32[]{:S(2)}, u32[]{:S(2)}) collective-permute-start(bf16[8,32,384]{2,1,0:T(8,128)(2,1)S(1)} %all_to_all.25.own_ref), channel_id=1, source_target_pairs={{8,16},{16,8},{24,32},{32,24},{40,48},{48,40},{56,64},{64,56},{72,... | collective-permute-start | bytes 589832 | tf_op jit(solution)/shard_map/ppermute | solution.py:491
  33.7 1.9 %collective-permute-start = (bf16[8,32,384]{2,1,0:T(8,128)(2,1)S(1)}, bf16[8,32,384]{2,1,0:T(8,128)(2,1)S(1)}, u32[]{:S(2)}, u32[]{:S(2)}) collective-permute-start(bf16[8,32,384]{2,1,0:T(8,128)(2,1)S(1)} %all_to_all.25.own_ref), channel_id=1, source_target_pairs={{0,8},{8,0},{16,24},{24,16},{32,40},{40,32},{48,56},{56,48},{64,72... | collective-permute-start | bytes 589832 | tf_op jit(solution)/shard_map/ppermute | solution.py:491
  35.6 2.5 %shard_map.130 = (bf16[128,768]{1,0:T(8,128)(2,1)S(1)}, bf16[192,192]{1,0:T(8,128)(2,1)S(1)}, bf16[192,192]{1,0:T(8,128)(2,1)}, f32[24,768]{1,0:T(8,128)S(1)}) custom-call(bf16[720,128]{1,0:T(8,128)(2,1)} %bitcast.30, bf16[3,4,12]{2,1,0:T(4,128)(2,1)} %weights_hbm.1, f32[3,4,720]{2,1,0:T(4,128)} %real_hbm.1, f32[3,4,720]{2,1,0:T(4,128)} %imag_hbm.1, ...), custom_call_target="tpu_custom_call" | custom-call | flops 141557760 | bytes 835584 | tf_op jit(solution)/shard_map/pallas_call | solution.py:517
  38.1 0.0 collective-permute-done.1.second_ref
  38.1 0.0 collective-permute-done.first_ref
  38.1 0.0 copy-start.1
  38.1 0.0 copy-start.2
  38.1 0.0 copy-start.3
  38.2 3.2 %shard_map.131 = bf16[8,96,384]{2,1,0:T(8,128)(2,1)S(1)} custom-call(bf16[8,32,384]{2,1,0:T(8,128)(2,1)S(1)} %collective-permute-done.first_ref, bf16[8,32,384]{2,1,0:T(8,128)(2,1)S(1)} %all_to_all.25.own_ref, bf16[8,32,384]{2,1,0:T(8,128)(2,1)S(1)} %collective-permute-done.1.second_ref, bf16[192,192]{1,0:T(8,128)(2,1)S(1)} %get-tuple-element.20.coupling_ref, ...), custom_call_target="tpu_custom_call" | custom-call | flops 905969664 | bytes 1179648 | tf_op jit(solution)/shard_map/pallas_call | solution.py:553
  41.3 0.0 copy-start
  41.4 21.1 %all_to_all.26.recv_ref = bf16[8,96,384]{2,1,0:T(8,128)(2,1)S(1)} all-to-all(bf16[8,96,384]{2,1,0:T(8,128)(2,1)S(1)} %shard_map.131), channel_id=1, replica_groups=mesh['ens'=2,'lat'=32,'lon'=8] {'lon'}, dimensions={0} | all-to-all | bytes 1179648 | tf_op jit(solution)/shard_map/all_to_all | solution.py:556
  62.4 0.0 copy-done.1
  62.4 0.0 copy-done.2
  62.4 0.0 copy-done.3
  62.5 2.2 %shard_map.132 = (bf16[768,128]{1,0:T(8,128)(2,1)}, bf16[896,128]{1,0:T(8,128)(2,1)S(1)}, f32[128,768]{1,0:T(8,128)}) custom-call(bf16[8,96,384]{2,1,0:T(8,128)(2,1)S(1)} %all_to_all.26.recv_ref, bf16[128,768]{1,0:T(8,128)(2,1)S(1)} %get-tuple-element.22.fields_ref, bf16[128,768]{1,0:T(8,128)(2,1)S(1)} %get-tuple-element.23.cot_ref, ...), custom_call_target="tpu_custom_call" | custom-call | flops 503316480 | bytes 1638400 | tf_op jit(solution)/shard_map/pallas_call | solution.py:558
  64.7 0.0 all-gather.2.cloned.1.call-update
  64.7 21.4 %all_to_all.27 = bf16[448,2,128]{2,1,0:T(2,128)(2,1)S(1)} all-to-all(bf16[448,2,128]{2,1,0:T(2,128)(2,1)S(1)} %bitcast.24), channel_id=1, replica_groups=mesh['ens'=2,'lat'=32,'lon'=8] {'ens','lat'}, dimensions={0} | all-to-all | bytes 458752 | tf_op jit(solution)/shard_map/all_to_all | solution.py:576
  86.1 0.2 shard_map.135
  86.4 9.3 %all_to_all.28 = bf16[56,2,128]{2,1,0:T(2,128)(2,1)S(1)} all-to-all(bf16[56,2,128]{2,1,0:T(2,128)(2,1)S(1)} %bitcast.25), channel_id=1, replica_groups=mesh['ens'=2,'lat'=32,'lon'=8] {'lon'}, dimensions={0} | all-to-all | bytes 57344 | tf_op jit(solution)/shard_map/all_to_all | solution.py:576
  95.6 1.0 shard_map.136
  96.6 7.5 %all-to-all-start.4 = ((bf16[448,2,128]{2,1,0:T(2,128)(2,1)}), bf16[448,2,128]{2,1,0:T(2,128)(2,1)S(1)}, u32[]{:S(2)}, u32[]{:S(2)}) async-start(bf16[448,2,128]{2,1,0:T(2,128)(2,1)} %bitcast.14), calls=%async_computation.4 | async-start | bytes 458752 | tf_op jit(solution)/shard_map/all_to_all | solution.py:576
  104.1 0.0 all-gather.2.cloned.1.call-done
  104.1 0.0 copy-done
  104.2 6.4 %shard_map.133 = (bf16[128,768]{1,0:T(8,128)(2,1)S(1)}, f32[128,768]{1,0:T(8,128)}, bf16[128,768]{1,0:T(8,128)(2,1)S(1)}) custom-call(bf16[8,768,128]{2,1,0:T(8,128)(2,1)} %bitcast.28, bf16[192,192]{1,0:T(8,128)(2,1)} %get-tuple-element.25.turned_hbm, f32[128,768]{1,0:T(8,128)} %get-tuple-element.26.state_grad_hbm, ...), custom_call_target="tpu_custom_call" | custom-call | flops 2113929216 | bytes 1572864 | tf_op jit(solution)/shard_map/pallas_call | solution.py:591
  110.6 4.0 %collective-permute-start.2 = (bf16[128,768]{1,0:T(8,128)(2,1)S(1)}, bf16[128,768]{1,0:T(8,128)(2,1)S(1)}, u32[]{:S(2)}, u32[]{:S(2)}) collective-permute-start(bf16[128,768]{1,0:T(8,128)(2,1)S(1)} %get-tuple-element.28), channel_id=1, source_target_pairs={{8,16},{16,8},{24,32},{32,24},{40,48},{48,40},{56,64},{64,56},{72,... | collective-permute-start | bytes 589832 | tf_op jit(solution)/shard_map/ppermute | solution.py:491
  114.6 1.9 %collective-permute-start.3 = (bf16[128,768]{1,0:T(8,128)(2,1)S(1)}, bf16[128,768]{1,0:T(8,128)(2,1)S(1)}, u32[]{:S(2)}, u32[]{:S(2)}) collective-permute-start(bf16[128,768]{1,0:T(8,128)(2,1)S(1)} %get-tuple-element.29), channel_id=1, source_target_pairs={{0,8},{8,0},{16,24},{24,16},{32,40},{40,32},{48,56},{56,48},{64,72... | collective-permute-start | bytes 589832 | tf_op jit(solution)/shard_map/ppermute | solution.py:491
  116.5 0.0 all-to-all-done.4
  116.5 0.8 shard_map.137
  117.3 0.6 collective-permute-done.2.first_ref
  117.9 0.0 collective-permute-done.3.second_ref
  117.9 2.1 %shard_map.134 = bf16[720,128]{1,0:T(8,128)(2,1)} custom-call(f32[128,768]{1,0:T(8,128)} %get-tuple-element.27.base_hbm, bf16[128,768]{1,0:T(8,128)(2,1)S(1)} %collective-permute-done.2.first_ref, bf16[128,768]{1,0:T(8,128)(2,1)S(1)} %collective-permute-done.3.second_ref), custom_call_target="tpu_custom_call" | custom-call | flops 141557760 | bytes 368640 | tf_op jit(solution)/shard_map/pallas_call | solution.py:612
Async XLA Ops:
  7.2 97.0 %all-gather.2.cloned.1.call-start = ((), (), s32[]{:S(2)}) async-start(), calls=%async_computation.5 | async-start | bytes 1769472 | tf_op jit(solution)/shard_map/all_gather | solution.py:570
  28.0 10.1 %collective-permute-start.1 = (bf16[8,32,384]{2,1,0:T(8,128)(2,1)S(1)}, bf16[8,32,384]{2,1,0:T(8,128)(2,1)S(1)}, u32[]{:S(2)}, u32[]{:S(2)}) collective-permute-start(bf16[8,32,384]{2,1,0:T(8,128)(2,1)S(1)} %all_to_all.25.own_ref), channel_id=1, source_target_pairs={{8,16},{16,8},{24,32},{32,24},{40,48},{48,40},{56,64},{64,56},{72,... | collective-permute-start | bytes 589832 | tf_op jit(solution)/shard_map/ppermute | solution.py:491
  33.7 4.4 %collective-permute-start = (bf16[8,32,384]{2,1,0:T(8,128)(2,1)S(1)}, bf16[8,32,384]{2,1,0:T(8,128)(2,1)S(1)}, u32[]{:S(2)}, u32[]{:S(2)}) collective-permute-start(bf16[8,32,384]{2,1,0:T(8,128)(2,1)S(1)} %all_to_all.25.own_ref), channel_id=1, source_target_pairs={{0,8},{8,0},{16,24},{24,16},{32,40},{40,32},{48,56},{56,48},{64,72... | collective-permute-start | bytes 589832 | tf_op jit(solution)/shard_map/ppermute | solution.py:491
  38.1 24.3 %copy-start.1 = (bf16[3,128,128]{2,1,0:T(8,128)(2,1)S(1)}, bf16[3,128,128]{2,1,0:T(8,128)(2,1)}, u32[]{:S(2)}) copy-start(bf16[3,128,128]{2,1,0:T(8,128)(2,1)} %filter_ref.3) | copy-start | bytes 294916
  38.1 24.3 %copy-start.2 = (bf16[128,256]{1,0:T(8,128)(2,1)S(1)}, bf16[128,256]{1,0:T(8,128)(2,1)}, u32[]{:S(2)}) copy-start(bf16[128,256]{1,0:T(8,128)(2,1)} %inner_ref.1) | copy-start | bytes 196612
  38.1 24.3 %copy-start.3 = (bf16[256,128]{1,0:T(8,128)(2,1)S(1)}, bf16[256,128]{1,0:T(8,128)(2,1)}, u32[]{:S(2)}) copy-start(bf16[256,128]{1,0:T(8,128)(2,1)} %outer_ref.1) | copy-start | bytes 196612
  41.3 62.8 %copy-start = (bf16[2,768,768]{2,1,0:T(8,128)(2,1)S(1)}, bf16[2,768,768]{2,1,0:T(8,128)(2,1)}, u32[]{:S(2)}) copy-start(bf16[2,768,768]{2,1,0:T(8,128)(2,1)} %constant.2.clone.table_hbm.table_ref) | copy-start | bytes 7077892
  96.6 19.9 %all-to-all-start.4 = ((bf16[448,2,128]{2,1,0:T(2,128)(2,1)}), bf16[448,2,128]{2,1,0:T(2,128)(2,1)S(1)}, u32[]{:S(2)}, u32[]{:S(2)}) async-start(bf16[448,2,128]{2,1,0:T(2,128)(2,1)} %bitcast.14), calls=%async_computation.4 | async-start | bytes 458752 | tf_op jit(solution)/shard_map/all_to_all | solution.py:576
  110.6 7.3 %collective-permute-start.2 = (bf16[128,768]{1,0:T(8,128)(2,1)S(1)}, bf16[128,768]{1,0:T(8,128)(2,1)S(1)}, u32[]{:S(2)}, u32[]{:S(2)}) collective-permute-start(bf16[128,768]{1,0:T(8,128)(2,1)S(1)} %get-tuple-element.28), channel_id=1, source_target_pairs={{8,16},{16,8},{24,32},{32,24},{40,48},{48,40},{56,64},{64,56},{72,... | collective-permute-start | bytes 589832 | tf_op jit(solution)/shard_map/ppermute | solution.py:491
  114.6 3.3 %collective-permute-start.3 = (bf16[128,768]{1,0:T(8,128)(2,1)S(1)}, bf16[128,768]{1,0:T(8,128)(2,1)S(1)}, u32[]{:S(2)}, u32[]{:S(2)}) collective-permute-start(bf16[128,768]{1,0:T(8,128)(2,1)S(1)} %get-tuple-element.29), channel_id=1, source_target_pairs={{0,8},{8,0},{16,24},{24,16},{32,40},{40,32},{48,56},{56,48},{64,72... | collective-permute-start | bytes 589832 | tf_op jit(solution)/shard_map/ppermute | solution.py:491
Sparse Core Ops, SparseCore 0:
  64.8 35.4 all-gather.1
